TPU v7x, 32 devices: a whole 2x2x4 slice. The times are simulated.
32 devices in a mesh: groups: 2 (over y), epoch: 4 (over z), strip: 2 (over x), band: 2 (over core).
Axes of the slice: x: 2, y: 2, z: 4, core: 2. Of those that a mesh axis runs over, the one named last changes fastest.
Arguments:
- template: bfloat16 [16, 48, 512], P(('groups', 'epoch'), 'strip', 'band'), parts along dimension 0, may hold values from -6 to 6
- science: float32 [32, 48, 512], P(('groups', 'epoch'), 'strip', 'band'), parts along dimension 0, may hold values from -6 to 6
- variance: float32 [32, 48, 512], P(('groups', 'epoch'), 'strip', 'band'), parts along dimension 0, may hold values from 2 to 40
- bad_mask: int32 [32, 48, 512], P(('groups', 'epoch'), 'strip', 'band'), parts along dimension 0, may hold values 0 or 1
- intersection: int32 [32], P('groups'), parts along dimension 0, may hold values from 0 to 7, as said below
- offsets: int32 [32, 2], P(('groups', 'epoch')), parts along dimension 0, may hold values from -4 to 4
- basis_index: int32 [32, 16], P(('groups', 'epoch')), parts along dimension 0, may hold values from 0 to 48
- coefficients: float32 [32, 16, 6], P(('groups', 'epoch')), parts along dimension 0, may hold values from -2 to 2
- basis: float32 [49, 19, 19], replicated, may hold values from -0.3125 to 0.3125
Outputs:
- residual_image: float32 [32, 48, 512], P(('groups', 'epoch'), 'strip', 'band'), parts along dimension 0
- coadd: float32 [16, 48, 512], P(('groups', 'epoch'), 'strip', 'band'), parts along dimension 0
There are 2 independent parts, one for each index of `groups`. A program takes and returns all parts, laid end to end along the dimension named above; an argument that names none is the same for every part. Nothing has to cross between parts.
Inputs may be any that keep to these rules, and one draw needn't show every extreme that they name: `intersection`: exposure d * 4 + k (k < 4) covers a tile with index from (k) * 2 to (k) * 2 + 1, chosen at random among these.
All inputs are finite; a program needn't handle non-finite values. No bound on the sum of `bad_mask` on one device may be relied on, other than what follows from the above.
Results may differ from a plain program's by a relative error of at most 0.0018.
Values may be sent and summed in bfloat16 or wider, within the bound.
No kernel may reach another device: no remote copies, remote signals or barrier semaphores. Data moves between devices by JAX's collectives and lax.ppermute only.
A program may use at most 64 MiB of HBM per device.

v0:
```python
import jax
import jax.numpy as jnp
from jax import lax
from jax.sharding import PartitionSpec as P

KS = 19
HALF = 9
SHIFT = 4
NPOLY = 6


highest = lax.Precision.HIGHEST


def padded_2(block, sides, width):
    for axis, dim in sides:
        count = lax.axis_size(axis)
        forward = [(i, i + 1) for i in range(count - 1)]
        backward = [(target, source) for source, target in forward]
        low = lax.ppermute(
            lax.slice_in_dim(block, block.shape[dim] - width, None, axis=dim), axis, forward
        )
        high = lax.ppermute(lax.slice_in_dim(block, 0, width, axis=dim), axis, backward)
        block = jnp.concatenate([low, block, high], axis=dim)
    return block


def poly_terms(rows_unit, cols_unit):
    ones = jnp.ones_like(rows_unit * cols_unit)
    return jnp.stack(
        [
            ones,
            rows_unit * ones,
            cols_unit * ones,
            rows_unit * rows_unit * ones,
            rows_unit * cols_unit,
            cols_unit * cols_unit * ones,
        ]
    )


def local(
    template, science, variance, bad_mask, intersection, offsets, basis_index, coefficients, basis
):
    n_epoch = lax.axis_size("epoch")
    my_index = lax.axis_index("epoch")
    tile_dev = template.shape[0]
    exp_dev, height, width = science.shape
    per_owner = exp_dev // n_epoch
    table = intersection.reshape(n_epoch, n_epoch, per_owner)
    wanted = lax.dynamic_index_in_dim(table, my_index, 1, keepdims=False)
    local_ids = jnp.clip(wanted - my_index * tile_dev, 0, tile_dev - 1).reshape(-1)
    my_tiles = lax.dynamic_slice_in_dim(intersection, my_index * exp_dev, exp_dev)
    piece = lax.all_gather(template, "epoch", axis=0, tiled=True)
    count = piece.shape[0]
    inside = (my_tiles >= 0) & (my_tiles < count)
    chosen = jnp.take(piece, jnp.clip(my_tiles, 0, count - 1), axis=0)
    arrived = jnp.where(
        inside[:, None, None], chosen, jnp.zeros((exp_dev, height, width), jnp.bfloat16)
    )
    padded = padded_2(arrived, (("strip", 1), ("band", 2)), HALF + SHIFT)
    picked = jnp.take(basis, basis_index, axis=0)
    kernels = jnp.einsum("ejp,ejab->epab", coefficients, picked, precision=highest).astype(
        jnp.bfloat16
    )
    span = height + 2 * HALF
    distance = jnp.arange(span)[None, :] - jnp.arange(height)[:, None]
    selector = (distance[None] == jnp.arange(KS)[:, None, None]).astype(jnp.bfloat16)
    row_global = lax.axis_index("strip") * height + jnp.arange(height)
    col_global = lax.axis_index("band") * width + jnp.arange(width)
    rows_unit = (2.0 * row_global.astype(jnp.float32) + 1.0) / (
        height * lax.axis_size("strip")
    ) - 1.0
    cols_unit = (2.0 * col_global.astype(jnp.float32) + 1.0) / (width * lax.axis_size("band")) - 1.0
    shapes = poly_terms(rows_unit[:, None], cols_unit[None, :])

    def one_model(item):
        slab, shift, kernel = item
        window = lax.dynamic_slice(
            slab, (SHIFT + shift[0], SHIFT + shift[1]), (span, width + 2 * HALF)
        )
        stacked = jnp.concatenate(
            [window[:, column : column + width] for column in range(KS)], axis=0
        )
        toeplitz = jnp.einsum("pij,iyz->pyjz", kernel, selector, preferred_element_type=jnp.float32)
        toeplitz = toeplitz.astype(jnp.bfloat16).reshape(NPOLY * height, KS * span)
        conv = jnp.dot(toeplitz, stacked, preferred_element_type=jnp.float32).reshape(
            NPOLY, height, width
        )
        return jnp.sum(conv * shapes, axis=0)

    models = lax.map(one_model, (padded, offsets, kernels))
    residual_image = science - models
    weight = bad_mask.astype(jnp.float32) / variance
    weighted = weight * residual_image
    numer_back, denom_back = (
        lax.all_to_all(
            weighted.reshape(n_epoch, per_owner, height, width),
            "epoch",
            split_axis=0,
            concat_axis=0,
            tiled=True,
        ),
        lax.all_to_all(
            weight.reshape(n_epoch, per_owner, height, width),
            "epoch",
            split_axis=0,
            concat_axis=0,
            tiled=True,
        ),
    )
    onehot = (local_ids[:, None] == jnp.arange(tile_dev)[None, :]).astype(jnp.float32)
    numer = jnp.einsum(
        "st,shw->thw", onehot, numer_back.reshape(-1, height, width), precision=highest
    )
    denom = jnp.einsum(
        "st,shw->thw", onehot, denom_back.reshape(-1, height, width), precision=highest
    )
    return (residual_image, numer / (denom + 1.0))


def solution(mesh):
    in_specs = (
        P(("groups", "epoch"), "strip", "band"),
        P(("groups", "epoch"), "strip", "band"),
        P(("groups", "epoch"), "strip", "band"),
        P(("groups", "epoch"), "strip", "band"),
        P("groups"),
        P(("groups", "epoch"), None),
        P(("groups", "epoch"), None),
        P(("groups", "epoch"), None, None),
        P(),
    )
    out_specs = (P(("groups", "epoch"), "strip", "band"), P(("groups", "epoch"), "strip", "band"))
    return jax.shard_map(local, mesh=mesh, in_specs=in_specs, out_specs=out_specs, check_vma=False)
```

profile of v0, /device:TPU:0, one launch (start us, length us, event | category | flops | bytes accessed | tf_op | source)
XLA Modules:
  0.0 87.0 jit_solution(12005535667029276163)
XLA Ops:
  0.6 15.2 %all_gather.3 = bf16[8,24,256]{2,1,0:T(8,128)(2,1)S(1)} all-gather(bf16[2,24,256]{2,1,0:T(8,128)(2,1)} %param.11), channel_id=1, replica_groups=mesh['groups'=2,'epoch'=4,'strip'=2,'band'=2] {'epoch'}, dimensions={0}, use_global_device_ids=true | all-gather | bytes 122880 | tf_op jit(solution)/shard_map/all_gather | solution.py:54
  15.9 0.7 compare_and_fusion
  16.6 0.6 gather_fusion.1
  17.3 1.3 %collective-permute-start.1 = (bf16[4,13,256]{2,1,0:T(8,128)(2,1)S(1)}, bf16[4,13,256]{2,1,0:T(8,128)(2,1)S(1)}, u32[]{:S(2)}, u32[]{:S(2)}) collective-permute-start(bf16[4,13,256]{2,1,0:T(8,128)(2,1)S(1)} %get-tuple-element.206), channel_id=1, source_target_pairs={{2,0},{3,1},{6,4},{7,5},{10,8},{11,9},{14,12},{15,13},{18,16},{19,... | collective-permute-start | bytes 79880 | tf_op jit(solution)/shard_map/ppermute | solution.py:23
  18.6 4.5 %collective-permute-start = (bf16[4,13,256]{2,1,0:T(8,128)(2,1)S(1)}, bf16[4,13,256]{2,1,0:T(8,128)(2,1)S(1)}, u32[]{:S(2)}, u32[]{:S(2)}) collective-permute-start(bf16[4,13,256]{2,1,0:T(8,128)(2,1)S(1)} %get-tuple-element.205), channel_id=1, source_target_pairs={{0,2},{1,3},{4,6},{5,7},{8,10},{9,11},{12,14},{13,15},{16,18},{17,... | collective-permute-start | bytes 79880 | tf_op jit(solution)/shard_map/ppermute | solution.py:20
  23.2 0.7 compare_select_fusion
  23.8 0.7 compare_and_fusion.2
  24.6 1.3 %copy.31 = f32[49,19,19]{2,1,0:T(8,128)S(1)} copy(f32[49,19,19]{0,2,1:T(8,128)} %param.19) | data formatting | bytes 141512 | tf_op args[8]
  25.9 0.6 gather_fusion
  26.6 0.6 copy.42
  27.6 4.5 %fusion.12 = bf16[4,6,19,19]{3,1,2,0:T(8,128)(2,1)S(1)} fusion(f32[4,16,19,19]{1,0,3,2:T(4,128)S(1)} %broadcast_select_fusion, f32[4,16,6,1]{1,0,2,3:T(4,128)S(1)} %bitcast.66), kind=kOutput, calls=%fused_computation.19 | convolution fusion | flops 1672152 | bytes 111280 | tf_op jit(solution)/shard_map/ejp,ejab->epab/dot_general | solution.py:63
  32.2 1.3 %collective-permute-start.3 = (bf16[4,50,13]{2,1,0:T(8,128)(2,1)S(1)}, bf16[4,50,13]{2,1,0:T(8,128)(2,1)S(1)}, u32[]{:S(2)}, u32[]{:S(2)}) collective-permute-start(bf16[4,50,13]{2,1,0:T(8,128)(2,1)S(1)} %get-tuple-element.204), channel_id=1, source_target_pairs={{1,0},{3,2},{5,4},{7,6},{9,8},{11,10},{13,12},{15,14},{17,16},{19,... | collective-permute-start | bytes 15608 | tf_op jit(solution)/shard_map/ppermute | solution.py:23
  33.5 3.0 %collective-permute-start.2 = (bf16[4,50,13]{2,1,0:T(8,128)(2,1)S(1)}, bf16[4,50,13]{2,1,0:T(8,128)(2,1)S(1)}, u32[]{:S(2)}, u32[]{:S(2)}) collective-permute-start(bf16[4,50,13]{2,1,0:T(8,128)(2,1)S(1)} %get-tuple-element.203), channel_id=1, source_target_pairs={{0,1},{2,3},{4,5},{6,7},{8,9},{10,11},{12,13},{14,15},{16,17},{18,... | collective-permute-start | bytes 15608 | tf_op jit(solution)/shard_map/ppermute | solution.py:20
  36.9 0.6 collective-permute-done.2
  37.7 27.8 %while.14 = (s32[]{:T(128)}, f32[4,24,256]{2,1,0:T(8,128)S(1)}, bf16[4,6,19,19]{2,3,1,0:T(8,128)(2,1)S(1)}, s32[4,2]{0,1:T(2,128)S(1)}, bf16[4,50,282]{2,1,0:T(8...) while((s32[]{:T(128)}, f32[4,24,256]{2,1,0:T(8,128)S(1)}, ...), condition=%wide.region_2.3_spmd.clone, body=%wide.region_0.2_spmd.clone.sunk | while | flops 63422412 | bytes 3278881 | solution.py:92
  38.1 0.5 dot_general.24
  38.6 0.5 fusion.46
  42.0 2.3 %concatenate.17 = bf16[798,256]{1,0:T(8,128)(2,1)S(1)} concatenate(bf16[42,256]{1,0:T(8,128)(2,1)S(1)} %get-tuple-element.276, bf16[42,256]{1,0:T(8,128)(2,1)S(1)} %get-tuple-element.277, bf16[42,256]{1,0:T(8,128)(2,1)S(1)} %get-tuple-element.278, bf16[42,256]{1,0:T(8,128)(2,1)S(1)} %get-tuple-element.279, bf16[42,256]{1,0:T(8,128)(2,1)S(1)} %get-tuple-element.280, ...), dimensions={0} | concatenate | bytes 817152 | tf_op jit(solution)/shard_map/while/body/eval_jaxpr/concatenate | solution.py:82
  45.0 0.5 dot_general.24
  45.6 0.5 fusion.46
  49.0 2.3 %concatenate.17 = bf16[798,256]{1,0:T(8,128)(2,1)S(1)} concatenate(bf16[42,256]{1,0:T(8,128)(2,1)S(1)} %get-tuple-element.276, bf16[42,256]{1,0:T(8,128)(2,1)S(1)} %get-tuple-element.277, bf16[42,256]{1,0:T(8,128)(2,1)S(1)} %get-tuple-element.278, bf16[42,256]{1,0:T(8,128)(2,1)S(1)} %get-tuple-element.279, bf16[42,256]{1,0:T(8,128)(2,1)S(1)} %get-tuple-element.280, ...), dimensions={0} | concatenate | bytes 817152 | tf_op jit(solution)/shard_map/while/body/eval_jaxpr/concatenate | solution.py:82
  52.0 0.5 dot_general.24
  52.5 0.5 fusion.46
  55.9 2.3 %concatenate.17 = bf16[798,256]{1,0:T(8,128)(2,1)S(1)} concatenate(bf16[42,256]{1,0:T(8,128)(2,1)S(1)} %get-tuple-element.276, bf16[42,256]{1,0:T(8,128)(2,1)S(1)} %get-tuple-element.277, bf16[42,256]{1,0:T(8,128)(2,1)S(1)} %get-tuple-element.278, bf16[42,256]{1,0:T(8,128)(2,1)S(1)} %get-tuple-element.279, bf16[42,256]{1,0:T(8,128)(2,1)S(1)} %get-tuple-element.280, ...), dimensions={0} | concatenate | bytes 817152 | tf_op jit(solution)/shard_map/while/body/eval_jaxpr/concatenate | solution.py:82
  59.5 0.5 fusion.46
  62.9 2.3 %concatenate.17 = bf16[798,256]{1,0:T(8,128)(2,1)S(1)} concatenate(bf16[42,256]{1,0:T(8,128)(2,1)S(1)} %get-tuple-element.276, bf16[42,256]{1,0:T(8,128)(2,1)S(1)} %get-tuple-element.277, bf16[42,256]{1,0:T(8,128)(2,1)S(1)} %get-tuple-element.278, bf16[42,256]{1,0:T(8,128)(2,1)S(1)} %get-tuple-element.279, bf16[42,256]{1,0:T(8,128)(2,1)S(1)} %get-tuple-element.280, ...), dimensions={0} | concatenate | bytes 817152 | tf_op jit(solution)/shard_map/while/body/eval_jaxpr/concatenate | solution.py:82
  65.6 0.7 multiply_bitcast_fusion
  66.3 4.7 %all-to-all-start = ((f32[4,1,24,256]{3,2,1,0:T(8,128)}), f32[4,1,24,256]{3,2,1,0:T(8,128)S(1)}, u32[]{:S(2)}, u32[]{:S(2)}) async-start(f32[4,1,24,256]{3,2,1,0:T(8,128)} %get-tuple-element.177), calls=%async_computation | async-start | bytes 196608 | tf_op jit(solution)/shard_map/all_to_all | solution.py:97
  71.3 5.7 %all-to-all-done = f32[4,1,24,256]{3,2,1,0:T(8,128)S(1)} async-done(((f32[4,1,24,256]{3,2,1,0:T(8,128)}), f32[4,1,24,256]{3,2,1,0:T(8,128)S(1)}, u32[]{:S(2)}, u32[]{:S(2)}) %all-to-all-start) | async-done | bytes 98336 | tf_op jit(solution)/shard_map/all_to_all | solution.py:97
  77.0 3.3 %all-to-all-start.1 = ((f32[4,1,24,256]{3,2,1,0:T(8,128)}), f32[4,1,24,256]{3,2,1,0:T(8,128)S(1)}, u32[]{:S(2)}, u32[]{:S(2)}) async-start(f32[4,1,24,256]{3,2,1,0:T(8,128)} %get-tuple-element.202), calls=%async_computation.1 | async-start | bytes 196608 | tf_op jit(solution)/shard_map/all_to_all | solution.py:104
  80.5 5.6 %all-to-all-done.1 = f32[4,1,24,256]{3,2,1,0:T(8,128)S(1)} async-done(((f32[4,1,24,256]{3,2,1,0:T(8,128)}), f32[4,1,24,256]{3,2,1,0:T(8,128)S(1)}, u32[]{:S(2)}, u32[]{:S(2)}) %all-to-all-start.1) | async-done | bytes 98336 | tf_op jit(solution)/shard_map/all_to_all | solution.py:104
  86.3 0.6 copy.39
  (65 shorter events, 6.4 us)
Async XLA Ops:
  0.6 26.9 %copy-start = (f32[4,16,6]{1,0,2:T(4,128)S(1)}, f32[4,16,6]{1,0,2:T(4,128)}, u32[]{:S(2)}) copy-start(f32[4,16,6]{1,0,2:T(4,128)} %param.18) | copy-start | bytes 4612
  17.3 14.8 %collective-permute-start.1 = (bf16[4,13,256]{2,1,0:T(8,128)(2,1)S(1)}, bf16[4,13,256]{2,1,0:T(8,128)(2,1)S(1)}, u32[]{:S(2)}, u32[]{:S(2)}) collective-permute-start(bf16[4,13,256]{2,1,0:T(8,128)(2,1)S(1)} %get-tuple-element.206), channel_id=1, source_target_pairs={{2,0},{3,1},{6,4},{7,5},{10,8},{11,9},{14,12},{15,13},{18,16},{19,... | collective-permute-start | bytes 79880 | tf_op jit(solution)/shard_map/ppermute | solution.py:23
  18.6 13.5 %collective-permute-start = (bf16[4,13,256]{2,1,0:T(8,128)(2,1)S(1)}, bf16[4,13,256]{2,1,0:T(8,128)(2,1)S(1)}, u32[]{:S(2)}, u32[]{:S(2)}) collective-permute-start(bf16[4,13,256]{2,1,0:T(8,128)(2,1)S(1)} %get-tuple-element.205), channel_id=1, source_target_pairs={{0,2},{1,3},{4,6},{5,7},{8,10},{9,11},{12,14},{13,15},{16,18},{17,... | collective-permute-start | bytes 79880 | tf_op jit(solution)/shard_map/ppermute | solution.py:20
  27.6 10.1 %copy-start.4 = (s32[4,2]{0,1:T(2,128)S(1)}, s32[4,2]{0,1:T(2,128)}, u32[]{:S(2)}) copy-start(s32[4,2]{0,1:T(2,128)} %param.16) | copy-start | bytes 100
  32.2 4.6 %collective-permute-start.3 = (bf16[4,50,13]{2,1,0:T(8,128)(2,1)S(1)}, bf16[4,50,13]{2,1,0:T(8,128)(2,1)S(1)}, u32[]{:S(2)}, u32[]{:S(2)}) collective-permute-start(bf16[4,50,13]{2,1,0:T(8,128)(2,1)S(1)} %get-tuple-element.204), channel_id=1, source_target_pairs={{1,0},{3,2},{5,4},{7,6},{9,8},{11,10},{13,12},{15,14},{17,16},{19,... | collective-permute-start | bytes 15608 | tf_op jit(solution)/shard_map/ppermute | solution.py:23
  33.5 3.9 %collective-permute-start.2 = (bf16[4,50,13]{2,1,0:T(8,128)(2,1)S(1)}, bf16[4,50,13]{2,1,0:T(8,128)(2,1)S(1)}, u32[]{:S(2)}, u32[]{:S(2)}) collective-permute-start(bf16[4,50,13]{2,1,0:T(8,128)(2,1)S(1)} %get-tuple-element.203), channel_id=1, source_target_pairs={{0,1},{2,3},{4,5},{6,7},{8,9},{10,11},{12,13},{14,15},{16,17},{18,... | collective-permute-start | bytes 15608 | tf_op jit(solution)/shard_map/ppermute | solution.py:20
  37.6 27.9 %copy-start.1 = (f32[4,24,256]{2,1,0:T(8,128)S(1)}, f32[4,24,256]{2,1,0:T(8,128)}, u32[]{:S(2)}) copy-start(f32[4,24,256]{2,1,0:T(8,128)} %param.13) | copy-start | bytes 294916
  37.6 27.9 %copy-start.2 = (s32[4,24,256]{2,1,0:T(8,128)S(1)}, s32[4,24,256]{2,1,0:T(8,128)}, u32[]{:S(2)}) copy-start(s32[4,24,256]{2,1,0:T(8,128)} %param.14) | copy-start | bytes 294916
  37.6 27.9 %copy-start.3 = (f32[4,24,256]{2,1,0:T(8,128)S(1)}, f32[4,24,256]{2,1,0:T(8,128)}, u32[]{:S(2)}) copy-start(f32[4,24,256]{2,1,0:T(8,128)} %param.12) | copy-start | bytes 294916
  65.5 5.5 %copy-start.5 = (s32[16]{0:T(128)S(1)}, s32[16]{0:T(128)}, u32[]{:S(2)}) copy-start(s32[16]{0:T(128)} %param.15) | copy-start | bytes 196
  66.3 10.7 %all-to-all-start = ((f32[4,1,24,256]{3,2,1,0:T(8,128)}), f32[4,1,24,256]{3,2,1,0:T(8,128)S(1)}, u32[]{:S(2)}, u32[]{:S(2)}) async-start(f32[4,1,24,256]{3,2,1,0:T(8,128)} %get-tuple-element.177), calls=%async_computation | async-start | bytes 196608 | tf_op jit(solution)/shard_map/all_to_all | solution.py:97
  77.0 9.1 %all-to-all-start.1 = ((f32[4,1,24,256]{3,2,1,0:T(8,128)}), f32[4,1,24,256]{3,2,1,0:T(8,128)S(1)}, u32[]{:S(2)}, u32[]{:S(2)}) async-start(f32[4,1,24,256]{3,2,1,0:T(8,128)} %get-tuple-element.202), calls=%async_computation.1 | async-start | bytes 196608 | tf_op jit(solution)/shard_map/all_to_all | solution.py:104
where the time goes:
time: 87.6 us; the launch traced here: 87 us
  local copies, waits for them, and re-layouts  19.1 us (22%)
  starting transfers between devices  18.2 us (21%)
  blocking collectives  15.2 us (17%)
  waiting for transfers between devices  11.8 us (13%)
  loops' own time  10.6 us (12%)
  matrix products  7.48 us (9%)
  other arithmetic  3.59 us (4%)
  between operations  0.89 us (1%)
    all_gather x1, blocking collectives, local(): piece = lax.all_gather(template, 'epoch', axis=0, tiled=True)  15.2 us
    another operation x1, loops' own time, local(): models = lax.map(one_model, (padded, offsets, kernels))  10.6 us
    concatenate x4, local copies, waits for them, and re-layouts, one_model(): jnp.concatenate([window[:, column:column + width] for column in range(KS)...  9.31 us
    ppermute x2, starting transfers between devices, padded_2(): lax.ppermute(lax.slice_in_dim(block, block.shape[dim] - width, None, axis...  7.58 us
    all_to_all x1, waiting for transfers between devices, local(): lax.all_to_all(weighted.reshape(n_epoch, per_owner, height, width), 'epoc...  5.71 us
    all_to_all x1, waiting for transfers between devices, local(): lax.all_to_all(weight.reshape(n_epoch, per_owner, height, width), 'epoch'...  5.56 us
    all_to_all x1, starting transfers between devices, local(): lax.all_to_all(weighted.reshape(n_epoch, per_owner, height, width), 'epoc...  4.72 us
    dot_general x1, matrix products, local(): jnp.einsum('ejp,ejab->epab', coefficients, picked, precision=highest)  4.52 us
  transfers between devices with their start and end apart: 6, of which 3 were waited for; matrix products, arithmetic and copies ran while one was open for 11% of the time, Pallas kernels for 0%

commit v1 on v0

v1 whole, which is shorter than its diff:
```python
import jax
import jax.numpy as jnp
from jax import lax
from jax.experimental import pallas as pl
from jax.experimental.pallas import tpu as pltpu
from jax.sharding import PartitionSpec as P

KS = 19
HALF = 9
SHIFT = 4
NPOLY = 6
REACH = HALF + SHIFT
SLOT = 8
CHUNK = 256
VMEM_LIMIT = 24 * 1024 * 1024

highest = lax.Precision.HIGHEST
f32 = jnp.float32
bf16 = jnp.bfloat16


def up(value, step):
    return -(-value // step) * step


class Sizes:
    def __init__(self, height, width):
        self.height, self.width = height, width
        self.rows = up(height + 2 * REACH, 8)
        self.lanes = up(width + 2 * REACH, 128)
        self.span = up(height + KS - 1, 16)
        self.per = CHUNK // self.span
        self.chunks = -(-KS // self.per)
        self.depth = self.chunks * CHUNK
        self.sw_rows = 4 * height
        self.r_rows = self.chunks * SLOT
        self.main_at = self.sw_rows + self.r_rows
        self.halo_at = self.main_at + self.rows
        self.groups = self.rows // 8
        self.halo_rows = up(self.groups * 32, width) // width * 8
        self.total = up(self.halo_at + self.halo_rows, 16)


def iota(shape, axis):
    return lax.broadcasted_iota(jnp.int32, shape, axis)


def split(value):
    high = value.astype(bf16).astype(f32)
    return high, value - high


def prepare(sz, count, nsel):
    lanes = count * SLOT
    nbasis = 128

    def body(sci, var, mask, offs, index, coef, basis, r_out, sw_out, table, place):
        for e in range(count):
            s_high, s_low = split(sci[e])
            w_high, w_low = split(mask[e].astype(f32) / var[e])
            sw_out[e] = jnp.concatenate([s_high, s_low, w_high, w_low], axis=0).astype(bf16)
        table[...] = jnp.zeros(table.shape, f32)
        for a in range(KS):
            table[a * 24 : a * 24 + KS, : basis.shape[2]] = basis[a]
        col = iota((24, sz.depth), 0)
        base = (col // sz.per) * CHUNK + (col % sz.per) * sz.span
        lane = iota((24, sz.depth), 1)
        base = jnp.where(col < KS, lane - base, -1)
        for a in range(0, KS + 1, 2):
            pair = jnp.concatenate([(base == a).astype(f32), (base == a + 1).astype(f32)], axis=0)
            if a + 1 == KS:
                pair = jnp.where(iota(pair.shape, 0) < 24, pair, 0.0)
            place[a * 24 : a * 24 + 48] = pair.astype(bf16)
        chosen = jnp.concatenate([index[e : e + 1, :] for e in range(count)], axis=1)
        onehot = (iota((nbasis, count * nsel), 0) == chosen).astype(f32)
        blocks = []
        for e in range(count):
            mine = jnp.concatenate([coef[:, e, :], jnp.zeros((SLOT - NPOLY, nsel), f32)], axis=0)
            wide = jnp.concatenate([mine] * count, axis=1)
            blocks.append(jnp.where(iota(wide.shape, 1) // nsel == e, wide, 0.0))
        combine = jnp.concatenate(blocks, axis=0)
        mixing = lax.dot_general(
            onehot, combine, (((1,), (1,)), ((), ())), precision=highest, preferred_element_type=f32
        )
        images = jnp.dot(table[...], mixing, precision=highest, preferred_element_type=f32)
        rows = lax.dot_general(
            images.astype(bf16), place[...], (((0,), (0,)), ((), ())), preferred_element_type=f32
        )
        for e in range(count):
            mine = rows[e * SLOT : (e + 1) * SLOT]
            mine = jnp.concatenate(
                [mine[:, i * CHUNK : (i + 1) * CHUNK] for i in range(sz.chunks)], axis=0
            )
            down, across = offs[0:1, e : e + 1].astype(f32), offs[1:2, e : e + 1].astype(f32)
            spot_row, spot = iota(mine.shape, 0), iota(mine.shape, 1)
            spare = spot_row == NPOLY
            mine = jnp.where(spare & (spot == 0), down, jnp.where(spare & (spot == 1), across, mine))
            r_out[e] = mine.astype(bf16)

    return pl.pallas_call(
        body,
        out_shape=(
            jax.ShapeDtypeStruct((count, sz.r_rows, CHUNK), bf16),
            jax.ShapeDtypeStruct((count, sz.sw_rows, sz.width), bf16),
        ),
        scratch_shapes=[
            pltpu.VMEM(((KS + 1) * 24, nbasis), f32),
            pltpu.VMEM(((KS + 1) * 24, sz.depth), bf16),
        ],
        compiler_params=pltpu.CompilerParams(vmem_limit_bytes=VMEM_LIMIT),
        cost_estimate=pl.CostEstimate(flops=200_000_000, bytes_accessed=3_000_000, transcendentals=0),
        name="prepare",
    )


def here(axis):
    return lax.axis_index(axis), lax.axis_size(axis)


def partner(me, n, k, back):
    if n & (n - 1) == 0:
        return me ^ k
    return (me + (n - k if back else k)) % n


def pack(sz, n_epoch, tiles, count, peers):
    per_owner = count // n_epoch
    h, w = sz.height, sz.width

    def body(inter, own, low, high, left, low_left, high_left, right, low_right, high_right, sw, r, *outs):
        slabs, sends = outs[0], outs[1:]
        me, _ = here("epoch")
        strip, strips = here("strip")
        band, bands = here("band")

        def column(middle, above, below, t, cut):
            above = jnp.where(strip > 0, above[t, h - 16 :, cut].astype(f32), 0.0)
            above = jnp.where(iota(above.shape, 0) >= 16 - REACH, above, 0.0)
            below = jnp.where(strip < strips - 1, below[t, :16, cut].astype(f32), 0.0)
            below = jnp.where(iota(below.shape, 0) < REACH, below, 0.0)
            parts = [middle[t, :, cut].astype(f32), below]
            gap = sz.rows - h - 32
            if gap:
                parts.append(jnp.zeros((gap, below.shape[1]), f32))
            return jnp.concatenate(parts + [above], axis=0)

        for t in range(tiles):
            slabs[t, :, :w] = column(own, low, high, t, slice(None)).astype(bf16)
            before = column(left, low_left, high_left, t, slice(w - 128, w))
            after = column(right, low_right, high_right, t, slice(0, 128))
            lane = iota(before.shape, 1)
            before = jnp.where((lane >= 128 - REACH) & (band > 0), before, 0.0)
            after = jnp.where((lane < REACH) & (band < bands - 1), after, 0.0)
            if sz.lanes - w == 128:
                slabs[t, :, w:] = (before + after).astype(bf16)
            else:
                slabs[t, :, w : w + 128] = after.astype(bf16)
                slabs[t, :, sz.lanes - 128 :] = before.astype(bf16)
        for k, out in zip(peers, sends):
            q = partner(me, n_epoch, k, False)
            for c in range(per_owner):
                tile = inter[q * count + me * per_owner + c] - me * tiles
                tile = jnp.clip(tile, 0, tiles - 1)
                mine = q * per_owner + c
                slab = slabs[tile].astype(f32)
                halo = pltpu.roll(slab[:, sz.lanes - 128 :], REACH, 1)
                if sz.lanes - w != 128:
                    halo = halo + pltpu.roll(slab[:, w : w + 128], REACH, 1)
                halo = jnp.where(iota(halo.shape, 1) < 32, halo, 0.0)
                bits = []
                for part in range(sz.halo_rows // 8 * (w // 128)):
                    piece = jnp.zeros((8, 128), f32)
                    for slot in range(4):
                        g = part * 4 + slot
                        if g < sz.groups:
                            piece = piece + pltpu.roll(halo[g * 8 : g * 8 + 8], slot * 32, 1)
                    bits.append(piece)
                wide = w // 128
                bits = [
                    jnp.concatenate(bits[i * wide : (i + 1) * wide], axis=1)
                    for i in range(sz.halo_rows // 8)
                ]
                parts = [r[mine].astype(f32), slab[:, :w]] + bits
                gap = sz.total - sz.halo_at - sz.halo_rows
                if gap:
                    parts.append(jnp.zeros((gap, w), f32))
                out[c, : sz.sw_rows] = sw[mine]
                out[c, sz.sw_rows :] = jnp.concatenate(parts, axis=0).astype(bf16)

    vmem, smem = pl.BlockSpec(memory_space=pltpu.VMEM), pl.BlockSpec(memory_space=pltpu.SMEM)
    return pl.pallas_call(
        body,
        in_specs=[smem] + [vmem] * 11,
        out_shape=(jax.ShapeDtypeStruct((tiles, sz.rows, sz.lanes), bf16),)
        + tuple(jax.ShapeDtypeStruct((per_owner, sz.total, w), bf16) for _ in peers),
        compiler_params=pltpu.CompilerParams(vmem_limit_bytes=VMEM_LIMIT),
        cost_estimate=pl.CostEstimate(flops=1_000_000, bytes_accessed=1_000_000, transcendentals=0),
        name="pack",
    )


def models(sz, n_epoch, tiles, count, ks, first, last, carried):
    per_owner = count // n_epoch
    h, w = sz.height, sz.width
    total_models = (2 * len(ks) + first) * per_owner

    def body(inter, sci, sw, r, slabs, *refs):
        refs = list(refs)
        pays = [refs.pop(0) for _ in ks]
        before = [] if first else [refs.pop(0) for _ in range(2)]
        done = [refs.pop(0) for _ in carried]
        if last:
            resid_out, coadd_out = refs.pop(0), refs.pop(0)
        else:
            numer_out, denom_out = refs.pop(0), refs.pop(0)
            resid_outs = [refs.pop(0) for _ in range(len(ks) + first)]
        rhs, lhs, numer, denom = refs
        me, _ = here("epoch")
        strip, strips = here("strip")
        band, bands = here("band")
        row = (strip * h + iota((h, w), 0)).astype(f32)
        col = (band * w + iota((h, w), 1)).astype(f32)
        r_unit = (2.0 * row + 1.0) / (h * strips) - 1.0
        c_unit = (2.0 * col + 1.0) / (w * bands) - 1.0
        for slot in range(2):
            for i in range(sz.chunks):
                used = min(sz.per, KS - i * sz.per) * sz.span
                if used < CHUNK:
                    rhs[slot, i * CHUNK + used : (i + 1) * CHUNK] = jnp.zeros((CHUNK - used, w), bf16)
        turn = [0]

        def model(slab, rows_of):
            slot = turn[0] % 2
            turn[0] += 1
            window, band_rows = rhs.at[slot], lhs.at[slot]
            down = rows_of[NPOLY, 0].astype(jnp.int32)
            across = rows_of[NPOLY, 1].astype(jnp.int32)
            slab = pltpu.roll(slab, lax.rem(sz.rows + HALF - down, sz.rows), 0)[: sz.span]
            slab = pltpu.roll(slab, lax.rem(sz.lanes + HALF - across, sz.lanes), 1).astype(bf16)
            for b in range(KS):
                at = b // sz.per * CHUNK + b % sz.per * sz.span
                window[at : at + sz.span] = slab[:, b : b + w]
            for p in range(NPOLY):
                for i in range(sz.chunks):
                    line = rows_of[i * SLOT + p : i * SLOT + p + 1]
                    line = pltpu.roll(
                        jnp.broadcast_to(line, (h, CHUNK)), 0, 1, stride=1, stride_axis=0
                    )
                    band_rows[p * h : (p + 1) * h, i * CHUNK : (i + 1) * CHUNK] = line
            conv = jnp.dot(band_rows[...].astype(bf16), window[...], preferred_element_type=f32)
            conv = [conv[p * h : (p + 1) * h] for p in range(NPOLY)]
            return (
                conv[0]
                + r_unit * (conv[1] + r_unit * conv[3] + c_unit * conv[4])
                + c_unit * (conv[2] + c_unit * conv[5])
            )

        def add(tile, pair, image):
            science = pair[:h] + pair[h : 2 * h]
            weight = pair[2 * h : 3 * h] + pair[3 * h : 4 * h]
            numer[tile] = numer[tile] + weight * (science - image)
            denom[tile] = denom[tile] + weight

        def tile_of(q, c):
            return jnp.clip(inter[q * count + me * per_owner + c] - me * tiles, 0, tiles - 1)

        def keep(j, c, mine, image):
            value = sci[mine] - image
            if last:
                resid_out[mine] = value
            else:
                resid_outs[j][c] = value

        if first:
            numer[...] = jnp.zeros(numer.shape, f32)
            denom[...] = jnp.zeros(denom.shape, f32)
        else:
            numer[...] = before[0][...]
            denom[...] = before[1][...]
        if first:
            for c in range(per_owner):
                mine = me * per_owner + c
                tile = tile_of(me, c)
                image = model(slabs[tile].astype(f32), r[mine].astype(f32))
                keep(len(ks), c, mine, image)
                add(tile, sw[mine].astype(f32), image)
        for j, (k, pay) in enumerate(zip(ks, pays)):
            q = partner(me, n_epoch, k, True)
            for c in range(per_owner):
                mine = q * per_owner + c
                got = pay[c, sz.sw_rows :].astype(f32)
                tile = tile_of(q, c)
                image = model(slabs[tile].astype(f32), got[: sz.r_rows])
                add(tile, pay[c, : sz.sw_rows].astype(f32), image)
                main = got[sz.r_rows : sz.r_rows + sz.rows]
                halo = got[sz.r_rows + sz.rows :]
                wide = w // 128
                bits = []
                for g in range(sz.groups):
                    part, slot = g // 4, g % 4
                    line, side = part // wide, part % wide
                    piece = halo[line * 8 : line * 8 + 8, side * 128 : side * 128 + 128]
                    piece = pltpu.roll(piece, (128 - slot * 32) % 128, 1)
                    bits.append(piece)
                halo = jnp.concatenate(bits, axis=0)
                lane = iota(halo.shape, 1)
                halo = pltpu.roll(jnp.where(lane < 2 * REACH, halo, 0.0), 128 - REACH, 1)
                if sz.lanes - w != 128:
                    lane = iota(halo.shape, 1)
                    gap = sz.lanes - w - 256
                    pieces = [jnp.where(lane < 64, halo, 0.0)]
                    if gap:
                        pieces.append(jnp.zeros((sz.rows, gap), f32))
                    halo = jnp.concatenate(pieces + [jnp.where(lane < 64, 0.0, halo)], axis=1)
                image = model(jnp.concatenate([main, halo], axis=1), r[mine].astype(f32))
                keep(j, c, mine, image)
        if last:
            for (k, where), value in zip(carried, done):
                q = me if k == 0 else partner(me, n_epoch, k, True)
                for c in range(per_owner):
                    resid_out[q * per_owner + c] = value[c]
            coadd_out[...] = numer[...] / (denom[...] + 1.0)
        else:
            numer_out[...] = numer[...]
            denom_out[...] = denom[...]

    image = jax.ShapeDtypeStruct((per_owner, h, w), f32)
    sums = jax.ShapeDtypeStruct((tiles, h, w), f32)
    if last:
        out_shape = (jax.ShapeDtypeStruct((count, h, w), f32), sums)
    else:
        out_shape = (sums, sums) + (image,) * (len(ks) + first)
    vmem, smem = pl.BlockSpec(memory_space=pltpu.VMEM), pl.BlockSpec(memory_space=pltpu.SMEM)
    return pl.pallas_call(
        body,
        in_specs=[smem] + [vmem] * (4 + len(ks) + (0 if first else 2) + len(carried)),
        out_shape=out_shape,
        scratch_shapes=[
            pltpu.VMEM((2, sz.depth, w), bf16),
            pltpu.VMEM((2, NPOLY * h, sz.depth), f32),
            pltpu.VMEM((tiles, h, w), f32),
            pltpu.VMEM((tiles, h, w), f32),
        ],
        compiler_params=pltpu.CompilerParams(vmem_limit_bytes=VMEM_LIMIT),
        cost_estimate=pl.CostEstimate(
            flops=total_models * 400_000_000, bytes_accessed=1_000_000, transcendentals=0
        ),
        name="models",
    )


def neighbours(block, axis):
    count = lax.axis_size(axis)
    if count == 1:
        return block, block
    if count == 2:
        other = lax.ppermute(block, axis, [(0, 1), (1, 0)])
        return other, other
    forward = [(i, i + 1) for i in range(count - 1)]
    backward = [(i + 1, i) for i in range(count - 1)]
    return lax.ppermute(block, axis, forward), lax.ppermute(block, axis, backward)


def local(
    template, science, variance, bad_mask, intersection, offsets, basis_index, coefficients, basis
):
    n_epoch = lax.axis_size("epoch")
    tiles = template.shape[0]
    count, height, width = science.shape
    sz = Sizes(height, width)
    low, high = neighbours(template, "strip")
    left, right = neighbours(template, "band")
    r, sw = prepare(sz, count, basis_index.shape[1])(
        science,
        variance,
        bad_mask,
        offsets.T,
        basis_index,
        coefficients.transpose(2, 0, 1),
        basis.transpose(1, 2, 0),
    )
    low_left, low_right = neighbours(low, "band")
    if high is low:
        high_left, high_right = low_left, low_right
    else:
        high_left, high_right = neighbours(high, "band")
    peers = list(range(1, n_epoch))
    slabs, *sends = pack(sz, n_epoch, tiles, count, peers)(
        intersection, template, low, high, left, low_left, high_left, right, low_right, high_right, sw, r
    )
    pays = {}
    for k, send in zip(peers, sends):
        pairs = [(i, partner(i, n_epoch, k, False)) for i in range(n_epoch)]
        pays[k] = lax.ppermute(send, "epoch", pairs)
    stages = [[]] + [[k] for k in reversed(peers)]
    sums, carried = [], []
    for i, ks in enumerate(stages):
        first, last = i == 0, i == len(stages) - 1
        kept = [(k, j) for j, (k, _) in enumerate(carried)] if last else []
        out = models(sz, n_epoch, tiles, count, ks, first, last, kept)(
            intersection,
            science,
            sw,
            r,
            slabs,
            *[pays[k] for k in ks],
            *sums,
            *([value for _, value in carried] if last else []),
        )
        if last:
            return out
        sums = list(out[:2])
        carried += list(zip(list(ks) + ([0] if first else []), out[2:]))


def solution(mesh):
    in_specs = (
        P(("groups", "epoch"), "strip", "band"),
        P(("groups", "epoch"), "strip", "band"),
        P(("groups", "epoch"), "strip", "band"),
        P(("groups", "epoch"), "strip", "band"),
        P("groups"),
        P(("groups", "epoch"), None),
        P(("groups", "epoch"), None),
        P(("groups", "epoch"), None, None),
        P(),
    )
    out_specs = (P(("groups", "epoch"), "strip", "band"), P(("groups", "epoch"), "strip", "band"))
    return jax.shard_map(local, mesh=mesh, in_specs=in_specs, out_specs=out_specs, check_vma=False)
```

time: 87.6 us -> 30.8 us (0.35)
  blocking collectives: 15.2 us -> 0 us
  local copies, waits for them, and re-layouts: 19.1 us -> 5.66 us
  loops' own time: 10.6 us -> 0 us
  starting transfers between devices: 18.2 us -> 7.79 us
  Pallas kernels: 0 us -> 9.09 us
  matrix products: 7.48 us -> 0 us
  waiting for transfers between devices: 11.8 us -> 7.28 us
  other arithmetic: 3.59 us -> 0 us
    all_gather x1 -> x0, blocking collectives: 15.2 us -> none  [local(): piece = lax.all_gather(template, 'epoch', axis=0, tiled=True)]
    all_to_all x2 -> x0, waiting for transfers between devices: 11.3 us -> none  [the longest x1 5.71 us: local(): lax.all_to_all(weighted.reshape(n_epoch, per_owner, height, width), 'epoc...]
    another operation x1 -> x0, loops' own time: 10.6 us -> none  [local(): models = lax.map(one_model, (padded, offsets, kernels))]
    concatenate x4 -> x0, local copies, waits for them, and re-layouts: 9.31 us -> none  [one_model(): jnp.concatenate([window[:, column:column + width] for column in range(KS)...]
    pallas_call x0 -> x6, Pallas kernels: none -> 9.09 us  [the longest x4 7.23 us: local(): models(sz, n_epoch, tiles, count, ks, first, last, kept)]
    all_to_all x2 -> x0, starting transfers between devices: 8.03 us -> none  [the longest x1 4.72 us: local(): lax.all_to_all(weighted.reshape(n_epoch, per_owner, height, width), 'epoc...]
    dot_general x11 -> x0, matrix products: 7.48 us -> none  [the longest x1 4.52 us: local(): jnp.einsum('ejp,ejab->epab', coefficients, picked, precision=highest)]
    ppermute x4 -> x6, waiting for transfers between devices: 0.57 us -> 7.28 us  [the longest x3 5.26 us: local(): pays[k] = lax.ppermute(send, 'epoch', pairs)]
  transfers between devices with their start and end apart: 6 -> 6, of which waited for: 3 -> 3; matrix products, arithmetic and copies ran while one was open for 11% -> 0% of each run, Pallas kernels for 0% -> 19%
where the time goes in v1:
time: 30.8 us; the launch traced here: 30.5 us
  Pallas kernels  9.09 us (30%)
  starting transfers between devices  7.79 us (25%)
  waiting for transfers between devices  7.28 us (24%)
  local copies, waits for them, and re-layouts  5.66 us (18%)
  between operations  0.71 us (2%)
    pallas_call x4, Pallas kernels, local(): models(sz, n_epoch, tiles, count, ks, first, last, kept)  7.23 us
    unnamed x18, local copies, waits for them, and re-layouts  5.66 us
    ppermute x3, waiting for transfers between devices, local(): pays[k] = lax.ppermute(send, 'epoch', pairs)  5.26 us
    ppermute x3, starting transfers between devices, local(): pays[k] = lax.ppermute(send, 'epoch', pairs)  4.78 us
    ppermute x3, starting transfers between devices, neighbours(): other = lax.ppermute(block, axis, [(0, 1), (1, 0)])  3.01 us
    ppermute x3, waiting for transfers between devices, neighbours(): other = lax.ppermute(block, axis, [(0, 1), (1, 0)])  2.02 us
    pallas_call x1, Pallas kernels, local(): prepare(sz, count, basis_index.shape[1])  1.13 us
    pallas_call x1, Pallas kernels, local(): pack(sz, n_epoch, tiles, count, peers)  0.73 us
  transfers between devices with their start and end apart: 6, of which 3 were waited for; matrix products, arithmetic and copies ran while one was open for 0% of the time, Pallas kernels for 19%

profile of v1, /device:TPU:0, one launch (start us, length us, event | category | flops | bytes accessed | tf_op | source)
XLA Modules:
  0.0 30.5 jit_solution(12402634827709639002)
XLA Ops:
  0.6 3.0 %collective-permute-start = (bf16[2,24,256]{2,1,0:T(8,128)(2,1)}, bf16[2,24,256]{2,1,0:T(8,128)(2,1)S(1)}, u32[]{:S(2)}, u32[]{:S(2)}) collective-permute-start(bf16[2,24,256]{2,1,0:T(8,128)(2,1)} %own.1), channel_id=1, source_target_pairs={{0,2},{2,0},{1,3},{3,1},{4,6},{6,4},{5,7},{7,5},{8,10},{10,8},{9,1... | collective-permute-start | bytes 73736 | tf_op jit(solution)/shard_map/ppermute | solution.py:357
  3.6 0.0 collective-permute-start.1
  3.6 2.0 %collective-permute-done.low.high = bf16[2,24,256]{2,1,0:T(8,128)(2,1)S(1)} collective-permute-done((bf16[2,24,256]{2,1,0:T(8,128)(2,1)}, bf16[2,24,256]{2,1,0:T(8,128)(2,1)S(1)}, u32[]{:S(2)}, u32[]{:S(2)}) %collective-permute-start) | collective-permute-done | bytes 24608 | tf_op jit(solution)/shard_map/ppermute | solution.py:357
  5.7 0.0 collective-permute-start.2
  5.7 0.0 copy-start.7
  5.7 0.0 copy-start.8
  5.7 0.7 %copy-done.7 = s32[4,16]{1,0:T(4,128)S(1)} copy-done((s32[4,16]{1,0:T(4,128)S(1)}, s32[4,16]{1,0:T(4,128)}, u32[]{:S(2)}) %copy-start.7) | copy-done | bytes 280
  6.3 0.0 copy-done.8
  6.4 0.0 copy-start.2
  6.4 0.9 %copy-done.2 = f32[49,19,19]{0,2,1:T(8,128)S(1)} copy-done((f32[49,19,19]{0,2,1:T(8,128)S(1)}, f32[49,19,19]{0,2,1:T(8,128)}, u32[]{:S(2)}) %copy-start.2) | copy-done | bytes 70780
  7.3 0.9 %copy-done.3 = f32[4,24,256]{2,1,0:T(8,128)S(1)} copy-done((f32[4,24,256]{2,1,0:T(8,128)S(1)}, f32[4,24,256]{2,1,0:T(8,128)}, u32[]{:S(2)}) %copy-start.3) | copy-done | bytes 98328
  8.2 0.0 copy-start.4
  8.2 0.9 %copy-done.4 = s32[4,24,256]{2,1,0:T(8,128)S(1)} copy-done((s32[4,24,256]{2,1,0:T(8,128)S(1)}, s32[4,24,256]{2,1,0:T(8,128)}, u32[]{:S(2)}) %copy-start.4) | copy-done | bytes 98328
  9.1 0.9 %copy-done.5 = f32[4,24,256]{2,1,0:T(8,128)S(1)} copy-done((f32[4,24,256]{2,1,0:T(8,128)S(1)}, f32[4,24,256]{2,1,0:T(8,128)}, u32[]{:S(2)}) %copy-start.5) | copy-done | bytes 98328
  10.0 0.7 %copy-done.6 = f32[4,16,6]{1,0,2:T(4,128)S(1)} copy-done((f32[4,16,6]{1,0,2:T(4,128)S(1)}, f32[4,16,6]{1,0,2:T(4,128)}, u32[]{:S(2)}) %copy-start.6) | copy-done | bytes 1560
  10.7 1.1 %prepare.1 = (bf16[4,32,256]{2,1,0:T(8,128)(2,1)S(1)}, bf16[4,96,256]{2,1,0:T(8,128)(2,1)S(1)}) custom-call(f32[4,24,256]{2,1,0:T(8,128)S(1)} %copy-done.5, f32[4,24,256]{2,1,0:T(8,128)S(1)} %copy-done.3, s32[4,24,256]{2,1,0:T(8,128)S(1)} %copy-done.4, s32[2,4]{1,0:T(2,128)S(1)} %bitcast.5, s32[4,16]{1,0:T(4,128)S(1)} %copy-done.7, f32[6,4,16]{2,1,0:T(4,128)S(1)} %bitcast.4, ...), custom_call_target="tpu_custom_call" | custom-call | flops 200000000 | bytes 3000000 | tf_op jit(solution)/shard_map/prepare/pallas_call | solution.py:373
  11.8 0.0 collective-permute-done.1.left.right
  11.8 0.0 collective-permute-done.2.low_left.high_left.low_right.high_right
  11.8 0.0 copy-start.1
  11.8 0.0 copy-done
  11.9 0.6 %copy-done.1 = s32[16]{0:T(128)S(1)} copy-done((s32[16]{0:T(128)S(1)}, s32[16]{0:T(128)}, u32[]{:S(2)}) %copy-start.1) | copy-done | bytes 88
  12.5 0.7 %pack.1 = (bf16[2,56,384]{2,1,0:T(8,128)(2,1)S(1)}, bf16[1,192,256]{2,1,0:T(8,128)(2,1)S(1)}, bf16[1,192,256]{2,1,0:T(8,128)(2,1)S(1)}, bf16[1,192,256]{2,1,0:T(8,128)(2,1)S(1)}) custom-call(s32[16]{0:T(128)S(1)} %copy-done.1, bf16[2,24,256]{2,1,0:T(8,128)(2,1)S(1)} %copy-done, bf16[2,24,256]{2,1,0:T(8,128)(2,1)S(1)} %collective-permute-done.low.high, ...), custom_call_target="tpu_custom_call" | custom-call | flops 1000000 | bytes 1000000 | tf_op jit(solution)/shard_map/pack/pallas_call | solution.py:388
  13.2 4.1 %collective-permute-start.5 = (bf16[1,192,256]{2,1,0:T(8,128)(2,1)S(1)}, bf16[1,192,256]{2,1,0:T(8,128)(2,1)S(1)}, u32[]{:S(2)}, u32[]{:S(2)}) collective-permute-start(bf16[1,192,256]{2,1,0:T(8,128)(2,1)S(1)} %get-tuple-element.22), channel_id=1, source_target_pairs={{0,12},{4,8},{8,4},{12,0},{1,13},{5,9},{9,5},{13,1},{2,14},{6,10},... | collective-permute-start | bytes 294920 | tf_op jit(solution)/shard_map/ppermute | solution.py:394
  17.4 0.0 collective-permute-start.3
  17.4 0.6 %collective-permute-start.4 = (bf16[1,192,256]{2,1,0:T(8,128)(2,1)S(1)}, bf16[1,192,256]{2,1,0:T(8,128)(2,1)S(1)}, u32[]{:S(2)}, u32[]{:S(2)}) collective-permute-start(bf16[1,192,256]{2,1,0:T(8,128)(2,1)S(1)} %get-tuple-element.21), channel_id=1, source_target_pairs={{0,8},{4,12},{8,0},{12,4},{1,9},{5,13},{9,1},{13,5},{2,10},{6,14},... | collective-permute-start | bytes 294920 | tf_op jit(solution)/shard_map/ppermute | solution.py:394
  18.0 1.2 %models.4 = (f32[2,24,256]{2,1,0:T(8,128)S(1)}, f32[2,24,256]{2,1,0:T(8,128)S(1)}, f32[1,24,256]{2,1,0:T(8,128)S(1)}) custom-call(s32[16]{0:T(128)S(1)} %copy-done.1, f32[4,24,256]{2,1,0:T(8,128)S(1)} %copy-done.5, bf16[4,96,256]{2,1,0:T(8,128)(2,1)S(1)} %get-tuple-element.17.sw, bf16[4,32,256]{2,1,0:T(8,128)(2,1)S(1)} %get-tuple-element.18.r, ...), custom_call_target="tpu_custom_call" | custom-call | flops 400000000 | bytes 1000000 | tf_op jit(solution)/shard_map/models/pallas_call | solution.py:400
  19.3 1.8 %collective-permute-done.5.refs_0_ = bf16[1,192,256]{2,1,0:T(8,128)(2,1)S(1)} collective-permute-done((bf16[1,192,256]{2,1,0:T(8,128)(2,1)S(1)}, bf16[1,192,256]{2,1,0:T(8,128)(2,1)S(1)}, u32[]{:S(2)}, u32[]{:S(2)}) %collective-permute-start.5) | collective-permute-done | bytes 98336 | tf_op jit(solution)/shard_map/ppermute | solution.py:394
  21.1 1.8 %models.5 = (f32[2,24,256]{2,1,0:T(8,128)S(1)}, f32[2,24,256]{2,1,0:T(8,128)S(1)}, f32[1,24,256]{2,1,0:T(8,128)S(1)}) custom-call(s32[16]{0:T(128)S(1)} %copy-done.1, f32[4,24,256]{2,1,0:T(8,128)S(1)} %copy-done.5, bf16[4,96,256]{2,1,0:T(8,128)(2,1)S(1)} %get-tuple-element.17.sw, bf16[4,32,256]{2,1,0:T(8,128)(2,1)S(1)} %get-tuple-element.18.r, ...), custom_call_target="tpu_custom_call" | custom-call | flops 800000000 | bytes 1000000 | tf_op jit(solution)/shard_map/models/pallas_call | solution.py:400
  22.8 3.5 %collective-permute-done.4.refs_0_ = bf16[1,192,256]{2,1,0:T(8,128)(2,1)S(1)} collective-permute-done((bf16[1,192,256]{2,1,0:T(8,128)(2,1)S(1)}, bf16[1,192,256]{2,1,0:T(8,128)(2,1)S(1)}, u32[]{:S(2)}, u32[]{:S(2)}) %collective-permute-start.4) | collective-permute-done | bytes 98336 | tf_op jit(solution)/shard_map/ppermute | solution.py:394
  26.3 1.8 %models.6 = (f32[2,24,256]{2,1,0:T(8,128)S(1)}, f32[2,24,256]{2,1,0:T(8,128)S(1)}, f32[1,24,256]{2,1,0:T(8,128)S(1)}) custom-call(s32[16]{0:T(128)S(1)} %copy-done.1, f32[4,24,256]{2,1,0:T(8,128)S(1)} %copy-done.5, bf16[4,96,256]{2,1,0:T(8,128)(2,1)S(1)} %get-tuple-element.17.sw, bf16[4,32,256]{2,1,0:T(8,128)(2,1)S(1)} %get-tuple-element.18.r, ...), custom_call_target="tpu_custom_call" | custom-call | flops 800000000 | bytes 1000000 | tf_op jit(solution)/shard_map/models/pallas_call | solution.py:400
  28.1 0.0 collective-permute-done.3.refs_0_
  28.1 2.4 %models.7 = (f32[4,24,256]{2,1,0:T(8,128)}, f32[2,24,256]{2,1,0:T(8,128)}) custom-call(s32[16]{0:T(128)S(1)} %copy-done.1, f32[4,24,256]{2,1,0:T(8,128)S(1)} %copy-done.5, bf16[4,96,256]{2,1,0:T(8,128)(2,1)S(1)} %get-tuple-element.17.sw, bf16[4,32,256]{2,1,0:T(8,128)(2,1)S(1)} %get-tuple-element.18.r, bf16[2,56,384]{2,1,0:T(8,128)(2,1)S(1)} %get-tuple-element.19.slabs, ...), custom_call_target="tpu_custom_call" | custom-call | flops 800000000 | bytes 1000000 | tf_op jit(solution)/shard_map/models/pallas_call | solution.py:400
  (4 shorter events, 0.0 us)
Async XLA Ops:
  0.6 5.0 %collective-permute-start = (bf16[2,24,256]{2,1,0:T(8,128)(2,1)}, bf16[2,24,256]{2,1,0:T(8,128)(2,1)S(1)}, u32[]{:S(2)}, u32[]{:S(2)}) collective-permute-start(bf16[2,24,256]{2,1,0:T(8,128)(2,1)} %own.1), channel_id=1, source_target_pairs={{0,2},{2,0},{1,3},{3,1},{4,6},{6,4},{5,7},{7,5},{8,10},{10,8},{9,1... | collective-permute-start | bytes 73736 | tf_op jit(solution)/shard_map/ppermute | solution.py:357
  3.6 8.2 %collective-permute-start.1 = (bf16[2,24,256]{2,1,0:T(8,128)(2,1)}, bf16[2,24,256]{2,1,0:T(8,128)(2,1)S(1)}, u32[]{:S(2)}, u32[]{:S(2)}) collective-permute-start(bf16[2,24,256]{2,1,0:T(8,128)(2,1)} %own.1), channel_id=1, source_target_pairs={{0,1},{1,0},{2,3},{3,2},{4,5},{5,4},{6,7},{7,6},{8,9},{9,8},{10,11... | collective-permute-start | bytes 73736 | tf_op jit(solution)/shard_map/ppermute | solution.py:357
  5.7 6.2 %collective-permute-start.2 = (bf16[2,24,256]{2,1,0:T(8,128)(2,1)S(1)}, bf16[2,24,256]{2,1,0:T(8,128)(2,1)S(1)}, u32[]{:S(2)}, u32[]{:S(2)}) collective-permute-start(bf16[2,24,256]{2,1,0:T(8,128)(2,1)S(1)} %collective-permute-done.low.high), channel_id=1, source_target_pairs={{0,1},{1,0},{2,3},{3,2},{4,5},{5,4},{6,7},{7,6},{8,9},{9,8},{10,11... | collective-permute-start | bytes 73736 | tf_op jit(solution)/shard_map/ppermute | solution.py:357
  5.7 0.7 %copy-start.7 = (s32[4,16]{1,0:T(4,128)S(1)}, s32[4,16]{1,0:T(4,128)}, u32[]{:S(2)}) copy-start(s32[4,16]{1,0:T(4,128)} %index.1) | copy-start | bytes 772
  5.7 0.7 %copy-start.8 = (s32[4,2]{0,1:T(2,128)S(1)}, s32[4,2]{0,1:T(2,128)}, u32[]{:S(2)}) copy-start(s32[4,2]{0,1:T(2,128)} %param.14) | copy-start | bytes 100
  6.4 0.9 %copy-start.2 = (f32[49,19,19]{0,2,1:T(8,128)S(1)}, f32[49,19,19]{0,2,1:T(8,128)}, u32[]{:S(2)}) copy-start(f32[49,19,19]{0,2,1:T(8,128)} %param.17) | copy-start | bytes 212272
  7.3 0.9 %copy-start.3 = (f32[4,24,256]{2,1,0:T(8,128)S(1)}, f32[4,24,256]{2,1,0:T(8,128)}, u32[]{:S(2)}) copy-start(f32[4,24,256]{2,1,0:T(8,128)} %var.1) | copy-start | bytes 294916
  8.2 0.9 %copy-start.4 = (s32[4,24,256]{2,1,0:T(8,128)S(1)}, s32[4,24,256]{2,1,0:T(8,128)}, u32[]{:S(2)}) copy-start(s32[4,24,256]{2,1,0:T(8,128)} %mask.1) | copy-start | bytes 294916
  9.1 0.9 %copy-start.5 = (f32[4,24,256]{2,1,0:T(8,128)S(1)}, f32[4,24,256]{2,1,0:T(8,128)}, u32[]{:S(2)}) copy-start(f32[4,24,256]{2,1,0:T(8,128)} %sci.9) | copy-start | bytes 294916
  10.0 0.7 %copy-start.6 = (f32[4,16,6]{1,0,2:T(4,128)S(1)}, f32[4,16,6]{1,0,2:T(4,128)}, u32[]{:S(2)}) copy-start(f32[4,16,6]{1,0,2:T(4,128)} %param.16) | copy-start | bytes 4612
  10.7 1.2 %copy-start = (bf16[2,24,256]{2,1,0:T(8,128)(2,1)S(1)}, bf16[2,24,256]{2,1,0:T(8,128)(2,1)}, u32[]{:S(2)}) copy-start(bf16[2,24,256]{2,1,0:T(8,128)(2,1)} %own.1) | copy-start | bytes 73732
  11.8 0.7 %copy-start.1 = (s32[16]{0:T(128)S(1)}, s32[16]{0:T(128)}, u32[]{:S(2)}) copy-start(s32[16]{0:T(128)} %inter.9) | copy-start | bytes 196
  13.2 7.8 %collective-permute-start.5 = (bf16[1,192,256]{2,1,0:T(8,128)(2,1)S(1)}, bf16[1,192,256]{2,1,0:T(8,128)(2,1)S(1)}, u32[]{:S(2)}, u32[]{:S(2)}) collective-permute-start(bf16[1,192,256]{2,1,0:T(8,128)(2,1)S(1)} %get-tuple-element.22), channel_id=1, source_target_pairs={{0,12},{4,8},{8,4},{12,0},{1,13},{5,9},{9,5},{13,1},{2,14},{6,10},... | collective-permute-start | bytes 294920 | tf_op jit(solution)/shard_map/ppermute | solution.py:394
  17.4 10.7 %collective-permute-start.3 = (bf16[1,192,256]{2,1,0:T(8,128)(2,1)S(1)}, bf16[1,192,256]{2,1,0:T(8,128)(2,1)S(1)}, u32[]{:S(2)}, u32[]{:S(2)}) collective-permute-start(bf16[1,192,256]{2,1,0:T(8,128)(2,1)S(1)} %get-tuple-element.20), channel_id=1, source_target_pairs={{0,4},{4,0},{8,12},{12,8},{1,5},{5,1},{9,13},{13,9},{2,6},{6,2},{1... | collective-permute-start | bytes 294920 | tf_op jit(solution)/shard_map/ppermute | solution.py:394
  17.4 8.9 %collective-permute-start.4 = (bf16[1,192,256]{2,1,0:T(8,128)(2,1)S(1)}, bf16[1,192,256]{2,1,0:T(8,128)(2,1)S(1)}, u32[]{:S(2)}, u32[]{:S(2)}) collective-permute-start(bf16[1,192,256]{2,1,0:T(8,128)(2,1)S(1)} %get-tuple-element.21), channel_id=1, source_target_pairs={{0,8},{4,12},{8,0},{12,4},{1,9},{5,13},{9,1},{13,5},{2,10},{6,14},... | collective-permute-start | bytes 294920 | tf_op jit(solution)/shard_map/ppermute | solution.py:394

commit v2 on v1

--- a/solution.py
+++ b/solution.py
@@ -12,6 +12,7 @@
 REACH = HALF + SHIFT
 SLOT = 8
 CHUNK = 256
+FINE = 24
 VMEM_LIMIT = 24 * 1024 * 1024
 
 highest = lax.Precision.HIGHEST
@@ -24,21 +25,30 @@
 
 
 class Sizes:
-    def __init__(self, height, width):
+    def __init__(self, height, width, strips):
         self.height, self.width = height, width
         self.rows = up(height + 2 * REACH, 8)
         self.lanes = up(width + 2 * REACH, 128)
-        self.span = up(height + KS - 1, 16)
+        self.span = up(height + KS - 1, 2 * FINE)
+        self.phases = self.span // FINE
         self.per = CHUNK // self.span
-        self.chunks = -(-KS // self.per)
+        self.lines = -(-KS // (self.per * self.phases))
+        self.chunks = self.lines * self.phases
         self.depth = self.chunks * CHUNK
         self.sw_rows = 4 * height
-        self.r_rows = self.chunks * SLOT
+        self.r_rows = self.lines * SLOT
+        self.one_side = strips <= 2
+        self.sent = height + 16 if self.one_side else self.rows
         self.main_at = self.sw_rows + self.r_rows
-        self.halo_at = self.main_at + self.rows
-        self.groups = self.rows // 8
+        self.halo_at = self.main_at + self.sent
+        self.groups = self.sent // 8
         self.halo_rows = up(self.groups * 32, width) // width * 8
-        self.total = up(self.halo_at + self.halo_rows, 16)
+        self.total = self.halo_at + self.halo_rows
+
+    def columns(self, chunk):
+        line, phase = divmod(chunk, self.phases)
+        first = line * self.per * self.phases + phase
+        return [b for b in range(first, first + self.per * self.phases, self.phases) if b < KS]
 
 
 def iota(shape, axis):
@@ -50,27 +60,38 @@
     return high, value - high
 
 
-def prepare(sz, count, nsel):
+def prepare(sz, n_epoch, tiles, count, nsel):
     lanes = count * SLOT
+    per_owner = count // n_epoch
+    width = sz.lines * CHUNK
     nbasis = 128
 
-    def body(sci, var, mask, offs, index, coef, basis, r_out, sw_out, table, place):
-        for e in range(count):
-            s_high, s_low = split(sci[e])
-            w_high, w_low = split(mask[e].astype(f32) / var[e])
-            sw_out[e] = jnp.concatenate([s_high, s_low, w_high, w_low], axis=0).astype(bf16)
+    def body(*refs):
+        sources, refs = refs[:9], refs[9:]
+        r_out, sw_out, own_out, sci_out = refs[:4]
+        var, mask, inter, offs, index, coef, basis, table, place, sems = refs[4:]
+        targets = [own_out, sci_out, var, mask, inter, offs, index, coef, basis]
+        copies = [
+            pltpu.make_async_copy(source, target, sems.at[i])
+            for i, (source, target) in enumerate(zip(sources, targets))
+        ]
+        for copy in reversed(copies):
+            copy.start()
+        me, _ = here("epoch")
         table[...] = jnp.zeros(table.shape, f32)
-        for a in range(KS):
-            table[a * 24 : a * 24 + KS, : basis.shape[2]] = basis[a]
-        col = iota((24, sz.depth), 0)
-        base = (col // sz.per) * CHUNK + (col % sz.per) * sz.span
-        lane = iota((24, sz.depth), 1)
-        base = jnp.where(col < KS, lane - base, -1)
+        col = iota((FINE, width), 0)
+        whole = sz.per * sz.phases
+        base = iota((FINE, width), 1) - (col // whole) * CHUNK - (col % whole) * FINE
+        base = jnp.where(col < KS, base, -1)
         for a in range(0, KS + 1, 2):
             pair = jnp.concatenate([(base == a).astype(f32), (base == a + 1).astype(f32)], axis=0)
             if a + 1 == KS:
-                pair = jnp.where(iota(pair.shape, 0) < 24, pair, 0.0)
-            place[a * 24 : a * 24 + 48] = pair.astype(bf16)
+                pair = jnp.where(iota(pair.shape, 0) < FINE, pair, 0.0)
+            place[a * FINE : (a + 2) * FINE] = pair.astype(bf16)
+        for copy in reversed(copies[4:]):
+            copy.wait()
+        for a in range(KS):
+            table[a * FINE : a * FINE + KS, : basis.shape[2]] = basis[a]
         chosen = jnp.concatenate([index[e : e + 1, :] for e in range(count)], axis=1)
         onehot = (iota((nbasis, count * nsel), 0) == chosen).astype(f32)
         blocks = []
@@ -89,28 +110,56 @@
         for e in range(count):
             mine = rows[e * SLOT : (e + 1) * SLOT]
             mine = jnp.concatenate(
-                [mine[:, i * CHUNK : (i + 1) * CHUNK] for i in range(sz.chunks)], axis=0
+                [mine[:, i * CHUNK : (i + 1) * CHUNK] for i in range(sz.lines)], axis=0
             )
+            tile = inter[e // per_owner * count + me * per_owner + e % per_owner] - me * tiles
+            tile = jnp.clip(tile, 0, tiles - 1).astype(f32)
             down, across = offs[0:1, e : e + 1].astype(f32), offs[1:2, e : e + 1].astype(f32)
-            spot_row, spot = iota(mine.shape, 0), iota(mine.shape, 1)
-            spare = spot_row == NPOLY
-            mine = jnp.where(spare & (spot == 0), down, jnp.where(spare & (spot == 1), across, mine))
+            spare, spot = iota(mine.shape, 0) == NPOLY, iota(mine.shape, 1)
+            for lane, value in enumerate((down, across, tile)):
+                mine = jnp.where(spare & (spot == lane), value, mine)
             r_out[e] = mine.astype(bf16)
-
-    return pl.pallas_call(
-        body,
-        out_shape=(
-            jax.ShapeDtypeStruct((count, sz.r_rows, CHUNK), bf16),
-            jax.ShapeDtypeStruct((count, sz.sw_rows, sz.width), bf16),
-        ),
-        scratch_shapes=[
-            pltpu.VMEM(((KS + 1) * 24, nbasis), f32),
-            pltpu.VMEM(((KS + 1) * 24, sz.depth), bf16),
-        ],
-        compiler_params=pltpu.CompilerParams(vmem_limit_bytes=VMEM_LIMIT),
-        cost_estimate=pl.CostEstimate(flops=200_000_000, bytes_accessed=3_000_000, transcendentals=0),
-        name="prepare",
-    )
+        for copy in reversed(copies[:4]):
+            copy.wait()
+        for e in range(count):
+            s_high, s_low = split(sci_out[e])
+            w_high, w_low = split(mask[e].astype(f32) / var[e])
+            sw_out[e] = jnp.concatenate([s_high, s_low, w_high, w_low], axis=0).astype(bf16)
+
+    hbm, vmem = pl.BlockSpec(memory_space=pltpu.HBM), pl.BlockSpec(memory_space=pltpu.VMEM)
+    shape = (count, sz.height, sz.width)
+
+    def call(template, science, variance, mask, inter, offs, index, coef, basis):
+        return pl.pallas_call(
+            body,
+            in_specs=[hbm] * 9,
+            out_specs=(vmem,) * 4,
+            out_shape=(
+                jax.ShapeDtypeStruct((count, sz.r_rows, CHUNK), bf16),
+                jax.ShapeDtypeStruct((count, sz.sw_rows, sz.width), bf16),
+                jax.ShapeDtypeStruct(template.shape, bf16),
+                jax.ShapeDtypeStruct(shape, f32),
+            ),
+            scratch_shapes=[
+                pltpu.VMEM(shape, f32),
+                pltpu.VMEM(shape, jnp.int32),
+                pltpu.SMEM(inter.shape, jnp.int32),
+                pltpu.VMEM(offs.shape, jnp.int32),
+                pltpu.VMEM(index.shape, jnp.int32),
+                pltpu.VMEM(coef.shape, f32),
+                pltpu.VMEM(basis.shape, f32),
+                pltpu.VMEM(((KS + 1) * FINE, nbasis), f32),
+                pltpu.VMEM(((KS + 1) * FINE, width), bf16),
+                pltpu.SemaphoreType.DMA((9,)),
+            ],
+            compiler_params=pltpu.CompilerParams(vmem_limit_bytes=VMEM_LIMIT),
+            cost_estimate=pl.CostEstimate(
+                flops=1_000_000_000, bytes_accessed=6_000_000, transcendentals=0
+            ),
+            name="prepare",
+        )(template, science, variance, mask, inter, offs, index, coef, basis)
+
+    return call
 
 
 def here(axis):
@@ -127,7 +176,7 @@
     per_owner = count // n_epoch
     h, w = sz.height, sz.width
 
-    def body(inter, own, low, high, left, low_left, high_left, right, low_right, high_right, sw, r, *outs):
+    def body(own, low, high, left, low_left, high_left, right, low_right, high_right, sw, r, *outs):
         slabs, sends = outs[0], outs[1:]
         me, _ = here("epoch")
         strip, strips = here("strip")
@@ -159,10 +208,13 @@
         for k, out in zip(peers, sends):
             q = partner(me, n_epoch, k, False)
             for c in range(per_owner):
-                tile = inter[q * count + me * per_owner + c] - me * tiles
-                tile = jnp.clip(tile, 0, tiles - 1)
                 mine = q * per_owner + c
+                lines = r[mine].astype(f32)
+                tile = lines[NPOLY, 2].astype(jnp.int32)
                 slab = slabs[tile].astype(f32)
+                if sz.one_side:
+                    side = jnp.where(strip == 0, slab[h : h + 16], slab[sz.rows - 16 :])
+                    slab = jnp.concatenate([slab[:h], side], axis=0)
                 halo = pltpu.roll(slab[:, sz.lanes - 128 :], REACH, 1)
                 if sz.lanes - w != 128:
                     halo = halo + pltpu.roll(slab[:, w : w + 128], REACH, 1)
@@ -180,17 +232,14 @@
                     jnp.concatenate(bits[i * wide : (i + 1) * wide], axis=1)
                     for i in range(sz.halo_rows // 8)
                 ]
-                parts = [r[mine].astype(f32), slab[:, :w]] + bits
-                gap = sz.total - sz.halo_at - sz.halo_rows
-                if gap:
-                    parts.append(jnp.zeros((gap, w), f32))
+                parts = [lines, slab[:, :w]] + bits
                 out[c, : sz.sw_rows] = sw[mine]
                 out[c, sz.sw_rows :] = jnp.concatenate(parts, axis=0).astype(bf16)
 
-    vmem, smem = pl.BlockSpec(memory_space=pltpu.VMEM), pl.BlockSpec(memory_space=pltpu.SMEM)
+    vmem = pl.BlockSpec(memory_space=pltpu.VMEM)
     return pl.pallas_call(
         body,
-        in_specs=[smem] + [vmem] * 11,
+        in_specs=[vmem] * 11,
         out_shape=(jax.ShapeDtypeStruct((tiles, sz.rows, sz.lanes), bf16),)
         + tuple(jax.ShapeDtypeStruct((per_owner, sz.total, w), bf16) for _ in peers),
         compiler_params=pltpu.CompilerParams(vmem_limit_bytes=VMEM_LIMIT),
@@ -204,7 +253,7 @@
     h, w = sz.height, sz.width
     total_models = (2 * len(ks) + first) * per_owner
 
-    def body(inter, sci, sw, r, slabs, *refs):
+    def body(sci, sw, r, slabs, *refs):
         refs = list(refs)
         pays = [refs.pop(0) for _ in ks]
         before = [] if first else [refs.pop(0) for _ in range(2)]
@@ -224,7 +273,7 @@
         c_unit = (2.0 * col + 1.0) / (w * bands) - 1.0
         for slot in range(2):
             for i in range(sz.chunks):
-                used = min(sz.per, KS - i * sz.per) * sz.span
+                used = len(sz.columns(i)) * sz.span
                 if used < CHUNK:
                     rhs[slot, i * CHUNK + used : (i + 1) * CHUNK] = jnp.zeros((CHUNK - used, w), bf16)
         turn = [0]
@@ -237,12 +286,19 @@
             across = rows_of[NPOLY, 1].astype(jnp.int32)
             slab = pltpu.roll(slab, lax.rem(sz.rows + HALF - down, sz.rows), 0)[: sz.span]
             slab = pltpu.roll(slab, lax.rem(sz.lanes + HALF - across, sz.lanes), 1).astype(bf16)
-            for b in range(KS):
-                at = b // sz.per * CHUNK + b % sz.per * sz.span
-                window[at : at + sz.span] = slab[:, b : b + w]
-            for p in range(NPOLY):
-                for i in range(sz.chunks):
-                    line = rows_of[i * SLOT + p : i * SLOT + p + 1]
+            for i in range(sz.chunks):
+                for slot, b in enumerate(sz.columns(i)):
+                    at = i * CHUNK + slot * sz.span
+                    window[at : at + sz.span] = slab[:, b : b + w]
+            for i in range(sz.chunks):
+                line, phase = divmod(i, sz.phases)
+                lines = rows_of[line * SLOT : (line + 1) * SLOT]
+                if phase:
+                    lines = pltpu.roll(lines, CHUNK - phase * FINE, 1)
+                spot = iota(lines.shape, 1)
+                lines = jnp.where((spot % sz.span < FINE) & (spot < sz.per * sz.span), lines, 0.0)
+                for p in range(NPOLY):
+                    line = lines[p : p + 1]
                     line = pltpu.roll(
                         jnp.broadcast_to(line, (h, CHUNK)), 0, 1, stride=1, stride_axis=0
                     )
@@ -261,8 +317,8 @@
             numer[tile] = numer[tile] + weight * (science - image)
             denom[tile] = denom[tile] + weight
 
-        def tile_of(q, c):
-            return jnp.clip(inter[q * count + me * per_owner + c] - me * tiles, 0, tiles - 1)
+        def tile_of(lines):
+            return lines[NPOLY, 2].astype(jnp.int32)
 
         def keep(j, c, mine, image):
             value = sci[mine] - image
@@ -280,8 +336,9 @@
         if first:
             for c in range(per_owner):
                 mine = me * per_owner + c
-                tile = tile_of(me, c)
-                image = model(slabs[tile].astype(f32), r[mine].astype(f32))
+                lines = r[mine].astype(f32)
+                tile = tile_of(lines)
+                image = model(slabs[tile].astype(f32), lines)
                 keep(len(ks), c, mine, image)
                 add(tile, sw[mine].astype(f32), image)
         for j, (k, pay) in enumerate(zip(ks, pays)):
@@ -289,11 +346,12 @@
             for c in range(per_owner):
                 mine = q * per_owner + c
                 got = pay[c, sz.sw_rows :].astype(f32)
-                tile = tile_of(q, c)
+                lines = r[mine].astype(f32)
+                tile = tile_of(lines)
                 image = model(slabs[tile].astype(f32), got[: sz.r_rows])
                 add(tile, pay[c, : sz.sw_rows].astype(f32), image)
-                main = got[sz.r_rows : sz.r_rows + sz.rows]
-                halo = got[sz.r_rows + sz.rows :]
+                main = got[sz.r_rows : sz.r_rows + sz.sent]
+                halo = got[sz.r_rows + sz.sent :]
                 wide = w // 128
                 bits = []
                 for g in range(sz.groups):
@@ -310,9 +368,15 @@
                     gap = sz.lanes - w - 256
                     pieces = [jnp.where(lane < 64, halo, 0.0)]
                     if gap:
-                        pieces.append(jnp.zeros((sz.rows, gap), f32))
+                        pieces.append(jnp.zeros((sz.sent, gap), f32))
                     halo = jnp.concatenate(pieces + [jnp.where(lane < 64, 0.0, halo)], axis=1)
-                image = model(jnp.concatenate([main, halo], axis=1), r[mine].astype(f32))
+                slab = jnp.concatenate([main, halo], axis=1)
+                if sz.one_side:
+                    side, none = slab[h:], jnp.zeros((sz.rows - h - 32, sz.lanes), f32)
+                    below, above = jnp.where(strip == 0, side, 0.0), jnp.where(strip == 0, 0.0, side)
+                    slab = [slab[:h], below, none, above] if none.size else [slab[:h], below, above]
+                    slab = jnp.concatenate(slab, axis=0)
+                image = model(slab, lines)
                 keep(j, c, mine, image)
         if last:
             for (k, where), value in zip(carried, done):
@@ -330,10 +394,10 @@
         out_shape = (jax.ShapeDtypeStruct((count, h, w), f32), sums)
     else:
         out_shape = (sums, sums) + (image,) * (len(ks) + first)
-    vmem, smem = pl.BlockSpec(memory_space=pltpu.VMEM), pl.BlockSpec(memory_space=pltpu.SMEM)
+    vmem = pl.BlockSpec(memory_space=pltpu.VMEM)
     return pl.pallas_call(
         body,
-        in_specs=[smem] + [vmem] * (4 + len(ks) + (0 if first else 2) + len(carried)),
+        in_specs=[vmem] * (4 + len(ks) + (0 if first else 2) + len(carried)),
         out_shape=out_shape,
         scratch_shapes=[
             pltpu.VMEM((2, sz.depth, w), bf16),
@@ -367,13 +431,15 @@
     n_epoch = lax.axis_size("epoch")
     tiles = template.shape[0]
     count, height, width = science.shape
-    sz = Sizes(height, width)
+    sz = Sizes(height, width, lax.axis_size("strip"))
     low, high = neighbours(template, "strip")
     left, right = neighbours(template, "band")
-    r, sw = prepare(sz, count, basis_index.shape[1])(
+    r, sw, own, sci = prepare(sz, n_epoch, tiles, count, basis_index.shape[1])(
+        template,
         science,
         variance,
         bad_mask,
+        intersection,
         offsets.T,
         basis_index,
         coefficients.transpose(2, 0, 1),
@@ -385,21 +451,21 @@
     else:
         high_left, high_right = neighbours(high, "band")
     peers = list(range(1, n_epoch))
+    order = peers[-1:] + peers[:-1]
     slabs, *sends = pack(sz, n_epoch, tiles, count, peers)(
-        intersection, template, low, high, left, low_left, high_left, right, low_right, high_right, sw, r
+        own, low, high, left, low_left, high_left, right, low_right, high_right, sw, r
     )
     pays = {}
-    for k, send in zip(peers, sends):
+    for k, send in zip(order, [sends[peers.index(k)] for k in order]):
         pairs = [(i, partner(i, n_epoch, k, False)) for i in range(n_epoch)]
         pays[k] = lax.ppermute(send, "epoch", pairs)
-    stages = [[]] + [[k] for k in reversed(peers)]
+    stages = [[]] + [[k] for k in order]
     sums, carried = [], []
     for i, ks in enumerate(stages):
         first, last = i == 0, i == len(stages) - 1
         kept = [(k, j) for j, (k, _) in enumerate(carried)] if last else []
         out = models(sz, n_epoch, tiles, count, ks, first, last, kept)(
-            intersection,
-            science,
+            sci,
             sw,
             r,
             slabs,

time: 30.8 us -> 27.5 us (0.89)
  waiting for transfers between devices: 7.28 us -> 5.3 us
  Pallas kernels: 9.09 us -> 7.57 us
    ppermute x3, waiting for transfers between devices: 5.26 us -> 3.28 us  [local(): pays[k] = lax.ppermute(send, 'epoch', pairs)]
    pallas_call x4, Pallas kernels: 7.23 us -> 5.66 us  [local(): models(sz, n_epoch, tiles, count, ks, first, last, kept)]
    pallas_call x1, Pallas kernels: 1.13 us -> 1.63 us  [call(): pl.pallas_call(body, in_specs=[hbm] * 9, out_specs=(vmem,) * 4, out_shape...]
    pallas_call x1, Pallas kernels: 0.73 us -> 0.28 us  [local(): pack(sz, n_epoch, tiles, count, peers)]
  transfers between devices with their start and end apart: 6 -> 6, of which waited for: 3 -> 4; matrix products, arithmetic and copies ran while one was open for 0% -> 0% of each run, Pallas kernels for 19% -> 19%
where the time goes in v2:
time: 27.5 us; the launch traced here: 27.2 us
  starting transfers between devices  7.85 us (29%)
  Pallas kernels  7.57 us (28%)
  local copies, waits for them, and re-layouts  5.75 us (21%)
  waiting for transfers between devices  5.3 us (19%)
  between operations  0.7 us (3%)
    unnamed x18, local copies, waits for them, and re-layouts  5.75 us
    pallas_call x4, Pallas kernels, local(): models(sz, n_epoch, tiles, count, ks, first, last, kept)  5.66 us
    ppermute x3, starting transfers between devices, local(): pays[k] = lax.ppermute(send, 'epoch', pairs)  4.84 us
    ppermute x3, waiting for transfers between devices, local(): pays[k] = lax.ppermute(send, 'epoch', pairs)  3.28 us
    ppermute x3, starting transfers between devices, neighbours(): other = lax.ppermute(block, axis, [(0, 1), (1, 0)])  3.01 us
    ppermute x3, waiting for transfers between devices, neighbours(): other = lax.ppermute(block, axis, [(0, 1), (1, 0)])  2.02 us
    pallas_call x1, Pallas kernels, call(): pl.pallas_call(body, in_specs=[hbm] * 9, out_specs=(vmem,) * 4, out_shape...  1.63 us
  transfers between devices with their start and end apart: 6, of which 4 were waited for; matrix products, arithmetic and copies ran while one was open for 0% of the time, Pallas kernels for 19%

profile of v2, /device:TPU:0, one launch (start us, length us, event | category | flops | bytes accessed | tf_op | source)
XLA Modules:
  0.0 27.2 jit_solution(3901560336550203006)
XLA Ops:
  0.6 3.0 %collective-permute-start = (bf16[2,24,256]{2,1,0:T(8,128)(2,1)}, bf16[2,24,256]{2,1,0:T(8,128)(2,1)S(1)}, u32[]{:S(2)}, u32[]{:S(2)}) collective-permute-start(bf16[2,24,256]{2,1,0:T(8,128)(2,1)} %refs_0_.1), channel_id=1, source_target_pairs={{0,2},{2,0},{1,3},{3,1},{4,6},{6,4},{5,7},{7,5},{8,10},{10,8},{9,1... | collective-permute-start | bytes 73736 | tf_op jit(solution)/shard_map/ppermute | solution.py:421
  3.6 0.0 collective-permute-start.1
  3.6 2.0 %collective-permute-done.low.high = bf16[2,24,256]{2,1,0:T(8,128)(2,1)S(1)} collective-permute-done((bf16[2,24,256]{2,1,0:T(8,128)(2,1)}, bf16[2,24,256]{2,1,0:T(8,128)(2,1)S(1)}, u32[]{:S(2)}, u32[]{:S(2)}) %collective-permute-start) | collective-permute-done | bytes 24608 | tf_op jit(solution)/shard_map/ppermute | solution.py:421
  5.7 0.0 collective-permute-start.2
  5.7 0.0 copy-start.6
  5.7 0.0 copy-start.7
  5.7 0.0 copy-start.8
  5.7 0.7 %copy-done.6 = s32[4,16]{1,0:T(4,128)S(1)} copy-done((s32[4,16]{1,0:T(4,128)S(1)}, s32[4,16]{1,0:T(4,128)}, u32[]{:S(2)}) %copy-start.6) | copy-done | bytes 280
  6.3 0.0 copy-done.7
  6.4 0.0 copy-done.8
  6.4 0.0 copy-start
  6.4 0.9 %copy-done = f32[49,19,19]{0,2,1:T(8,128)S(1)} copy-done((f32[49,19,19]{0,2,1:T(8,128)S(1)}, f32[49,19,19]{0,2,1:T(8,128)}, u32[]{:S(2)}) %copy-start) | copy-done | bytes 70780
  7.3 0.0 copy-start.1
  7.3 0.9 %copy-done.1 = f32[4,24,256]{2,1,0:T(8,128)S(1)} copy-done((f32[4,24,256]{2,1,0:T(8,128)S(1)}, f32[4,24,256]{2,1,0:T(8,128)}, u32[]{:S(2)}) %copy-start.1) | copy-done | bytes 98328
  8.2 0.9 %copy-done.2 = f32[4,24,256]{2,1,0:T(8,128)S(1)} copy-done((f32[4,24,256]{2,1,0:T(8,128)S(1)}, f32[4,24,256]{2,1,0:T(8,128)}, u32[]{:S(2)}) %copy-start.2) | copy-done | bytes 98328
  9.1 0.9 %copy-done.3 = s32[4,24,256]{2,1,0:T(8,128)S(1)} copy-done((s32[4,24,256]{2,1,0:T(8,128)S(1)}, s32[4,24,256]{2,1,0:T(8,128)}, u32[]{:S(2)}) %copy-start.3) | copy-done | bytes 98328
  10.0 0.7 %copy-done.4 = bf16[2,24,256]{2,1,0:T(8,128)(2,1)S(1)} copy-done((bf16[2,24,256]{2,1,0:T(8,128)(2,1)S(1)}, bf16[2,24,256]{2,1,0:T(8,128)(2,1)}, u32[]{:S(2)}) %copy-start.4) | copy-done | bytes 24600
  10.7 0.7 %copy-done.5 = f32[4,16,6]{1,0,2:T(4,128)S(1)} copy-done((f32[4,16,6]{1,0,2:T(4,128)S(1)}, f32[4,16,6]{1,0,2:T(4,128)}, u32[]{:S(2)}) %copy-start.5) | copy-done | bytes 1560
  11.4 1.6 %prepare.1 = (bf16[4,16,256]{2,1,0:T(8,128)(2,1)S(1)}, bf16[4,96,256]{2,1,0:T(8,128)(2,1)S(1)}, bf16[2,24,256]{2,1,0:T(8,128)(2,1)S(1)}, f32[4,24,256]{2,1,0:T(8,128)S(1)}) custom-call(bf16[2,24,256]{2,1,0:T(8,128)(2,1)S(1)} %copy-done.4, f32[4,24,256]{2,1,0:T(8,128)S(1)} %copy-done.1, f32[4,24,256]{2,1,0:T(8,128)S(1)} %copy-done.2, ...), custom_call_target="tpu_custom_call" | custom-call | flops 1000000000 | bytes 6000000 | tf_op jit(solution)/shard_map/prepare/pallas_call | solution.py:133
  13.1 0.0 collective-permute-done.1.left.right
  13.1 0.0 collective-permute-done.2.low_left.high_left.low_right.high_right
  13.1 0.3 %pack.1 = (bf16[2,56,384]{2,1,0:T(8,128)(2,1)S(1)}, bf16[1,160,256]{2,1,0:T(8,128)(2,1)S(1)}, bf16[1,160,256]{2,1,0:T(8,128)(2,1)S(1)}, bf16[1,160,256]{2,1,0:T(8,128)(2,1)S(1)}) custom-call(bf16[2,24,256]{2,1,0:T(8,128)(2,1)S(1)} %get-tuple-element.22.own, bf16[2,24,256]{2,1,0:T(8,128)(2,1)S(1)} %collective-permute-done.low.high, ...), custom_call_target="tpu_custom_call" | custom-call | flops 1000000 | bytes 1000000 | tf_op jit(solution)/shard_map/pack/pallas_call | solution.py:455
  13.4 4.2 %collective-permute-start.5 = (bf16[1,160,256]{2,1,0:T(8,128)(2,1)S(1)}, bf16[1,160,256]{2,1,0:T(8,128)(2,1)S(1)}, u32[]{:S(2)}, u32[]{:S(2)}) collective-permute-start(bf16[1,160,256]{2,1,0:T(8,128)(2,1)S(1)} %get-tuple-element.26), channel_id=1, source_target_pairs={{0,12},{4,8},{8,4},{12,0},{1,13},{5,9},{9,5},{13,1},{2,14},{6,10},... | collective-permute-start | bytes 245768 | tf_op jit(solution)/shard_map/ppermute | solution.py:461
  17.6 0.0 collective-permute-start.3
  17.6 0.6 %collective-permute-start.4 = (bf16[1,160,256]{2,1,0:T(8,128)(2,1)S(1)}, bf16[1,160,256]{2,1,0:T(8,128)(2,1)S(1)}, u32[]{:S(2)}, u32[]{:S(2)}) collective-permute-start(bf16[1,160,256]{2,1,0:T(8,128)(2,1)S(1)} %get-tuple-element.25), channel_id=1, source_target_pairs={{0,4},{4,0},{8,12},{12,8},{1,5},{5,1},{9,13},{13,9},{2,6},{6,2},{1... | collective-permute-start | bytes 245768 | tf_op jit(solution)/shard_map/ppermute | solution.py:461
  18.2 0.7 %models.4 = (f32[2,24,256]{2,1,0:T(8,128)S(1)}, f32[2,24,256]{2,1,0:T(8,128)S(1)}, f32[1,24,256]{2,1,0:T(8,128)S(1)}) custom-call(f32[4,24,256]{2,1,0:T(8,128)S(1)} %get-tuple-element.19.sci, bf16[4,96,256]{2,1,0:T(8,128)(2,1)S(1)} %get-tuple-element.20.sw, bf16[4,16,256]{2,1,0:T(8,128)(2,1)S(1)} %get-tuple-element.21.r, ...), custom_call_target="tpu_custom_call" | custom-call | flops 400000000 | bytes 1000000 | tf_op jit(solution)/shard_map/models/pallas_call | solution.py:467
  18.9 2.0 %collective-permute-done.5.refs_0_ = bf16[1,160,256]{2,1,0:T(8,128)(2,1)S(1)} collective-permute-done((bf16[1,160,256]{2,1,0:T(8,128)(2,1)S(1)}, bf16[1,160,256]{2,1,0:T(8,128)(2,1)S(1)}, u32[]{:S(2)}, u32[]{:S(2)}) %collective-permute-start.5) | collective-permute-done | bytes 81952 | tf_op jit(solution)/shard_map/ppermute | solution.py:461
  21.0 1.4 %models.5 = (f32[2,24,256]{2,1,0:T(8,128)S(1)}, f32[2,24,256]{2,1,0:T(8,128)S(1)}, f32[1,24,256]{2,1,0:T(8,128)S(1)}) custom-call(f32[4,24,256]{2,1,0:T(8,128)S(1)} %get-tuple-element.19.sci, bf16[4,96,256]{2,1,0:T(8,128)(2,1)S(1)} %get-tuple-element.20.sw, bf16[4,16,256]{2,1,0:T(8,128)(2,1)S(1)} %get-tuple-element.21.r, ...), custom_call_target="tpu_custom_call" | custom-call | flops 800000000 | bytes 1000000 | tf_op jit(solution)/shard_map/models/pallas_call | solution.py:467
  22.4 1.1 %collective-permute-done.4.refs_0_ = bf16[1,160,256]{2,1,0:T(8,128)(2,1)S(1)} collective-permute-done((bf16[1,160,256]{2,1,0:T(8,128)(2,1)S(1)}, bf16[1,160,256]{2,1,0:T(8,128)(2,1)S(1)}, u32[]{:S(2)}, u32[]{:S(2)}) %collective-permute-start.4) | collective-permute-done | bytes 81952 | tf_op jit(solution)/shard_map/ppermute | solution.py:461
  23.5 1.4 %models.6 = (f32[2,24,256]{2,1,0:T(8,128)S(1)}, f32[2,24,256]{2,1,0:T(8,128)S(1)}, f32[1,24,256]{2,1,0:T(8,128)S(1)}) custom-call(f32[4,24,256]{2,1,0:T(8,128)S(1)} %get-tuple-element.19.sci, bf16[4,96,256]{2,1,0:T(8,128)(2,1)S(1)} %get-tuple-element.20.sw, bf16[4,16,256]{2,1,0:T(8,128)(2,1)S(1)} %get-tuple-element.21.r, ...), custom_call_target="tpu_custom_call" | custom-call | flops 800000000 | bytes 1000000 | tf_op jit(solution)/shard_map/models/pallas_call | solution.py:467
  24.9 0.2 collective-permute-done.3.refs_0_
  25.1 2.1 %models.7 = (f32[4,24,256]{2,1,0:T(8,128)}, f32[2,24,256]{2,1,0:T(8,128)}) custom-call(f32[4,24,256]{2,1,0:T(8,128)S(1)} %get-tuple-element.19.sci, bf16[4,96,256]{2,1,0:T(8,128)(2,1)S(1)} %get-tuple-element.20.sw, bf16[4,16,256]{2,1,0:T(8,128)(2,1)S(1)} %get-tuple-element.21.r, bf16[2,56,384]{2,1,0:T(8,128)(2,1)S(1)} %get-tuple-element.23.slabs, ...), custom_call_target="tpu_custom_call" | custom-call | flops 800000000 | bytes 1000000 | tf_op jit(solution)/shard_map/models/pallas_call | solution.py:467
  (4 shorter events, 0.0 us)
Async XLA Ops:
  0.6 5.0 %collective-permute-start = (bf16[2,24,256]{2,1,0:T(8,128)(2,1)}, bf16[2,24,256]{2,1,0:T(8,128)(2,1)S(1)}, u32[]{:S(2)}, u32[]{:S(2)}) collective-permute-start(bf16[2,24,256]{2,1,0:T(8,128)(2,1)} %refs_0_.1), channel_id=1, source_target_pairs={{0,2},{2,0},{1,3},{3,1},{4,6},{6,4},{5,7},{7,5},{8,10},{10,8},{9,1... | collective-permute-start | bytes 73736 | tf_op jit(solution)/shard_map/ppermute | solution.py:421
  3.6 9.4 %collective-permute-start.1 = (bf16[2,24,256]{2,1,0:T(8,128)(2,1)}, bf16[2,24,256]{2,1,0:T(8,128)(2,1)S(1)}, u32[]{:S(2)}, u32[]{:S(2)}) collective-permute-start(bf16[2,24,256]{2,1,0:T(8,128)(2,1)} %refs_0_.1), channel_id=1, source_target_pairs={{0,1},{1,0},{2,3},{3,2},{4,5},{5,4},{6,7},{7,6},{8,9},{9,8},{10,11... | collective-permute-start | bytes 73736 | tf_op jit(solution)/shard_map/ppermute | solution.py:421
  5.7 7.4 %collective-permute-start.2 = (bf16[2,24,256]{2,1,0:T(8,128)(2,1)S(1)}, bf16[2,24,256]{2,1,0:T(8,128)(2,1)S(1)}, u32[]{:S(2)}, u32[]{:S(2)}) collective-permute-start(bf16[2,24,256]{2,1,0:T(8,128)(2,1)S(1)} %collective-permute-done.low.high), channel_id=1, source_target_pairs={{0,1},{1,0},{2,3},{3,2},{4,5},{5,4},{6,7},{7,6},{8,9},{9,8},{10,11... | collective-permute-start | bytes 73736 | tf_op jit(solution)/shard_map/ppermute | solution.py:421
  5.7 0.7 %copy-start.6 = (s32[4,16]{1,0:T(4,128)S(1)}, s32[4,16]{1,0:T(4,128)}, u32[]{:S(2)}) copy-start(s32[4,16]{1,0:T(4,128)} %refs_6_.1) | copy-start | bytes 772
  5.7 0.7 %copy-start.7 = (s32[4,2]{0,1:T(2,128)S(1)}, s32[4,2]{0,1:T(2,128)}, u32[]{:S(2)}) copy-start(s32[4,2]{0,1:T(2,128)} %param.14) | copy-start | bytes 100
  5.7 0.7 %copy-start.8 = (s32[16]{0:T(128)S(1)}, s32[16]{0:T(128)}, u32[]{:S(2)}) copy-start(s32[16]{0:T(128)} %refs_4_.1) | copy-start | bytes 196
  6.4 0.9 %copy-start = (f32[49,19,19]{0,2,1:T(8,128)S(1)}, f32[49,19,19]{0,2,1:T(8,128)}, u32[]{:S(2)}) copy-start(f32[49,19,19]{0,2,1:T(8,128)} %param.17) | copy-start | bytes 212272
  7.3 0.9 %copy-start.1 = (f32[4,24,256]{2,1,0:T(8,128)S(1)}, f32[4,24,256]{2,1,0:T(8,128)}, u32[]{:S(2)}) copy-start(f32[4,24,256]{2,1,0:T(8,128)} %refs_1_.1) | copy-start | bytes 294916
  8.2 0.9 %copy-start.2 = (f32[4,24,256]{2,1,0:T(8,128)S(1)}, f32[4,24,256]{2,1,0:T(8,128)}, u32[]{:S(2)}) copy-start(f32[4,24,256]{2,1,0:T(8,128)} %refs_2_.1) | copy-start | bytes 294916
  9.1 0.9 %copy-start.3 = (s32[4,24,256]{2,1,0:T(8,128)S(1)}, s32[4,24,256]{2,1,0:T(8,128)}, u32[]{:S(2)}) copy-start(s32[4,24,256]{2,1,0:T(8,128)} %refs_3_.1) | copy-start | bytes 294916
  10.0 0.7 %copy-start.4 = (bf16[2,24,256]{2,1,0:T(8,128)(2,1)S(1)}, bf16[2,24,256]{2,1,0:T(8,128)(2,1)}, u32[]{:S(2)}) copy-start(bf16[2,24,256]{2,1,0:T(8,128)(2,1)} %refs_0_.1) | copy-start | bytes 73732
  10.7 0.7 %copy-start.5 = (f32[4,16,6]{1,0,2:T(4,128)S(1)}, f32[4,16,6]{1,0,2:T(4,128)}, u32[]{:S(2)}) copy-start(f32[4,16,6]{1,0,2:T(4,128)} %param.16) | copy-start | bytes 4612
  13.4 7.6 %collective-permute-start.5 = (bf16[1,160,256]{2,1,0:T(8,128)(2,1)S(1)}, bf16[1,160,256]{2,1,0:T(8,128)(2,1)S(1)}, u32[]{:S(2)}, u32[]{:S(2)}) collective-permute-start(bf16[1,160,256]{2,1,0:T(8,128)(2,1)S(1)} %get-tuple-element.26), channel_id=1, source_target_pairs={{0,12},{4,8},{8,4},{12,0},{1,13},{5,9},{9,5},{13,1},{2,14},{6,10},... | collective-permute-start | bytes 245768 | tf_op jit(solution)/shard_map/ppermute | solution.py:461
  17.6 7.5 %collective-permute-start.3 = (bf16[1,160,256]{2,1,0:T(8,128)(2,1)S(1)}, bf16[1,160,256]{2,1,0:T(8,128)(2,1)S(1)}, u32[]{:S(2)}, u32[]{:S(2)}) collective-permute-start(bf16[1,160,256]{2,1,0:T(8,128)(2,1)S(1)} %get-tuple-element.24), channel_id=1, source_target_pairs={{0,8},{4,12},{8,0},{12,4},{1,9},{5,13},{9,1},{13,5},{2,10},{6,14},... | collective-permute-start | bytes 245768 | tf_op jit(solution)/shard_map/ppermute | solution.py:461
  17.6 5.9 %collective-permute-start.4 = (bf16[1,160,256]{2,1,0:T(8,128)(2,1)S(1)}, bf16[1,160,256]{2,1,0:T(8,128)(2,1)S(1)}, u32[]{:S(2)}, u32[]{:S(2)}) collective-permute-start(bf16[1,160,256]{2,1,0:T(8,128)(2,1)S(1)} %get-tuple-element.25), channel_id=1, source_target_pairs={{0,4},{4,0},{8,12},{12,8},{1,5},{5,1},{9,13},{13,9},{2,6},{6,2},{1... | collective-permute-start | bytes 245768 | tf_op jit(solution)/shard_map/ppermute | solution.py:461

commit v3 on v2

--- a/solution.py
+++ b/solution.py
@@ -129,7 +129,8 @@
     hbm, vmem = pl.BlockSpec(memory_space=pltpu.HBM), pl.BlockSpec(memory_space=pltpu.VMEM)
     shape = (count, sz.height, sz.width)
 
-    def call(template, science, variance, mask, inter, offs, index, coef, basis):
+    def call(*sources):
+        template, _, _, _, inter, offs, index, coef, basis = sources
         return pl.pallas_call(
             body,
             in_specs=[hbm] * 9,
@@ -157,7 +158,7 @@
                 flops=1_000_000_000, bytes_accessed=6_000_000, transcendentals=0
             ),
             name="prepare",
-        )(template, science, variance, mask, inter, offs, index, coef, basis)
+        )(*[pltpu.with_memory_space_constraint(source, pltpu.HBM) for source in sources])
 
     return call
 
@@ -445,10 +446,13 @@
         coefficients.transpose(2, 0, 1),
         basis.transpose(1, 2, 0),
     )
-    low_left, low_right = neighbours(low, "band")
     if high is low:
-        high_left, high_right = low_left, low_right
+        low, r = lax.optimization_barrier((low, r))
+        high = low
+        high_left, high_right = low_left, low_right = neighbours(low, "band")
     else:
+        low, high, r = lax.optimization_barrier((low, high, r))
+        low_left, low_right = neighbours(low, "band")
         high_left, high_right = neighbours(high, "band")
     peers = list(range(1, n_epoch))
     order = peers[-1:] + peers[:-1]

time: 27.5 us -> 20.8 us (0.76)
  local copies, waits for them, and re-layouts: 5.75 us -> 0 us
  waiting for transfers between devices: 5.3 us -> 3.98 us
  Pallas kernels: 7.57 us -> 7.93 us
    unnamed x18 -> x0, local copies, waits for them, and re-layouts: 5.75 us -> none
    ppermute x3, waiting for transfers between devices: 2.02 us -> 1.04 us  [neighbours(): other = lax.ppermute(block, axis, [(0, 1), (1, 0)])]
    pallas_call x1, Pallas kernels: 1.63 us -> 2 us  [call(): pl.pallas_call(body, in_specs=[hbm] * 9, out_specs=(vmem,) * 4, out_shape...]
    ppermute x3, waiting for transfers between devices: 3.28 us -> 2.94 us  [local(): pays[k] = lax.ppermute(send, 'epoch', pairs)]
    ppermute x3, starting transfers between devices: 3.01 us -> 3.31 us  [neighbours(): other = lax.ppermute(block, axis, [(0, 1), (1, 0)])]
  transfers between devices with their start and end apart: 6 -> 6, of which waited for: 4 -> 4; matrix products, arithmetic and copies ran while one was open for 0% -> 0% of each run, Pallas kernels for 19% -> 27%
where the time goes in v3:
time: 20.8 us; the launch traced here: 20.7 us
  starting transfers between devices  8.08 us (39%)
  Pallas kernels  7.93 us (38%)
  waiting for transfers between devices  3.98 us (19%)
  between operations  0.67 us (3%)
    pallas_call x4, Pallas kernels, local(): models(sz, n_epoch, tiles, count, ks, first, last, kept)  5.66 us
    ppermute x3, starting transfers between devices, local(): pays[k] = lax.ppermute(send, 'epoch', pairs)  4.78 us
    ppermute x3, starting transfers between devices, neighbours(): other = lax.ppermute(block, axis, [(0, 1), (1, 0)])  3.31 us
    ppermute x3, waiting for transfers between devices, local(): pays[k] = lax.ppermute(send, 'epoch', pairs)  2.94 us
    pallas_call x1, Pallas kernels, call(): pl.pallas_call(body, in_specs=[hbm] * 9, out_specs=(vmem,) * 4, out_shape...  2 us
    ppermute x3, waiting for transfers between devices, neighbours(): other = lax.ppermute(block, axis, [(0, 1), (1, 0)])  1.04 us
  transfers between devices with their start and end apart: 6, of which 4 were waited for; matrix products, arithmetic and copies ran while one was open for 0% of the time, Pallas kernels for 27%

profile of v3, /device:TPU:0, one launch (start us, length us, event | category | flops | bytes accessed | tf_op | source)
XLA Modules:
  0.0 20.7 jit_solution(3226699563992578284)
XLA Ops:
  0.6 0.5 %collective-permute-start.1 = (bf16[2,24,256]{2,1,0:T(8,128)(2,1)}, bf16[2,24,256]{2,1,0:T(8,128)(2,1)S(1)}, u32[]{:S(2)}, u32[]{:S(2)}) collective-permute-start(bf16[2,24,256]{2,1,0:T(8,128)(2,1)} %refs_0_.1), channel_id=1, source_target_pairs={{0,1},{1,0},{2,3},{3,2},{4,5},{5,4},{6,7},{7,6},{8,9},{9,8},{10,11... | collective-permute-start | bytes 73736 | tf_op jit(solution)/shard_map/ppermute | solution.py:422
  1.2 2.6 %collective-permute-start = (bf16[2,24,256]{2,1,0:T(8,128)(2,1)}, bf16[2,24,256]{2,1,0:T(8,128)(2,1)S(1)}, u32[]{:S(2)}, u32[]{:S(2)}) collective-permute-start(bf16[2,24,256]{2,1,0:T(8,128)(2,1)} %refs_0_.1), channel_id=1, source_target_pairs={{0,2},{2,0},{1,3},{3,1},{4,6},{6,4},{5,7},{7,5},{8,10},{10,8},{9,1... | collective-permute-start | bytes 73736 | tf_op jit(solution)/shard_map/ppermute | solution.py:422
  3.7 2.0 %prepare.1 = (bf16[4,16,256]{2,1,0:T(8,128)(2,1)S(1)}, bf16[4,96,256]{2,1,0:T(8,128)(2,1)S(1)}, bf16[2,24,256]{2,1,0:T(8,128)(2,1)S(1)}, f32[4,24,256]{2,1,0:T(8,128)S(1)}) custom-call(bf16[2,24,256]{2,1,0:T(8,128)(2,1)} %refs_0_.1, f32[4,24,256]{2,1,0:T(8,128)} %refs_1_.1, f32[4,24,256]{2,1,0:T(8,128)} %refs_2_.1, s32[4,24,256]{2,1,0:T(8,128)} %refs_3_.1, ...), custom_call_target="tpu_custom_call" | custom-call | flops 1000000000 | bytes 6000000 | tf_op jit(solution)/shard_map/prepare/pallas_call | solution.py:134
  5.7 0.0 collective-permute-done.low.high
  5.7 0.2 %collective-permute-start.2 = (bf16[2,24,256]{2,1,0:T(8,128)(2,1)S(1)}, bf16[2,24,256]{2,1,0:T(8,128)(2,1)S(1)}, u32[]{:S(2)}, u32[]{:S(2)}) collective-permute-start(bf16[2,24,256]{2,1,0:T(8,128)(2,1)S(1)} %collective-permute-done.low.high), channel_id=1, source_target_pairs={{0,1},{1,0},{2,3},{3,2},{4,5},{5,4},{6,7},{7,6},{8,9},{9,8},{10,11... | collective-permute-start | bytes 73736 | tf_op jit(solution)/shard_map/ppermute | solution.py:422
  6.0 0.0 collective-permute-done.1.left.right
  6.0 1.0 %collective-permute-done.2.low_left.high_left.low_right.high_right = bf16[2,24,256]{2,1,0:T(8,128)(2,1)S(1)} collective-permute-done((bf16[2,24,256]{2,1,0:T(8,128)(2,1)S(1)}, bf16[2,24,256]{2,1,0:T(8,128)(2,1)S(1)}, u32[]{:S(2)}, u32[]{:S(2)}) %collective-permute-start.2) | collective-permute-done | bytes 24608 | tf_op jit(solution)/shard_map/ppermute | solution.py:422
  7.0 0.3 %pack.1 = (bf16[2,56,384]{2,1,0:T(8,128)(2,1)S(1)}, bf16[1,160,256]{2,1,0:T(8,128)(2,1)S(1)}, bf16[1,160,256]{2,1,0:T(8,128)(2,1)S(1)}, bf16[1,160,256]{2,1,0:T(8,128)(2,1)S(1)}) custom-call(bf16[2,24,256]{2,1,0:T(8,128)(2,1)S(1)} %get-tuple-element.25.own, bf16[2,24,256]{2,1,0:T(8,128)(2,1)S(1)} %collective-permute-done.low.high, ...), custom_call_target="tpu_custom_call" | custom-call | flops 1000000 | bytes 1000000 | tf_op jit(solution)/shard_map/pack/pallas_call | solution.py:459
  7.3 4.1 %collective-permute-start.5 = (bf16[1,160,256]{2,1,0:T(8,128)(2,1)S(1)}, bf16[1,160,256]{2,1,0:T(8,128)(2,1)S(1)}, u32[]{:S(2)}, u32[]{:S(2)}) collective-permute-start(bf16[1,160,256]{2,1,0:T(8,128)(2,1)S(1)} %get-tuple-element.30), channel_id=1, source_target_pairs={{0,12},{4,8},{8,4},{12,0},{1,13},{5,9},{9,5},{13,1},{2,14},{6,10},... | collective-permute-start | bytes 245768 | tf_op jit(solution)/shard_map/ppermute | solution.py:465
  11.4 0.0 collective-permute-start.3
  11.4 0.6 %collective-permute-start.4 = (bf16[1,160,256]{2,1,0:T(8,128)(2,1)S(1)}, bf16[1,160,256]{2,1,0:T(8,128)(2,1)S(1)}, u32[]{:S(2)}, u32[]{:S(2)}) collective-permute-start(bf16[1,160,256]{2,1,0:T(8,128)(2,1)S(1)} %get-tuple-element.29), channel_id=1, source_target_pairs={{0,4},{4,0},{8,12},{12,8},{1,5},{5,1},{9,13},{13,9},{2,6},{6,2},{1... | collective-permute-start | bytes 245768 | tf_op jit(solution)/shard_map/ppermute | solution.py:465
  12.0 0.7 %models.4 = (f32[2,24,256]{2,1,0:T(8,128)S(1)}, f32[2,24,256]{2,1,0:T(8,128)S(1)}, f32[1,24,256]{2,1,0:T(8,128)S(1)}) custom-call(f32[4,24,256]{2,1,0:T(8,128)S(1)} %get-tuple-element.21.sci, bf16[4,96,256]{2,1,0:T(8,128)(2,1)S(1)} %get-tuple-element.22.sw, bf16[4,16,256]{2,1,0:T(8,128)(2,1)S(1)} %get-tuple-element.24.r, ...), custom_call_target="tpu_custom_call" | custom-call | flops 400000000 | bytes 1000000 | tf_op jit(solution)/shard_map/models/pallas_call | solution.py:471
  12.8 2.0 %collective-permute-done.5.refs_0_ = bf16[1,160,256]{2,1,0:T(8,128)(2,1)S(1)} collective-permute-done((bf16[1,160,256]{2,1,0:T(8,128)(2,1)S(1)}, bf16[1,160,256]{2,1,0:T(8,128)(2,1)S(1)}, u32[]{:S(2)}, u32[]{:S(2)}) %collective-permute-start.5) | collective-permute-done | bytes 81952 | tf_op jit(solution)/shard_map/ppermute | solution.py:465
  14.7 1.4 %models.5 = (f32[2,24,256]{2,1,0:T(8,128)S(1)}, f32[2,24,256]{2,1,0:T(8,128)S(1)}, f32[1,24,256]{2,1,0:T(8,128)S(1)}) custom-call(f32[4,24,256]{2,1,0:T(8,128)S(1)} %get-tuple-element.21.sci, bf16[4,96,256]{2,1,0:T(8,128)(2,1)S(1)} %get-tuple-element.22.sw, bf16[4,16,256]{2,1,0:T(8,128)(2,1)S(1)} %get-tuple-element.24.r, ...), custom_call_target="tpu_custom_call" | custom-call | flops 800000000 | bytes 1000000 | tf_op jit(solution)/shard_map/models/pallas_call | solution.py:471
  16.2 0.8 %collective-permute-done.4.refs_0_ = bf16[1,160,256]{2,1,0:T(8,128)(2,1)S(1)} collective-permute-done((bf16[1,160,256]{2,1,0:T(8,128)(2,1)S(1)}, bf16[1,160,256]{2,1,0:T(8,128)(2,1)S(1)}, u32[]{:S(2)}, u32[]{:S(2)}) %collective-permute-start.4) | collective-permute-done | bytes 81952 | tf_op jit(solution)/shard_map/ppermute | solution.py:465
  17.0 1.4 %models.6 = (f32[2,24,256]{2,1,0:T(8,128)S(1)}, f32[2,24,256]{2,1,0:T(8,128)S(1)}, f32[1,24,256]{2,1,0:T(8,128)S(1)}) custom-call(f32[4,24,256]{2,1,0:T(8,128)S(1)} %get-tuple-element.21.sci, bf16[4,96,256]{2,1,0:T(8,128)(2,1)S(1)} %get-tuple-element.22.sw, bf16[4,16,256]{2,1,0:T(8,128)(2,1)S(1)} %get-tuple-element.24.r, ...), custom_call_target="tpu_custom_call" | custom-call | flops 800000000 | bytes 1000000 | tf_op jit(solution)/shard_map/models/pallas_call | solution.py:471
  18.4 0.2 collective-permute-done.3.refs_0_
  18.6 2.1 %models.7 = (f32[4,24,256]{2,1,0:T(8,128)}, f32[2,24,256]{2,1,0:T(8,128)}) custom-call(f32[4,24,256]{2,1,0:T(8,128)S(1)} %get-tuple-element.21.sci, bf16[4,96,256]{2,1,0:T(8,128)(2,1)S(1)} %get-tuple-element.22.sw, bf16[4,16,256]{2,1,0:T(8,128)(2,1)S(1)} %get-tuple-element.24.r, bf16[2,56,384]{2,1,0:T(8,128)(2,1)S(1)} %get-tuple-element.27.slabs, ...), custom_call_target="tpu_custom_call" | custom-call | flops 800000000 | bytes 1000000 | tf_op jit(solution)/shard_map/models/pallas_call | solution.py:471
Async XLA Ops:
  0.6 5.3 %collective-permute-start.1 = (bf16[2,24,256]{2,1,0:T(8,128)(2,1)}, bf16[2,24,256]{2,1,0:T(8,128)(2,1)S(1)}, u32[]{:S(2)}, u32[]{:S(2)}) collective-permute-start(bf16[2,24,256]{2,1,0:T(8,128)(2,1)} %refs_0_.1), channel_id=1, source_target_pairs={{0,1},{1,0},{2,3},{3,2},{4,5},{5,4},{6,7},{7,6},{8,9},{9,8},{10,11... | collective-permute-start | bytes 73736 | tf_op jit(solution)/shard_map/ppermute | solution.py:422
  1.2 4.6 %collective-permute-start = (bf16[2,24,256]{2,1,0:T(8,128)(2,1)}, bf16[2,24,256]{2,1,0:T(8,128)(2,1)S(1)}, u32[]{:S(2)}, u32[]{:S(2)}) collective-permute-start(bf16[2,24,256]{2,1,0:T(8,128)(2,1)} %refs_0_.1), channel_id=1, source_target_pairs={{0,2},{2,0},{1,3},{3,1},{4,6},{6,4},{5,7},{7,5},{8,10},{10,8},{9,1... | collective-permute-start | bytes 73736 | tf_op jit(solution)/shard_map/ppermute | solution.py:422
  5.7 1.3 %collective-permute-start.2 = (bf16[2,24,256]{2,1,0:T(8,128)(2,1)S(1)}, bf16[2,24,256]{2,1,0:T(8,128)(2,1)S(1)}, u32[]{:S(2)}, u32[]{:S(2)}) collective-permute-start(bf16[2,24,256]{2,1,0:T(8,128)(2,1)S(1)} %collective-permute-done.low.high), channel_id=1, source_target_pairs={{0,1},{1,0},{2,3},{3,2},{4,5},{5,4},{6,7},{7,6},{8,9},{9,8},{10,11... | collective-permute-start | bytes 73736 | tf_op jit(solution)/shard_map/ppermute | solution.py:422
  7.3 7.5 %collective-permute-start.5 = (bf16[1,160,256]{2,1,0:T(8,128)(2,1)S(1)}, bf16[1,160,256]{2,1,0:T(8,128)(2,1)S(1)}, u32[]{:S(2)}, u32[]{:S(2)}) collective-permute-start(bf16[1,160,256]{2,1,0:T(8,128)(2,1)S(1)} %get-tuple-element.30), channel_id=1, source_target_pairs={{0,12},{4,8},{8,4},{12,0},{1,13},{5,9},{9,5},{13,1},{2,14},{6,10},... | collective-permute-start | bytes 245768 | tf_op jit(solution)/shard_map/ppermute | solution.py:465
  11.4 7.2 %collective-permute-start.3 = (bf16[1,160,256]{2,1,0:T(8,128)(2,1)S(1)}, bf16[1,160,256]{2,1,0:T(8,128)(2,1)S(1)}, u32[]{:S(2)}, u32[]{:S(2)}) collective-permute-start(bf16[1,160,256]{2,1,0:T(8,128)(2,1)S(1)} %get-tuple-element.28), channel_id=1, source_target_pairs={{0,8},{4,12},{8,0},{12,4},{1,9},{5,13},{9,1},{13,5},{2,10},{6,14},... | collective-permute-start | bytes 245768 | tf_op jit(solution)/shard_map/ppermute | solution.py:465
  11.4 5.6 %collective-permute-start.4 = (bf16[1,160,256]{2,1,0:T(8,128)(2,1)S(1)}, bf16[1,160,256]{2,1,0:T(8,128)(2,1)S(1)}, u32[]{:S(2)}, u32[]{:S(2)}) collective-permute-start(bf16[1,160,256]{2,1,0:T(8,128)(2,1)S(1)} %get-tuple-element.29), channel_id=1, source_target_pairs={{0,4},{4,0},{8,12},{12,8},{1,5},{5,1},{9,13},{13,9},{2,6},{6,2},{1... | collective-permute-start | bytes 245768 | tf_op jit(solution)/shard_map/ppermute | solution.py:465

commit v4 on v3

--- a/solution.py
+++ b/solution.py
@@ -35,7 +35,7 @@
         self.lines = -(-KS // (self.per * self.phases))
         self.chunks = self.lines * self.phases
         self.depth = self.chunks * CHUNK
-        self.sw_rows = 4 * height
+        self.sw_rows = 3 * height
         self.r_rows = self.lines * SLOT
         self.one_side = strips <= 2
         self.sent = height + 16 if self.one_side else self.rows
@@ -45,10 +45,9 @@
         self.halo_rows = up(self.groups * 32, width) // width * 8
         self.total = self.halo_at + self.halo_rows
 
-    def columns(self, chunk):
-        line, phase = divmod(chunk, self.phases)
-        first = line * self.per * self.phases + phase
-        return [b for b in range(first, first + self.per * self.phases, self.phases) if b < KS]
+    def place(self, column):
+        slot, chunk = column // self.chunks, column % self.chunks
+        return chunk // self.phases * CHUNK + (slot * self.phases + chunk % self.phases) * FINE
 
 
 def iota(shape, axis):
@@ -58,6 +57,25 @@
 def split(value):
     high = value.astype(bf16).astype(f32)
     return high, value - high
+
+
+def encode(weight):
+    code = jnp.minimum((weight * 65536.0 + 0.5).astype(jnp.int32), 32767)
+    value = (128 + ((code >> 1) & 127)).astype(f32) * 2.0**-70
+    for bit in range(7):
+        value = jnp.where((code >> (8 + bit)) & 1 == 1, value * 2.0 ** (1 << bit), value)
+    return jnp.where(code & 1 == 1, -value, value)
+
+
+def decode(value):
+    size = jnp.abs(value)
+    code = jnp.zeros_like(size)
+    for bit in range(6, -1, -1):
+        above = size >= 2.0 ** ((1 << bit) - 63)
+        size = jnp.where(above, size * 2.0 ** -(1 << bit), size)
+        code = jnp.where(above, code + (256 << bit), code)
+    code = code + (size * 2.0**71 - 256.0)
+    return jnp.where(value < 0.0, code + 1.0, code) * 2.0**-16
 
 
 def prepare(sz, n_epoch, tiles, count, nsel):
@@ -68,8 +86,8 @@
 
     def body(*refs):
         sources, refs = refs[:9], refs[9:]
-        r_out, sw_out, own_out, sci_out = refs[:4]
-        var, mask, inter, offs, index, coef, basis, table, place, sems = refs[4:]
+        r_out, sw_out, own_out, sci_out, weight_out = refs[:5]
+        var, mask, inter, offs, index, coef, basis, table, place, sems = refs[5:]
         targets = [own_out, sci_out, var, mask, inter, offs, index, coef, basis]
         copies = [
             pltpu.make_async_copy(source, target, sems.at[i])
@@ -80,8 +98,7 @@
         me, _ = here("epoch")
         table[...] = jnp.zeros(table.shape, f32)
         col = iota((FINE, width), 0)
-        whole = sz.per * sz.phases
-        base = iota((FINE, width), 1) - (col // whole) * CHUNK - (col % whole) * FINE
+        base = iota((FINE, width), 1) - sz.place(col)
         base = jnp.where(col < KS, base, -1)
         for a in range(0, KS + 1, 2):
             pair = jnp.concatenate([(base == a).astype(f32), (base == a + 1).astype(f32)], axis=0)
@@ -122,9 +139,9 @@
         for copy in reversed(copies[:4]):
             copy.wait()
         for e in range(count):
-            s_high, s_low = split(sci_out[e])
-            w_high, w_low = split(mask[e].astype(f32) / var[e])
-            sw_out[e] = jnp.concatenate([s_high, s_low, w_high, w_low], axis=0).astype(bf16)
+            weight_out[e] = mask[e].astype(f32) / var[e]
+            parts = [*split(sci_out[e]), encode(weight_out[e])]
+            sw_out[e] = jnp.concatenate(parts, axis=0).astype(bf16)
 
     hbm, vmem = pl.BlockSpec(memory_space=pltpu.HBM), pl.BlockSpec(memory_space=pltpu.VMEM)
     shape = (count, sz.height, sz.width)
@@ -134,11 +151,12 @@
         return pl.pallas_call(
             body,
             in_specs=[hbm] * 9,
-            out_specs=(vmem,) * 4,
+            out_specs=(vmem,) * 5,
             out_shape=(
                 jax.ShapeDtypeStruct((count, sz.r_rows, CHUNK), bf16),
                 jax.ShapeDtypeStruct((count, sz.sw_rows, sz.width), bf16),
                 jax.ShapeDtypeStruct(template.shape, bf16),
+                jax.ShapeDtypeStruct(shape, f32),
                 jax.ShapeDtypeStruct(shape, f32),
             ),
             scratch_shapes=[
@@ -233,9 +251,8 @@
                     jnp.concatenate(bits[i * wide : (i + 1) * wide], axis=1)
                     for i in range(sz.halo_rows // 8)
                 ]
-                parts = [lines, slab[:, :w]] + bits
-                out[c, : sz.sw_rows] = sw[mine]
-                out[c, sz.sw_rows :] = jnp.concatenate(parts, axis=0).astype(bf16)
+                parts = [sw[mine].astype(f32), lines, slab[:, :w]] + bits
+                out[c] = jnp.concatenate(parts, axis=0).astype(bf16)
 
     vmem = pl.BlockSpec(memory_space=pltpu.VMEM)
     return pl.pallas_call(
@@ -254,7 +271,7 @@
     h, w = sz.height, sz.width
     total_models = (2 * len(ks) + first) * per_owner
 
-    def body(sci, sw, r, slabs, *refs):
+    def body(sci, weight, r, slabs, *refs):
         refs = list(refs)
         pays = [refs.pop(0) for _ in ks]
         before = [] if first else [refs.pop(0) for _ in range(2)]
@@ -264,130 +281,129 @@
         else:
             numer_out, denom_out = refs.pop(0), refs.pop(0)
             resid_outs = [refs.pop(0) for _ in range(len(ks) + first)]
-        rhs, lhs, numer, denom = refs
+        rhs, lhs = refs
         me, _ = here("epoch")
         strip, strips = here("strip")
         band, bands = here("band")
-        row = (strip * h + iota((h, w), 0)).astype(f32)
-        col = (band * w + iota((h, w), 1)).astype(f32)
-        r_unit = (2.0 * row + 1.0) / (h * strips) - 1.0
-        c_unit = (2.0 * col + 1.0) / (w * bands) - 1.0
-        for slot in range(2):
-            for i in range(sz.chunks):
-                used = len(sz.columns(i)) * sz.span
-                if used < CHUNK:
-                    rhs[slot, i * CHUNK + used : (i + 1) * CHUNK] = jnp.zeros((CHUNK - used, w), bf16)
-        turn = [0]
-
-        def model(slab, rows_of):
-            slot = turn[0] % 2
-            turn[0] += 1
-            window, band_rows = rhs.at[slot], lhs.at[slot]
-            down = rows_of[NPOLY, 0].astype(jnp.int32)
-            across = rows_of[NPOLY, 1].astype(jnp.int32)
-            slab = pltpu.roll(slab, lax.rem(sz.rows + HALF - down, sz.rows), 0)[: sz.span]
-            slab = pltpu.roll(slab, lax.rem(sz.lanes + HALF - across, sz.lanes), 1).astype(bf16)
-            for i in range(sz.chunks):
-                for slot, b in enumerate(sz.columns(i)):
-                    at = i * CHUNK + slot * sz.span
-                    window[at : at + sz.span] = slab[:, b : b + w]
-            for i in range(sz.chunks):
-                line, phase = divmod(i, sz.phases)
-                lines = rows_of[line * SLOT : (line + 1) * SLOT]
-                if phase:
-                    lines = pltpu.roll(lines, CHUNK - phase * FINE, 1)
-                spot = iota(lines.shape, 1)
-                lines = jnp.where((spot % sz.span < FINE) & (spot < sz.per * sz.span), lines, 0.0)
-                for p in range(NPOLY):
-                    line = lines[p : p + 1]
-                    line = pltpu.roll(
-                        jnp.broadcast_to(line, (h, CHUNK)), 0, 1, stride=1, stride_axis=0
-                    )
-                    band_rows[p * h : (p + 1) * h, i * CHUNK : (i + 1) * CHUNK] = line
-            conv = jnp.dot(band_rows[...].astype(bf16), window[...], preferred_element_type=f32)
-            conv = [conv[p * h : (p + 1) * h] for p in range(NPOLY)]
-            return (
-                conv[0]
-                + r_unit * (conv[1] + r_unit * conv[3] + c_unit * conv[4])
-                + c_unit * (conv[2] + c_unit * conv[5])
-            )
-
-        def add(tile, pair, image):
-            science = pair[:h] + pair[h : 2 * h]
-            weight = pair[2 * h : 3 * h] + pair[3 * h : 4 * h]
-            numer[tile] = numer[tile] + weight * (science - image)
-            denom[tile] = denom[tile] + weight
-
-        def tile_of(lines):
-            return lines[NPOLY, 2].astype(jnp.int32)
-
-        def keep(j, c, mine, image):
-            value = sci[mine] - image
-            if last:
-                resid_out[mine] = value
-            else:
-                resid_outs[j][c] = value
-
-        if first:
-            numer[...] = jnp.zeros(numer.shape, f32)
-            denom[...] = jnp.zeros(denom.shape, f32)
-        else:
-            numer[...] = before[0][...]
-            denom[...] = before[1][...]
+
+        jobs = []
+
+        def job(kind, q, c, slab, lines):
+            mine = q * per_owner + c
+            own = lines if kind == "local" else r[mine].astype(f32)
+            scalars = [lines[NPOLY, lane].astype(jnp.int32) for lane in range(2)]
+            tile = None if kind == "sent" else own[NPOLY, 2].astype(jnp.int32)
+            jobs.append((kind, mine, slab, lines, scalars, tile, own))
+
         if first:
             for c in range(per_owner):
-                mine = me * per_owner + c
-                lines = r[mine].astype(f32)
-                tile = tile_of(lines)
-                image = model(slabs[tile].astype(f32), lines)
-                keep(len(ks), c, mine, image)
-                add(tile, sw[mine].astype(f32), image)
-        for j, (k, pay) in enumerate(zip(ks, pays)):
+                job("local", me, c, None, r[me * per_owner + c].astype(f32))
+        for k, pay in zip(ks, pays):
             q = partner(me, n_epoch, k, True)
             for c in range(per_owner):
-                mine = q * per_owner + c
-                got = pay[c, sz.sw_rows :].astype(f32)
-                lines = r[mine].astype(f32)
-                tile = tile_of(lines)
-                image = model(slabs[tile].astype(f32), got[: sz.r_rows])
-                add(tile, pay[c, : sz.sw_rows].astype(f32), image)
-                main = got[sz.r_rows : sz.r_rows + sz.sent]
-                halo = got[sz.r_rows + sz.sent :]
-                wide = w // 128
-                bits = []
-                for g in range(sz.groups):
-                    part, slot = g // 4, g % 4
-                    line, side = part // wide, part % wide
-                    piece = halo[line * 8 : line * 8 + 8, side * 128 : side * 128 + 128]
-                    piece = pltpu.roll(piece, (128 - slot * 32) % 128, 1)
-                    bits.append(piece)
-                halo = jnp.concatenate(bits, axis=0)
-                lane = iota(halo.shape, 1)
-                halo = pltpu.roll(jnp.where(lane < 2 * REACH, halo, 0.0), 128 - REACH, 1)
-                if sz.lanes - w != 128:
-                    lane = iota(halo.shape, 1)
-                    gap = sz.lanes - w - 256
-                    pieces = [jnp.where(lane < 64, halo, 0.0)]
-                    if gap:
-                        pieces.append(jnp.zeros((sz.sent, gap), f32))
-                    halo = jnp.concatenate(pieces + [jnp.where(lane < 64, 0.0, halo)], axis=1)
-                slab = jnp.concatenate([main, halo], axis=1)
-                if sz.one_side:
-                    side, none = slab[h:], jnp.zeros((sz.rows - h - 32, sz.lanes), f32)
-                    below, above = jnp.where(strip == 0, side, 0.0), jnp.where(strip == 0, 0.0, side)
-                    slab = [slab[:h], below, none, above] if none.size else [slab[:h], below, above]
-                    slab = jnp.concatenate(slab, axis=0)
-                image = model(slab, lines)
-                keep(j, c, mine, image)
+                got = pay[c].astype(f32)
+                job("owned", q, c, got, got[sz.sw_rows : sz.main_at])
+                job("sent", q, c, got, r[q * per_owner + c].astype(f32))
+
+        row = (strip * h + iota((h, sz.lanes), 0)).astype(f32)
+        r_unit = (2.0 * row + 1.0) / (h * strips) - 1.0
+        for slot in range(2):
+            used = sz.per * sz.span
+            if used < CHUNK:
+                rhs[slot, used:] = jnp.zeros((CHUNK - used, sz.lanes), bf16)
+
+        def model(turn, slab, lines, scalars):
+            window, band_rows = rhs.at[turn % 2], lhs.at[turn % 2]
+            down, across = scalars
+            slab = pltpu.roll(slab, lax.rem(sz.rows + HALF - down, sz.rows), 0)[: sz.span]
+            slab = pltpu.roll(slab.astype(bf16), lax.rem(sz.lanes + HALF - across, sz.lanes), 1)
+            for slot in range(sz.per):
+                moved = pltpu.roll(slab, sz.lanes - slot * sz.chunks, 1) if slot else slab
+                window[slot * sz.span : (slot + 1) * sz.span] = moved
+            image = None
+            for i in reversed(range(sz.chunks)):
+                line, phase = divmod(i, sz.phases)
+                part = lines[line * SLOT : (line + 1) * SLOT]
+                if phase:
+                    part = pltpu.roll(part, CHUNK - phase * FINE, 1)
+                spot = iota(part.shape, 1)
+                part = jnp.where((spot % sz.span < FINE) & (spot < sz.per * sz.span), part, 0.0)
+                at = i * NPOLY * h
+                for p in range(NPOLY):
+                    band_rows[at + p * h : at + (p + 1) * h] = pltpu.roll(
+                        jnp.broadcast_to(part[p : p + 1], (h, CHUNK)), 0, 1, stride=1, stride_axis=0
+                    )
+                conv = jnp.dot(
+                    band_rows[at : at + NPOLY * h].astype(bf16), window[...], preferred_element_type=f32
+                )
+                conv = [conv[p * h : (p + 1) * h] for p in range(NPOLY)]
+                col = (band * w + iota((h, sz.lanes), 1) - i).astype(f32)
+                c_unit = (2.0 * col + 1.0) / (w * bands) - 1.0
+                value = (
+                    conv[0]
+                    + r_unit * (conv[1] + r_unit * conv[3] + c_unit * conv[4])
+                    + c_unit * (conv[2] + c_unit * conv[5])
+                )
+                image = value if image is None else pltpu.roll(image, sz.lanes - 1, 1) + value
+            return image[:, :w]
+
+        def sent_slab(got):
+            main, halo = got[sz.main_at : sz.halo_at], got[sz.halo_at :]
+            wide = w // 128
+            bits = []
+            for g in range(sz.groups):
+                part, slot = g // 4, g % 4
+                line, side = part // wide, part % wide
+                piece = halo[line * 8 : line * 8 + 8, side * 128 : side * 128 + 128]
+                bits.append(pltpu.roll(piece, (128 - slot * 32) % 128, 1))
+            halo = jnp.concatenate(bits, axis=0)
+            lane = iota(halo.shape, 1)
+            halo = pltpu.roll(jnp.where(lane < 2 * REACH, halo, 0.0), 128 - REACH, 1)
+            if sz.lanes - w != 128:
+                gap = sz.lanes - w - 256
+                pieces = [jnp.where(lane < 64, halo, 0.0)]
+                if gap:
+                    pieces.append(jnp.zeros((sz.sent, gap), f32))
+                halo = jnp.concatenate(pieces + [jnp.where(lane < 64, 0.0, halo)], axis=1)
+            slab = jnp.concatenate([main, halo], axis=1)
+            if sz.one_side:
+                side, none = slab[h:], jnp.zeros((sz.rows - h - 32, sz.lanes), f32)
+                below, above = jnp.where(strip == 0, side, 0.0), jnp.where(strip == 0, 0.0, side)
+                slab = [slab[:h], below, none, above] if none.size else [slab[:h], below, above]
+                slab = jnp.concatenate(slab, axis=0)
+            return slab
+
+        numer = [before[0][t] if before else jnp.zeros((h, w), f32) for t in range(tiles)]
+        denom = [before[1][t] if before else jnp.zeros((h, w), f32) for t in range(tiles)]
+        kept = 0
+        for turn, (kind, mine, got, lines, scalars, tile, own) in enumerate(jobs):
+            slab = sent_slab(got) if kind == "sent" else slabs[tile].astype(f32)
+            image = model(turn, slab, lines, scalars)
+            if kind == "owned":
+                science, seen = got[:h] + got[h : 2 * h], decode(got[2 * h : 3 * h])
+            else:
+                science, seen = sci[mine], weight[mine]
+                if last:
+                    resid_out[mine] = science - image
+                else:
+                    resid_outs[kept // per_owner][kept % per_owner] = science - image
+                kept += 1
+            if kind != "sent":
+                change = seen * (science - image)
+                covered = jnp.broadcast_to(own[NPOLY : NPOLY + 1, 2:3], (h, w))
+                for t in range(tiles):
+                    numer[t] = numer[t] + jnp.where(covered == t, change, 0.0)
+                    denom[t] = denom[t] + jnp.where(covered == t, seen, 0.0)
+        for t in range(tiles):
+            if last:
+                coadd_out[t] = numer[t] / (denom[t] + 1.0)
+            else:
+                numer_out[t], denom_out[t] = numer[t], denom[t]
         if last:
-            for (k, where), value in zip(carried, done):
+            for k, value in zip(carried, done):
                 q = me if k == 0 else partner(me, n_epoch, k, True)
                 for c in range(per_owner):
                     resid_out[q * per_owner + c] = value[c]
-            coadd_out[...] = numer[...] / (denom[...] + 1.0)
-        else:
-            numer_out[...] = numer[...]
-            denom_out[...] = denom[...]
 
     image = jax.ShapeDtypeStruct((per_owner, h, w), f32)
     sums = jax.ShapeDtypeStruct((tiles, h, w), f32)
@@ -401,10 +417,8 @@
         in_specs=[vmem] * (4 + len(ks) + (0 if first else 2) + len(carried)),
         out_shape=out_shape,
         scratch_shapes=[
-            pltpu.VMEM((2, sz.depth, w), bf16),
-            pltpu.VMEM((2, NPOLY * h, sz.depth), f32),
-            pltpu.VMEM((tiles, h, w), f32),
-            pltpu.VMEM((tiles, h, w), f32),
+            pltpu.VMEM((2, CHUNK, sz.lanes), bf16),
+            pltpu.VMEM((2, sz.chunks * NPOLY * h, CHUNK), f32),
         ],
         compiler_params=pltpu.CompilerParams(vmem_limit_bytes=VMEM_LIMIT),
         cost_estimate=pl.CostEstimate(
@@ -435,7 +449,7 @@
     sz = Sizes(height, width, lax.axis_size("strip"))
     low, high = neighbours(template, "strip")
     left, right = neighbours(template, "band")
-    r, sw, own, sci = prepare(sz, n_epoch, tiles, count, basis_index.shape[1])(
+    r, sw, own, sci, weight = prepare(sz, n_epoch, tiles, count, basis_index.shape[1])(
         template,
         science,
         variance,
@@ -467,10 +481,10 @@
     sums, carried = [], []
     for i, ks in enumerate(stages):
         first, last = i == 0, i == len(stages) - 1
-        kept = [(k, j) for j, (k, _) in enumerate(carried)] if last else []
+        kept = [k for k, _ in carried] if last else []
         out = models(sz, n_epoch, tiles, count, ks, first, last, kept)(
             sci,
-            sw,
+            weight,
             r,
             slabs,
             *[pays[k] for k in ks],

time: 20.8 us -> 19.4 us (0.933)
  Pallas kernels: 7.93 us -> 6.84 us
    pallas_call x4, Pallas kernels: 5.66 us -> 4.43 us  [local(): models(sz, n_epoch, tiles, count, ks, first, last, kept)]
  transfers between devices with their start and end apart: 6 -> 6, of which waited for: 4 -> 4; matrix products, arithmetic and copies ran while one was open for 0% -> 0% of each run, Pallas kernels for 27% -> 25%
where the time goes in v4:
time: 19.4 us; the launch traced here: 19.3 us
  starting transfers between devices  7.94 us (41%)
  Pallas kernels  6.84 us (35%)
  waiting for transfers between devices  3.82 us (20%)
  between operations  0.66 us (3%)
    ppermute x3, starting transfers between devices, local(): pays[k] = lax.ppermute(send, 'epoch', pairs)  4.63 us
    pallas_call x4, Pallas kernels, local(): models(sz, n_epoch, tiles, count, ks, first, last, kept)  4.43 us
    ppermute x3, starting transfers between devices, neighbours(): other = lax.ppermute(block, axis, [(0, 1), (1, 0)])  3.31 us
    ppermute x3, waiting for transfers between devices, local(): pays[k] = lax.ppermute(send, 'epoch', pairs)  2.79 us
    pallas_call x1, Pallas kernels, call(): pl.pallas_call(body, in_specs=[hbm] * 9, out_specs=(vmem,) * 5, out_shape...  2.14 us
    ppermute x3, waiting for transfers between devices, neighbours(): other = lax.ppermute(block, axis, [(0, 1), (1, 0)])  1.03 us
  transfers between devices with their start and end apart: 6, of which 4 were waited for; matrix products, arithmetic and copies ran while one was open for 0% of the time, Pallas kernels for 25%

profile of v4, /device:TPU:0, one launch (start us, length us, event | category | flops | bytes accessed | tf_op | source)
XLA Modules:
  0.0 19.3 jit_solution(13075138807940080183)
XLA Ops:
  0.6 0.5 %collective-permute-start.1 = (bf16[2,24,256]{2,1,0:T(8,128)(2,1)}, bf16[2,24,256]{2,1,0:T(8,128)(2,1)S(1)}, u32[]{:S(2)}, u32[]{:S(2)}) collective-permute-start(bf16[2,24,256]{2,1,0:T(8,128)(2,1)} %refs_0_.1), channel_id=1, source_target_pairs={{0,1},{1,0},{2,3},{3,2},{4,5},{5,4},{6,7},{7,6},{8,9},{9,8},{10,11... | collective-permute-start | bytes 73736 | tf_op jit(solution)/shard_map/ppermute | solution.py:436
  1.2 2.6 %collective-permute-start = (bf16[2,24,256]{2,1,0:T(8,128)(2,1)}, bf16[2,24,256]{2,1,0:T(8,128)(2,1)S(1)}, u32[]{:S(2)}, u32[]{:S(2)}) collective-permute-start(bf16[2,24,256]{2,1,0:T(8,128)(2,1)} %refs_0_.1), channel_id=1, source_target_pairs={{0,2},{2,0},{1,3},{3,1},{4,6},{6,4},{5,7},{7,5},{8,10},{10,8},{9,1... | collective-permute-start | bytes 73736 | tf_op jit(solution)/shard_map/ppermute | solution.py:436
  3.7 2.1 %prepare.1 = (bf16[4,16,256]{2,1,0:T(8,128)(2,1)S(1)}, bf16[4,72,256]{2,1,0:T(8,128)(2,1)S(1)}, bf16[2,24,256]{2,1,0:T(8,128)(2,1)S(1)}, f32[4,24,256]{2,1,0:T(8,128)S(1)}, f32[4,24,256]{2,1,0:T(8,128)S(1)}) custom-call(bf16[2,24,256]{2,1,0:T(8,128)(2,1)} %refs_0_.1, f32[4,24,256]{2,1,0:T(8,128)} %refs_1_.1, f32[4,24,256]{2,1,0:T(8,128)} %refs_2_.1, ...), custom_call_target="tpu_custom_call" | custom-call | flops 1000000000 | bytes 6000000 | tf_op jit(solution)/shard_map/prepare/pallas_call | solution.py:151
  5.9 0.0 collective-permute-done.low.high
  5.9 0.2 %collective-permute-start.2 = (bf16[2,24,256]{2,1,0:T(8,128)(2,1)S(1)}, bf16[2,24,256]{2,1,0:T(8,128)(2,1)S(1)}, u32[]{:S(2)}, u32[]{:S(2)}) collective-permute-start(bf16[2,24,256]{2,1,0:T(8,128)(2,1)S(1)} %collective-permute-done.low.high), channel_id=1, source_target_pairs={{0,1},{1,0},{2,3},{3,2},{4,5},{5,4},{6,7},{7,6},{8,9},{9,8},{10,11... | collective-permute-start | bytes 73736 | tf_op jit(solution)/shard_map/ppermute | solution.py:436
  6.1 0.0 collective-permute-done.1.left.right
  6.1 1.0 %collective-permute-done.2.low_left.high_left.low_right.high_right = bf16[2,24,256]{2,1,0:T(8,128)(2,1)S(1)} collective-permute-done((bf16[2,24,256]{2,1,0:T(8,128)(2,1)S(1)}, bf16[2,24,256]{2,1,0:T(8,128)(2,1)S(1)}, u32[]{:S(2)}, u32[]{:S(2)}) %collective-permute-start.2) | collective-permute-done | bytes 24608 | tf_op jit(solution)/shard_map/ppermute | solution.py:436
  7.1 0.3 %pack.1 = (bf16[2,56,384]{2,1,0:T(8,128)(2,1)S(1)}, bf16[1,136,256]{2,1,0:T(8,128)(2,1)S(1)}, bf16[1,136,256]{2,1,0:T(8,128)(2,1)S(1)}, bf16[1,136,256]{2,1,0:T(8,128)(2,1)S(1)}) custom-call(bf16[2,24,256]{2,1,0:T(8,128)(2,1)S(1)} %get-tuple-element.26.own, bf16[2,24,256]{2,1,0:T(8,128)(2,1)S(1)} %collective-permute-done.low.high, ...), custom_call_target="tpu_custom_call" | custom-call | flops 1000000 | bytes 1000000 | tf_op jit(solution)/shard_map/pack/pallas_call | solution.py:473
  7.4 4.0 %collective-permute-start.5 = (bf16[1,136,256]{2,1,0:T(8,128)(2,1)S(1)}, bf16[1,136,256]{2,1,0:T(8,128)(2,1)S(1)}, u32[]{:S(2)}, u32[]{:S(2)}) collective-permute-start(bf16[1,136,256]{2,1,0:T(8,128)(2,1)S(1)} %get-tuple-element.32), channel_id=1, source_target_pairs={{0,12},{4,8},{8,4},{12,0},{1,13},{5,9},{9,5},{13,1},{2,14},{6,10},... | collective-permute-start | bytes 208904 | tf_op jit(solution)/shard_map/ppermute | solution.py:479
  11.4 0.0 collective-permute-start.3
  11.4 0.6 %collective-permute-start.4 = (bf16[1,136,256]{2,1,0:T(8,128)(2,1)S(1)}, bf16[1,136,256]{2,1,0:T(8,128)(2,1)S(1)}, u32[]{:S(2)}, u32[]{:S(2)}) collective-permute-start(bf16[1,136,256]{2,1,0:T(8,128)(2,1)S(1)} %get-tuple-element.31), channel_id=1, source_target_pairs={{0,4},{4,0},{8,12},{12,8},{1,5},{5,1},{9,13},{13,9},{2,6},{6,2},{1... | collective-permute-start | bytes 208904 | tf_op jit(solution)/shard_map/ppermute | solution.py:479
  12.0 0.7 %models.4 = (f32[2,24,256]{2,1,0:T(8,128)S(1)}, f32[2,24,256]{2,1,0:T(8,128)S(1)}, f32[1,24,256]{2,1,0:T(8,128)S(1)}) custom-call(f32[4,24,256]{2,1,0:T(8,128)S(1)} %get-tuple-element.22.sci, f32[4,24,256]{2,1,0:T(8,128)S(1)} %get-tuple-element.23.weight, bf16[4,16,256]{2,1,0:T(8,128)(2,1)S(1)} %get-tuple-element.25.r, ...), custom_call_target="tpu_custom_call" | custom-call | flops 400000000 | bytes 1000000 | tf_op jit(solution)/shard_map/models/pallas_call | solution.py:485
  12.8 1.5 %collective-permute-done.5.refs_0_ = bf16[1,136,256]{2,1,0:T(8,128)(2,1)S(1)} collective-permute-done((bf16[1,136,256]{2,1,0:T(8,128)(2,1)S(1)}, bf16[1,136,256]{2,1,0:T(8,128)(2,1)S(1)}, u32[]{:S(2)}, u32[]{:S(2)}) %collective-permute-start.5) | collective-permute-done | bytes 69664 | tf_op jit(solution)/shard_map/ppermute | solution.py:479
  14.2 1.0 %models.5 = (f32[2,24,256]{2,1,0:T(8,128)S(1)}, f32[2,24,256]{2,1,0:T(8,128)S(1)}, f32[1,24,256]{2,1,0:T(8,128)S(1)}) custom-call(f32[4,24,256]{2,1,0:T(8,128)S(1)} %get-tuple-element.22.sci, f32[4,24,256]{2,1,0:T(8,128)S(1)} %get-tuple-element.23.weight, bf16[4,16,256]{2,1,0:T(8,128)(2,1)S(1)} %get-tuple-element.25.r, ...), custom_call_target="tpu_custom_call" | custom-call | flops 800000000 | bytes 1000000 | tf_op jit(solution)/shard_map/models/pallas_call | solution.py:485
  15.2 1.0 %collective-permute-done.4.refs_0_ = bf16[1,136,256]{2,1,0:T(8,128)(2,1)S(1)} collective-permute-done((bf16[1,136,256]{2,1,0:T(8,128)(2,1)S(1)}, bf16[1,136,256]{2,1,0:T(8,128)(2,1)S(1)}, u32[]{:S(2)}, u32[]{:S(2)}) %collective-permute-start.4) | collective-permute-done | bytes 69664 | tf_op jit(solution)/shard_map/ppermute | solution.py:479
  16.2 1.0 %models.6 = (f32[2,24,256]{2,1,0:T(8,128)S(1)}, f32[2,24,256]{2,1,0:T(8,128)S(1)}, f32[1,24,256]{2,1,0:T(8,128)S(1)}) custom-call(f32[4,24,256]{2,1,0:T(8,128)S(1)} %get-tuple-element.22.sci, f32[4,24,256]{2,1,0:T(8,128)S(1)} %get-tuple-element.23.weight, bf16[4,16,256]{2,1,0:T(8,128)(2,1)S(1)} %get-tuple-element.25.r, ...), custom_call_target="tpu_custom_call" | custom-call | flops 800000000 | bytes 1000000 | tf_op jit(solution)/shard_map/models/pallas_call | solution.py:485
  17.2 0.4 %collective-permute-done.3.refs_0_ = bf16[1,136,256]{2,1,0:T(8,128)(2,1)S(1)} collective-permute-done((bf16[1,136,256]{2,1,0:T(8,128)(2,1)S(1)}, bf16[1,136,256]{2,1,0:T(8,128)(2,1)S(1)}, u32[]{:S(2)}, u32[]{:S(2)}) %collective-permute-start.3) | collective-permute-done | bytes 69664 | tf_op jit(solution)/shard_map/ppermute | solution.py:479
  17.6 1.7 %models.7 = (f32[4,24,256]{2,1,0:T(8,128)}, f32[2,24,256]{2,1,0:T(8,128)}) custom-call(f32[4,24,256]{2,1,0:T(8,128)S(1)} %get-tuple-element.22.sci, f32[4,24,256]{2,1,0:T(8,128)S(1)} %get-tuple-element.23.weight, bf16[4,16,256]{2,1,0:T(8,128)(2,1)S(1)} %get-tuple-element.25.r, bf16[2,56,384]{2,1,0:T(8,128)(2,1)S(1)} %get-tuple-element.29.slabs, ...), custom_call_target="tpu_custom_call" | custom-call | flops 800000000 | bytes 1000000 | tf_op jit(solution)/shard_map/models/pallas_call | solution.py:485
Async XLA Ops:
  0.6 5.5 %collective-permute-start.1 = (bf16[2,24,256]{2,1,0:T(8,128)(2,1)}, bf16[2,24,256]{2,1,0:T(8,128)(2,1)S(1)}, u32[]{:S(2)}, u32[]{:S(2)}) collective-permute-start(bf16[2,24,256]{2,1,0:T(8,128)(2,1)} %refs_0_.1), channel_id=1, source_target_pairs={{0,1},{1,0},{2,3},{3,2},{4,5},{5,4},{6,7},{7,6},{8,9},{9,8},{10,11... | collective-permute-start | bytes 73736 | tf_op jit(solution)/shard_map/ppermute | solution.py:436
  1.2 4.7 %collective-permute-start = (bf16[2,24,256]{2,1,0:T(8,128)(2,1)}, bf16[2,24,256]{2,1,0:T(8,128)(2,1)S(1)}, u32[]{:S(2)}, u32[]{:S(2)}) collective-permute-start(bf16[2,24,256]{2,1,0:T(8,128)(2,1)} %refs_0_.1), channel_id=1, source_target_pairs={{0,2},{2,0},{1,3},{3,1},{4,6},{6,4},{5,7},{7,5},{8,10},{10,8},{9,1... | collective-permute-start | bytes 73736 | tf_op jit(solution)/shard_map/ppermute | solution.py:436
  5.9 1.3 %collective-permute-start.2 = (bf16[2,24,256]{2,1,0:T(8,128)(2,1)S(1)}, bf16[2,24,256]{2,1,0:T(8,128)(2,1)S(1)}, u32[]{:S(2)}, u32[]{:S(2)}) collective-permute-start(bf16[2,24,256]{2,1,0:T(8,128)(2,1)S(1)} %collective-permute-done.low.high), channel_id=1, source_target_pairs={{0,1},{1,0},{2,3},{3,2},{4,5},{5,4},{6,7},{7,6},{8,9},{9,8},{10,11... | collective-permute-start | bytes 73736 | tf_op jit(solution)/shard_map/ppermute | solution.py:436
  7.4 6.8 %collective-permute-start.5 = (bf16[1,136,256]{2,1,0:T(8,128)(2,1)S(1)}, bf16[1,136,256]{2,1,0:T(8,128)(2,1)S(1)}, u32[]{:S(2)}, u32[]{:S(2)}) collective-permute-start(bf16[1,136,256]{2,1,0:T(8,128)(2,1)S(1)} %get-tuple-element.32), channel_id=1, source_target_pairs={{0,12},{4,8},{8,4},{12,0},{1,13},{5,9},{9,5},{13,1},{2,14},{6,10},... | collective-permute-start | bytes 208904 | tf_op jit(solution)/shard_map/ppermute | solution.py:479
  11.4 6.2 %collective-permute-start.3 = (bf16[1,136,256]{2,1,0:T(8,128)(2,1)S(1)}, bf16[1,136,256]{2,1,0:T(8,128)(2,1)S(1)}, u32[]{:S(2)}, u32[]{:S(2)}) collective-permute-start(bf16[1,136,256]{2,1,0:T(8,128)(2,1)S(1)} %get-tuple-element.30), channel_id=1, source_target_pairs={{0,8},{4,12},{8,0},{12,4},{1,9},{5,13},{9,1},{13,5},{2,10},{6,14},... | collective-permute-start | bytes 208904 | tf_op jit(solution)/shard_map/ppermute | solution.py:479
  11.4 4.8 %collective-permute-start.4 = (bf16[1,136,256]{2,1,0:T(8,128)(2,1)S(1)}, bf16[1,136,256]{2,1,0:T(8,128)(2,1)S(1)}, u32[]{:S(2)}, u32[]{:S(2)}) collective-permute-start(bf16[1,136,256]{2,1,0:T(8,128)(2,1)S(1)} %get-tuple-element.31), channel_id=1, source_target_pairs={{0,4},{4,0},{8,12},{12,8},{1,5},{5,1},{9,13},{13,9},{2,6},{6,2},{1... | collective-permute-start | bytes 208904 | tf_op jit(solution)/shard_map/ppermute | solution.py:479

commit v5 on v4

--- a/solution.py
+++ b/solution.py
@@ -281,10 +281,22 @@
         else:
             numer_out, denom_out = refs.pop(0), refs.pop(0)
             resid_outs = [refs.pop(0) for _ in range(len(ks) + first)]
-        rhs, lhs = refs
+        rhs, lhs, *refs = refs
         me, _ = here("epoch")
         strip, strips = here("strip")
         band, bands = here("band")
+
+        copies = []
+
+        def send(source, target):
+            copies.append(pltpu.make_async_copy(source, target, out_sems.at[len(copies)]))
+            copies[-1].start()
+
+        if last:
+            fresh, sums, out_sems = refs
+            for k, value in zip(carried, done):
+                q = me if k == 0 else partner(me, n_epoch, k, True)
+                send(value, resid_out.at[pl.ds(q * per_owner, per_owner)])
 
         jobs = []
 
@@ -303,7 +315,8 @@
             for c in range(per_owner):
                 got = pay[c].astype(f32)
                 job("owned", q, c, got, got[sz.sw_rows : sz.main_at])
-                job("sent", q, c, got, r[q * per_owner + c].astype(f32))
+            for c in range(per_owner):
+                job("sent", q, c, pay[c].astype(f32), r[q * per_owner + c].astype(f32))
 
         row = (strip * h + iota((h, sz.lanes), 0)).astype(f32)
         r_unit = (2.0 * row + 1.0) / (h * strips) - 1.0
@@ -376,6 +389,7 @@
         numer = [before[0][t] if before else jnp.zeros((h, w), f32) for t in range(tiles)]
         denom = [before[1][t] if before else jnp.zeros((h, w), f32) for t in range(tiles)]
         kept = 0
+        settled = max(turn for turn, job in enumerate(jobs) if job[0] != "sent")
         for turn, (kind, mine, got, lines, scalars, tile, own) in enumerate(jobs):
             slab = sent_slab(got) if kind == "sent" else slabs[tile].astype(f32)
             image = model(turn, slab, lines, scalars)
@@ -384,7 +398,8 @@
             else:
                 science, seen = sci[mine], weight[mine]
                 if last:
-                    resid_out[mine] = science - image
+                    fresh[kept] = science - image
+                    send(fresh.at[kept], resid_out.at[mine])
                 else:
                     resid_outs[kept // per_owner][kept % per_owner] = science - image
                 kept += 1
@@ -394,16 +409,16 @@
                 for t in range(tiles):
                     numer[t] = numer[t] + jnp.where(covered == t, change, 0.0)
                     denom[t] = denom[t] + jnp.where(covered == t, seen, 0.0)
-        for t in range(tiles):
-            if last:
-                coadd_out[t] = numer[t] / (denom[t] + 1.0)
-            else:
-                numer_out[t], denom_out[t] = numer[t], denom[t]
-        if last:
-            for k, value in zip(carried, done):
-                q = me if k == 0 else partner(me, n_epoch, k, True)
-                for c in range(per_owner):
-                    resid_out[q * per_owner + c] = value[c]
+            if turn == settled:
+                for t in range(tiles):
+                    if last:
+                        sums[t] = numer[t] / (denom[t] + 1.0)
+                    else:
+                        numer_out[t], denom_out[t] = numer[t], denom[t]
+                if last:
+                    send(sums, coadd_out)
+        for copy in copies:
+            copy.wait()
 
     image = jax.ShapeDtypeStruct((per_owner, h, w), f32)
     sums = jax.ShapeDtypeStruct((tiles, h, w), f32)
@@ -411,15 +426,24 @@
         out_shape = (jax.ShapeDtypeStruct((count, h, w), f32), sums)
     else:
         out_shape = (sums, sums) + (image,) * (len(ks) + first)
-    vmem = pl.BlockSpec(memory_space=pltpu.VMEM)
+    vmem, hbm = pl.BlockSpec(memory_space=pltpu.VMEM), pl.BlockSpec(memory_space=pltpu.HBM)
+    scratch = [
+        pltpu.VMEM((2, CHUNK, sz.lanes), bf16),
+        pltpu.VMEM((2, sz.chunks * NPOLY * h, CHUNK), f32),
+    ]
+    if last:
+        new = len(ks) * per_owner
+        scratch += [
+            pltpu.VMEM((new, h, w), f32),
+            pltpu.VMEM((tiles, h, w), f32),
+            pltpu.SemaphoreType.DMA((len(carried) + new + 1,)),
+        ]
     return pl.pallas_call(
         body,
         in_specs=[vmem] * (4 + len(ks) + (0 if first else 2) + len(carried)),
+        out_specs=(hbm if last else vmem,) * len(out_shape),
         out_shape=out_shape,
-        scratch_shapes=[
-            pltpu.VMEM((2, CHUNK, sz.lanes), bf16),
-            pltpu.VMEM((2, sz.chunks * NPOLY * h, CHUNK), f32),
-        ],
+        scratch_shapes=scratch,
         compiler_params=pltpu.CompilerParams(vmem_limit_bytes=VMEM_LIMIT),
         cost_estimate=pl.CostEstimate(
             flops=total_models * 400_000_000, bytes_accessed=1_000_000, transcendentals=0
@@ -428,16 +452,25 @@
     )
 
 
-def neighbours(block, axis):
-    count = lax.axis_size(axis)
-    if count == 1:
-        return block, block
-    if count == 2:
-        other = lax.ppermute(block, axis, [(0, 1), (1, 0)])
-        return other, other
-    forward = [(i, i + 1) for i in range(count - 1)]
-    backward = [(i + 1, i) for i in range(count - 1)]
-    return lax.ppermute(block, axis, forward), lax.ppermute(block, axis, backward)
+def surroundings(block):
+    strips, bands = lax.axis_size("strip"), lax.axis_size("band")
+    sent, found = {}, {}
+    for down in (-1, 0, 1):
+        for across in (-1, 0, 1):
+            if down == 0 and across == 0:
+                continue
+            pairs = []
+            for s in range(strips):
+                for b in range(bands):
+                    to_s = s ^ 1 if strips == 2 and down else s - down
+                    to_b = b ^ 1 if bands == 2 and across else b - across
+                    if 0 <= to_s < strips and 0 <= to_b < bands:
+                        pairs.append((s * bands + b, to_s * bands + to_b))
+            key = tuple(pairs)
+            if key and key not in sent:
+                sent[key] = lax.ppermute(block, ("strip", "band"), pairs)
+            found[down, across] = key
+    return {step: sent.get(key, block) for step, key in found.items()}
 
 
 def local(
@@ -447,8 +480,7 @@
     tiles = template.shape[0]
     count, height, width = science.shape
     sz = Sizes(height, width, lax.axis_size("strip"))
-    low, high = neighbours(template, "strip")
-    left, right = neighbours(template, "band")
+    around = surroundings(template)
     r, sw, own, sci, weight = prepare(sz, n_epoch, tiles, count, basis_index.shape[1])(
         template,
         science,
@@ -460,18 +492,11 @@
         coefficients.transpose(2, 0, 1),
         basis.transpose(1, 2, 0),
     )
-    if high is low:
-        low, r = lax.optimization_barrier((low, r))
-        high = low
-        high_left, high_right = low_left, low_right = neighbours(low, "band")
-    else:
-        low, high, r = lax.optimization_barrier((low, high, r))
-        low_left, low_right = neighbours(low, "band")
-        high_left, high_right = neighbours(high, "band")
+    around[0, 0] = own
     peers = list(range(1, n_epoch))
     order = peers[-1:] + peers[:-1]
     slabs, *sends = pack(sz, n_epoch, tiles, count, peers)(
-        own, low, high, left, low_left, high_left, right, low_right, high_right, sw, r
+        *[around[down, across] for across in (0, -1, 1) for down in (0, -1, 1)], sw, r
     )
     pays = {}
     for k, send in zip(order, [sends[peers.index(k)] for k in order]):

time: 19.4 us -> 19.6 us (1.010)
  waiting for transfers between devices: 3.82 us -> 4.33 us
  starting transfers between devices: 7.94 us -> 7.65 us
    ppermute x3, waiting for transfers between devices: 2.79 us -> 3.22 us  [local(): pays[k] = lax.ppermute(send, 'epoch', pairs)]
  transfers between devices with their start and end apart: 6 -> 6, of which waited for: 4 -> 3; matrix products, arithmetic and copies ran while one was open for 0% -> 0% of each run, Pallas kernels for 25% -> 25%
where the time goes in v5:
time: 19.6 us; the launch traced here: 19.5 us
  starting transfers between devices  7.65 us (39%)
  Pallas kernels  6.85 us (35%)
  waiting for transfers between devices  4.33 us (22%)
  between operations  0.66 us (3%)
    ppermute x3, starting transfers between devices, local(): pays[k] = lax.ppermute(send, 'epoch', pairs)  4.45 us
    pallas_call x4, Pallas kernels, local(): models(sz, n_epoch, tiles, count, ks, first, last, kept)  4.44 us
    ppermute x3, waiting for transfers between devices, local(): pays[k] = lax.ppermute(send, 'epoch', pairs)  3.22 us
    ppermute x3, starting transfers between devices, surroundings(): sent[key] = lax.ppermute(block, ('strip', 'band'), pairs)  3.2 us
    pallas_call x1, Pallas kernels, call(): pl.pallas_call(body, in_specs=[hbm] * 9, out_specs=(vmem,) * 5, out_shape...  2.14 us
    ppermute x3, waiting for transfers between devices, surroundings(): sent[key] = lax.ppermute(block, ('strip', 'band'), pairs)  1.11 us
  transfers between devices with their start and end apart: 6, of which 3 were waited for; matrix products, arithmetic and copies ran while one was open for 0% of the time, Pallas kernels for 25%

profile of v5, /device:TPU:0, one launch (start us, length us, event | category | flops | bytes accessed | tf_op | source)
XLA Modules:
  0.0 19.5 jit_solution(11312124570531893142)
XLA Ops:
  0.6 3.0 %collective-permute-start = (bf16[2,24,256]{2,1,0:T(8,128)(2,1)}, bf16[2,24,256]{2,1,0:T(8,128)(2,1)S(1)}, u32[]{:S(2)}, u32[]{:S(2)}) collective-permute-start(bf16[2,24,256]{2,1,0:T(8,128)(2,1)} %refs_0_.1), channel_id=1, source_target_pairs={{0,2},{1,3},{2,0},{3,1},{4,6},{5,7},{6,4},{7,5},{8,10},{9,11},{10,... | collective-permute-start | bytes 73736 | tf_op jit(solution)/shard_map/ppermute | solution.py:471
  3.6 0.0 collective-permute-start.2
  3.6 0.2 collective-permute-start.1
  3.8 2.1 %prepare.1 = (bf16[4,16,256]{2,1,0:T(8,128)(2,1)S(1)}, bf16[4,72,256]{2,1,0:T(8,128)(2,1)S(1)}, bf16[2,24,256]{2,1,0:T(8,128)(2,1)S(1)}, f32[4,24,256]{2,1,0:T(8,128)S(1)}, f32[4,24,256]{2,1,0:T(8,128)S(1)}) custom-call(bf16[2,24,256]{2,1,0:T(8,128)(2,1)} %refs_0_.1, f32[4,24,256]{2,1,0:T(8,128)} %refs_1_.1, f32[4,24,256]{2,1,0:T(8,128)} %refs_2_.1, ...), custom_call_target="tpu_custom_call" | custom-call | flops 1000000000 | bytes 6000000 | tf_op jit(solution)/shard_map/prepare/pallas_call | solution.py:151
  6.0 0.0 collective-permute-done.low.high
  6.0 1.1 %collective-permute-done.2.low_left.high_left.low_right.high_right = bf16[2,24,256]{2,1,0:T(8,128)(2,1)S(1)} collective-permute-done((bf16[2,24,256]{2,1,0:T(8,128)(2,1)}, bf16[2,24,256]{2,1,0:T(8,128)(2,1)S(1)}, u32[]{:S(2)}, u32[]{:S(2)}) %collective-permute-start.2) | collective-permute-done | bytes 24608 | tf_op jit(solution)/shard_map/ppermute | solution.py:471
  7.1 0.0 collective-permute-done.1.left.right
  7.1 0.3 %pack.1 = (bf16[2,56,384]{2,1,0:T(8,128)(2,1)S(1)}, bf16[1,136,256]{2,1,0:T(8,128)(2,1)S(1)}, bf16[1,136,256]{2,1,0:T(8,128)(2,1)S(1)}, bf16[1,136,256]{2,1,0:T(8,128)(2,1)S(1)}) custom-call(bf16[2,24,256]{2,1,0:T(8,128)(2,1)S(1)} %get-tuple-element.23.own, bf16[2,24,256]{2,1,0:T(8,128)(2,1)S(1)} %collective-permute-done.low.high, ...), custom_call_target="tpu_custom_call" | custom-call | flops 1000000 | bytes 1000000 | tf_op jit(solution)/shard_map/pack/pallas_call | solution.py:498
  7.4 3.7 %collective-permute-start.5 = (bf16[1,136,256]{2,1,0:T(8,128)(2,1)S(1)}, bf16[1,136,256]{2,1,0:T(8,128)(2,1)S(1)}, u32[]{:S(2)}, u32[]{:S(2)}) collective-permute-start(bf16[1,136,256]{2,1,0:T(8,128)(2,1)S(1)} %get-tuple-element.28), channel_id=1, source_target_pairs={{0,12},{4,8},{8,4},{12,0},{1,13},{5,9},{9,5},{13,1},{2,14},{6,10},... | collective-permute-start | bytes 208904 | tf_op jit(solution)/shard_map/ppermute | solution.py:504
  11.0 0.0 collective-permute-start.3
  11.0 0.8 %collective-permute-start.4 = (bf16[1,136,256]{2,1,0:T(8,128)(2,1)S(1)}, bf16[1,136,256]{2,1,0:T(8,128)(2,1)S(1)}, u32[]{:S(2)}, u32[]{:S(2)}) collective-permute-start(bf16[1,136,256]{2,1,0:T(8,128)(2,1)S(1)} %get-tuple-element.27), channel_id=1, source_target_pairs={{0,4},{4,0},{8,12},{12,8},{1,5},{5,1},{9,13},{13,9},{2,6},{6,2},{1... | collective-permute-start | bytes 208904 | tf_op jit(solution)/shard_map/ppermute | solution.py:504
  11.8 0.7 %models.4 = (f32[2,24,256]{2,1,0:T(8,128)S(1)}, f32[2,24,256]{2,1,0:T(8,128)S(1)}, f32[1,24,256]{2,1,0:T(8,128)S(1)}) custom-call(f32[4,24,256]{2,1,0:T(8,128)S(1)} %get-tuple-element.20.sci, f32[4,24,256]{2,1,0:T(8,128)S(1)} %get-tuple-element.21.weight, bf16[4,16,256]{2,1,0:T(8,128)(2,1)S(1)} %get-tuple-element.22.r, ...), custom_call_target="tpu_custom_call" | custom-call | flops 400000000 | bytes 1000000 | tf_op jit(solution)/shard_map/models/pallas_call | solution.py:510
  12.6 1.8 %collective-permute-done.5.refs_0_ = bf16[1,136,256]{2,1,0:T(8,128)(2,1)S(1)} collective-permute-done((bf16[1,136,256]{2,1,0:T(8,128)(2,1)S(1)}, bf16[1,136,256]{2,1,0:T(8,128)(2,1)S(1)}, u32[]{:S(2)}, u32[]{:S(2)}) %collective-permute-start.5) | collective-permute-done | bytes 69664 | tf_op jit(solution)/shard_map/ppermute | solution.py:504
  14.4 1.0 %models.5 = (f32[2,24,256]{2,1,0:T(8,128)S(1)}, f32[2,24,256]{2,1,0:T(8,128)S(1)}, f32[1,24,256]{2,1,0:T(8,128)S(1)}) custom-call(f32[4,24,256]{2,1,0:T(8,128)S(1)} %get-tuple-element.20.sci, f32[4,24,256]{2,1,0:T(8,128)S(1)} %get-tuple-element.21.weight, bf16[4,16,256]{2,1,0:T(8,128)(2,1)S(1)} %get-tuple-element.22.r, ...), custom_call_target="tpu_custom_call" | custom-call | flops 800000000 | bytes 1000000 | tf_op jit(solution)/shard_map/models/pallas_call | solution.py:510
  15.4 1.4 %collective-permute-done.4.refs_0_ = bf16[1,136,256]{2,1,0:T(8,128)(2,1)S(1)} collective-permute-done((bf16[1,136,256]{2,1,0:T(8,128)(2,1)S(1)}, bf16[1,136,256]{2,1,0:T(8,128)(2,1)S(1)}, u32[]{:S(2)}, u32[]{:S(2)}) %collective-permute-start.4) | collective-permute-done | bytes 69664 | tf_op jit(solution)/shard_map/ppermute | solution.py:504
  16.8 1.0 %models.6 = (f32[2,24,256]{2,1,0:T(8,128)S(1)}, f32[2,24,256]{2,1,0:T(8,128)S(1)}, f32[1,24,256]{2,1,0:T(8,128)S(1)}) custom-call(f32[4,24,256]{2,1,0:T(8,128)S(1)} %get-tuple-element.20.sci, f32[4,24,256]{2,1,0:T(8,128)S(1)} %get-tuple-element.21.weight, bf16[4,16,256]{2,1,0:T(8,128)(2,1)S(1)} %get-tuple-element.22.r, ...), custom_call_target="tpu_custom_call" | custom-call | flops 800000000 | bytes 1000000 | tf_op jit(solution)/shard_map/models/pallas_call | solution.py:510
  17.8 0.0 collective-permute-done.3.refs_0_
  17.8 1.7 %models.7 = (f32[4,24,256]{2,1,0:T(8,128)}, f32[2,24,256]{2,1,0:T(8,128)}) custom-call(f32[4,24,256]{2,1,0:T(8,128)S(1)} %get-tuple-element.20.sci, f32[4,24,256]{2,1,0:T(8,128)S(1)} %get-tuple-element.21.weight, bf16[4,16,256]{2,1,0:T(8,128)(2,1)S(1)} %get-tuple-element.22.r, bf16[2,56,384]{2,1,0:T(8,128)(2,1)S(1)} %get-tuple-element.25.slabs, ...), custom_call_target="tpu_custom_call" | custom-call | flops 800000000 | bytes 1000000 | tf_op jit(solution)/shard_map/models/pallas_call | solution.py:510
Async XLA Ops:
  0.6 5.4 %collective-permute-start = (bf16[2,24,256]{2,1,0:T(8,128)(2,1)}, bf16[2,24,256]{2,1,0:T(8,128)(2,1)S(1)}, u32[]{:S(2)}, u32[]{:S(2)}) collective-permute-start(bf16[2,24,256]{2,1,0:T(8,128)(2,1)} %refs_0_.1), channel_id=1, source_target_pairs={{0,2},{1,3},{2,0},{3,1},{4,6},{5,7},{6,4},{7,5},{8,10},{9,11},{10,... | collective-permute-start | bytes 73736 | tf_op jit(solution)/shard_map/ppermute | solution.py:471
  3.6 3.5 %collective-permute-start.2 = (bf16[2,24,256]{2,1,0:T(8,128)(2,1)}, bf16[2,24,256]{2,1,0:T(8,128)(2,1)S(1)}, u32[]{:S(2)}, u32[]{:S(2)}) collective-permute-start(bf16[2,24,256]{2,1,0:T(8,128)(2,1)} %refs_0_.1), channel_id=1, source_target_pairs={{0,3},{1,2},{2,1},{3,0},{4,7},{5,6},{6,5},{7,4},{8,11},{9,10},{10,... | collective-permute-start | bytes 73736 | tf_op jit(solution)/shard_map/ppermute | solution.py:471
  3.6 3.5 %collective-permute-start.1 = (bf16[2,24,256]{2,1,0:T(8,128)(2,1)}, bf16[2,24,256]{2,1,0:T(8,128)(2,1)S(1)}, u32[]{:S(2)}, u32[]{:S(2)}) collective-permute-start(bf16[2,24,256]{2,1,0:T(8,128)(2,1)} %refs_0_.1), channel_id=1, source_target_pairs={{0,1},{1,0},{2,3},{3,2},{4,5},{5,4},{6,7},{7,6},{8,9},{9,8},{10,11... | collective-permute-start | bytes 73736 | tf_op jit(solution)/shard_map/ppermute | solution.py:471
  7.4 7.0 %collective-permute-start.5 = (bf16[1,136,256]{2,1,0:T(8,128)(2,1)S(1)}, bf16[1,136,256]{2,1,0:T(8,128)(2,1)S(1)}, u32[]{:S(2)}, u32[]{:S(2)}) collective-permute-start(bf16[1,136,256]{2,1,0:T(8,128)(2,1)S(1)} %get-tuple-element.28), channel_id=1, source_target_pairs={{0,12},{4,8},{8,4},{12,0},{1,13},{5,9},{9,5},{13,1},{2,14},{6,10},... | collective-permute-start | bytes 208904 | tf_op jit(solution)/shard_map/ppermute | solution.py:504
  11.0 6.8 %collective-permute-start.3 = (bf16[1,136,256]{2,1,0:T(8,128)(2,1)S(1)}, bf16[1,136,256]{2,1,0:T(8,128)(2,1)S(1)}, u32[]{:S(2)}, u32[]{:S(2)}) collective-permute-start(bf16[1,136,256]{2,1,0:T(8,128)(2,1)S(1)} %get-tuple-element.26), channel_id=1, source_target_pairs={{0,8},{4,12},{8,0},{12,4},{1,9},{5,13},{9,1},{13,5},{2,10},{6,14},... | collective-permute-start | bytes 208904 | tf_op jit(solution)/shard_map/ppermute | solution.py:504
  11.0 5.7 %collective-permute-start.4 = (bf16[1,136,256]{2,1,0:T(8,128)(2,1)S(1)}, bf16[1,136,256]{2,1,0:T(8,128)(2,1)S(1)}, u32[]{:S(2)}, u32[]{:S(2)}) collective-permute-start(bf16[1,136,256]{2,1,0:T(8,128)(2,1)S(1)} %get-tuple-element.27), channel_id=1, source_target_pairs={{0,4},{4,0},{8,12},{12,8},{1,5},{5,1},{9,13},{13,9},{2,6},{6,2},{1... | collective-permute-start | bytes 208904 | tf_op jit(solution)/shard_map/ppermute | solution.py:504

commit v6 on v5

--- a/solution.py
+++ b/solution.py
@@ -318,47 +318,56 @@
             for c in range(per_owner):
                 job("sent", q, c, pay[c].astype(f32), r[q * per_owner + c].astype(f32))
 
-        row = (strip * h + iota((h, sz.lanes), 0)).astype(f32)
+        row = (strip * h + iota((h, 128), 0)).astype(f32)
         r_unit = (2.0 * row + 1.0) / (h * strips) - 1.0
+        r_unit = jnp.concatenate([r_unit] * (sz.lanes // 128), axis=1)
+        spot = iota((SLOT, CHUNK), 1)
+        filled = (spot % sz.span < FINE) & (spot < sz.per * sz.span)
+        c_units = []
+        for i in range(sz.chunks):
+            col = (band * w + iota((8, sz.lanes), 1) - i).astype(f32)
+            col = (2.0 * col + 1.0) / (w * bands) - 1.0
+            c_units.append(jnp.concatenate([col] * (h // 8), axis=0))
         for slot in range(2):
             used = sz.per * sz.span
             if used < CHUNK:
                 rhs[slot, used:] = jnp.zeros((CHUNK - used, sz.lanes), bf16)
 
-        def model(turn, slab, lines, scalars):
-            window, band_rows = rhs.at[turn % 2], lhs.at[turn % 2]
+        def windows(turn, slab, scalars):
+            window = rhs.at[turn % 2]
             down, across = scalars
             slab = pltpu.roll(slab, lax.rem(sz.rows + HALF - down, sz.rows), 0)[: sz.span]
             slab = pltpu.roll(slab.astype(bf16), lax.rem(sz.lanes + HALF - across, sz.lanes), 1)
             for slot in range(sz.per):
                 moved = pltpu.roll(slab, sz.lanes - slot * sz.chunks, 1) if slot else slab
                 window[slot * sz.span : (slot + 1) * sz.span] = moved
-            image = None
-            for i in reversed(range(sz.chunks)):
+
+        def band_matrix(turn, lines):
+            band_rows = lhs.at[turn % 2]
+            for i in range(sz.chunks):
                 line, phase = divmod(i, sz.phases)
                 part = lines[line * SLOT : (line + 1) * SLOT]
                 if phase:
                     part = pltpu.roll(part, CHUNK - phase * FINE, 1)
-                spot = iota(part.shape, 1)
-                part = jnp.where((spot % sz.span < FINE) & (spot < sz.per * sz.span), part, 0.0)
+                part = jnp.where(filled, part, 0.0)
                 at = i * NPOLY * h
                 for p in range(NPOLY):
                     band_rows[at + p * h : at + (p + 1) * h] = pltpu.roll(
                         jnp.broadcast_to(part[p : p + 1], (h, CHUNK)), 0, 1, stride=1, stride_axis=0
                     )
-                conv = jnp.dot(
-                    band_rows[at : at + NPOLY * h].astype(bf16), window[...], preferred_element_type=f32
-                )
-                conv = [conv[p * h : (p + 1) * h] for p in range(NPOLY)]
-                col = (band * w + iota((h, sz.lanes), 1) - i).astype(f32)
-                c_unit = (2.0 * col + 1.0) / (w * bands) - 1.0
-                value = (
-                    conv[0]
-                    + r_unit * (conv[1] + r_unit * conv[3] + c_unit * conv[4])
-                    + c_unit * (conv[2] + c_unit * conv[5])
-                )
-                image = value if image is None else pltpu.roll(image, sz.lanes - 1, 1) + value
-            return image[:, :w]
+
+        def chunk_image(turn, i):
+            at = i * NPOLY * h
+            conv = jnp.dot(
+                lhs[turn % 2, at : at + NPOLY * h].astype(bf16), rhs[turn % 2], preferred_element_type=f32
+            )
+            conv = [conv[p * h : (p + 1) * h] for p in range(NPOLY)]
+            c_unit = c_units[i]
+            return (
+                conv[0]
+                + r_unit * (conv[1] + r_unit * conv[3] + c_unit * conv[4])
+                + c_unit * (conv[2] + c_unit * conv[5])
+            )
 
         def sent_slab(got):
             main, halo = got[sz.main_at : sz.halo_at], got[sz.halo_at :]
@@ -390,9 +399,22 @@
         denom = [before[1][t] if before else jnp.zeros((h, w), f32) for t in range(tiles)]
         kept = 0
         settled = max(turn for turn, job in enumerate(jobs) if job[0] != "sent")
+        images = []
+        for turn in range(0, len(jobs), 2):
+            pair = list(enumerate(jobs))[turn : turn + 2]
+            for at, (kind, mine, got, lines, scalars, tile, own) in pair:
+                band_matrix(at, lines)
+            for at, (kind, mine, got, lines, scalars, tile, own) in pair:
+                windows(at, sent_slab(got) if kind == "sent" else slabs[tile].astype(f32), scalars)
+            parts = [None for _ in pair]
+            for i in reversed(range(sz.chunks)):
+                for slot, (at, _) in enumerate(pair):
+                    value = chunk_image(at, i)
+                    value = pltpu.roll(value, sz.lanes - i, 1) if i else value
+                    parts[slot] = value if parts[slot] is None else parts[slot] + value
+            images += [part[:, :w] for part in parts]
         for turn, (kind, mine, got, lines, scalars, tile, own) in enumerate(jobs):
-            slab = sent_slab(got) if kind == "sent" else slabs[tile].astype(f32)
-            image = model(turn, slab, lines, scalars)
+            image = images[turn]
             if kind == "owned":
                 science, seen = got[:h] + got[h : 2 * h], decode(got[2 * h : 3 * h])
             else:

time: 19.6 us -> 19.3 us (0.985)
  Pallas kernels: 6.85 us -> 6.28 us
  waiting for transfers between devices: 4.33 us -> 4.55 us
    pallas_call x4, Pallas kernels: 4.44 us -> 3.86 us  [local(): models(sz, n_epoch, tiles, count, ks, first, last, kept)]
    ppermute x3, waiting for transfers between devices: 3.22 us -> 3.44 us  [local(): pays[k] = lax.ppermute(send, 'epoch', pairs)]
  transfers between devices with their start and end apart: 6 -> 6, of which waited for: 3 -> 3; matrix products, arithmetic and copies ran while one was open for 0% -> 0% of each run, Pallas kernels for 25% -> 23%
where the time goes in v6:
time: 19.3 us; the launch traced here: 19.2 us
  starting transfers between devices  7.65 us (40%)
  Pallas kernels  6.28 us (33%)
  waiting for transfers between devices  4.55 us (24%)
  between operations  0.69 us (4%)
    ppermute x3, starting transfers between devices, local(): pays[k] = lax.ppermute(send, 'epoch', pairs)  4.45 us
    pallas_call x4, Pallas kernels, local(): models(sz, n_epoch, tiles, count, ks, first, last, kept)  3.86 us
    ppermute x3, waiting for transfers between devices, local(): pays[k] = lax.ppermute(send, 'epoch', pairs)  3.44 us
    ppermute x3, starting transfers between devices, surroundings(): sent[key] = lax.ppermute(block, ('strip', 'band'), pairs)  3.2 us
    pallas_call x1, Pallas kernels, call(): pl.pallas_call(body, in_specs=[hbm] * 9, out_specs=(vmem,) * 5, out_shape...  2.14 us
    ppermute x3, waiting for transfers between devices, surroundings(): sent[key] = lax.ppermute(block, ('strip', 'band'), pairs)  1.11 us
  transfers between devices with their start and end apart: 6, of which 3 were waited for; matrix products, arithmetic and copies ran while one was open for 0% of the time, Pallas kernels for 23%

profile of v6, /device:TPU:0, one launch (start us, length us, event | category | flops | bytes accessed | tf_op | source)
XLA Modules:
  0.0 19.2 jit_solution(11757988758174564703)
XLA Ops:
  0.6 3.0 %collective-permute-start = (bf16[2,24,256]{2,1,0:T(8,128)(2,1)}, bf16[2,24,256]{2,1,0:T(8,128)(2,1)S(1)}, u32[]{:S(2)}, u32[]{:S(2)}) collective-permute-start(bf16[2,24,256]{2,1,0:T(8,128)(2,1)} %refs_0_.1), channel_id=1, source_target_pairs={{0,2},{1,3},{2,0},{3,1},{4,6},{5,7},{6,4},{7,5},{8,10},{9,11},{10,... | collective-permute-start | bytes 73736 | tf_op jit(solution)/shard_map/ppermute | solution.py:493
  3.6 0.0 collective-permute-start.2
  3.6 0.2 collective-permute-start.1
  3.8 2.1 %prepare.1 = (bf16[4,16,256]{2,1,0:T(8,128)(2,1)S(1)}, bf16[4,72,256]{2,1,0:T(8,128)(2,1)S(1)}, bf16[2,24,256]{2,1,0:T(8,128)(2,1)S(1)}, f32[4,24,256]{2,1,0:T(8,128)S(1)}, f32[4,24,256]{2,1,0:T(8,128)S(1)}) custom-call(bf16[2,24,256]{2,1,0:T(8,128)(2,1)} %refs_0_.1, f32[4,24,256]{2,1,0:T(8,128)} %refs_1_.1, f32[4,24,256]{2,1,0:T(8,128)} %refs_2_.1, ...), custom_call_target="tpu_custom_call" | custom-call | flops 1000000000 | bytes 6000000 | tf_op jit(solution)/shard_map/prepare/pallas_call | solution.py:151
  6.0 0.0 collective-permute-done.low.high
  6.0 1.1 %collective-permute-done.2.low_left.high_left.low_right.high_right = bf16[2,24,256]{2,1,0:T(8,128)(2,1)S(1)} collective-permute-done((bf16[2,24,256]{2,1,0:T(8,128)(2,1)}, bf16[2,24,256]{2,1,0:T(8,128)(2,1)S(1)}, u32[]{:S(2)}, u32[]{:S(2)}) %collective-permute-start.2) | collective-permute-done | bytes 24608 | tf_op jit(solution)/shard_map/ppermute | solution.py:493
  7.1 0.0 collective-permute-done.1.left.right
  7.1 0.3 %pack.1 = (bf16[2,56,384]{2,1,0:T(8,128)(2,1)S(1)}, bf16[1,136,256]{2,1,0:T(8,128)(2,1)S(1)}, bf16[1,136,256]{2,1,0:T(8,128)(2,1)S(1)}, bf16[1,136,256]{2,1,0:T(8,128)(2,1)S(1)}) custom-call(bf16[2,24,256]{2,1,0:T(8,128)(2,1)S(1)} %get-tuple-element.23.own, bf16[2,24,256]{2,1,0:T(8,128)(2,1)S(1)} %collective-permute-done.low.high, ...), custom_call_target="tpu_custom_call" | custom-call | flops 1000000 | bytes 1000000 | tf_op jit(solution)/shard_map/pack/pallas_call | solution.py:520
  7.4 3.7 %collective-permute-start.5 = (bf16[1,136,256]{2,1,0:T(8,128)(2,1)S(1)}, bf16[1,136,256]{2,1,0:T(8,128)(2,1)S(1)}, u32[]{:S(2)}, u32[]{:S(2)}) collective-permute-start(bf16[1,136,256]{2,1,0:T(8,128)(2,1)S(1)} %get-tuple-element.28), channel_id=1, source_target_pairs={{0,12},{4,8},{8,4},{12,0},{1,13},{5,9},{9,5},{13,1},{2,14},{6,10},... | collective-permute-start | bytes 208904 | tf_op jit(solution)/shard_map/ppermute | solution.py:526
  11.0 0.0 collective-permute-start.3
  11.0 0.8 %collective-permute-start.4 = (bf16[1,136,256]{2,1,0:T(8,128)(2,1)S(1)}, bf16[1,136,256]{2,1,0:T(8,128)(2,1)S(1)}, u32[]{:S(2)}, u32[]{:S(2)}) collective-permute-start(bf16[1,136,256]{2,1,0:T(8,128)(2,1)S(1)} %get-tuple-element.27), channel_id=1, source_target_pairs={{0,4},{4,0},{8,12},{12,8},{1,5},{5,1},{9,13},{13,9},{2,6},{6,2},{1... | collective-permute-start | bytes 208904 | tf_op jit(solution)/shard_map/ppermute | solution.py:526
  11.8 0.7 %models.4 = (f32[2,24,256]{2,1,0:T(8,128)S(1)}, f32[2,24,256]{2,1,0:T(8,128)S(1)}, f32[1,24,256]{2,1,0:T(8,128)S(1)}) custom-call(f32[4,24,256]{2,1,0:T(8,128)S(1)} %get-tuple-element.20.sci, f32[4,24,256]{2,1,0:T(8,128)S(1)} %get-tuple-element.21.weight, bf16[4,16,256]{2,1,0:T(8,128)(2,1)S(1)} %get-tuple-element.22.r, ...), custom_call_target="tpu_custom_call" | custom-call | flops 400000000 | bytes 1000000 | tf_op jit(solution)/shard_map/models/pallas_call | solution.py:532
  12.5 1.9 %collective-permute-done.5.refs_0_ = bf16[1,136,256]{2,1,0:T(8,128)(2,1)S(1)} collective-permute-done((bf16[1,136,256]{2,1,0:T(8,128)(2,1)S(1)}, bf16[1,136,256]{2,1,0:T(8,128)(2,1)S(1)}, u32[]{:S(2)}, u32[]{:S(2)}) %collective-permute-start.5) | collective-permute-done | bytes 69664 | tf_op jit(solution)/shard_map/ppermute | solution.py:526
  14.4 0.9 %models.5 = (f32[2,24,256]{2,1,0:T(8,128)S(1)}, f32[2,24,256]{2,1,0:T(8,128)S(1)}, f32[1,24,256]{2,1,0:T(8,128)S(1)}) custom-call(f32[4,24,256]{2,1,0:T(8,128)S(1)} %get-tuple-element.20.sci, f32[4,24,256]{2,1,0:T(8,128)S(1)} %get-tuple-element.21.weight, bf16[4,16,256]{2,1,0:T(8,128)(2,1)S(1)} %get-tuple-element.22.r, ...), custom_call_target="tpu_custom_call" | custom-call | flops 800000000 | bytes 1000000 | tf_op jit(solution)/shard_map/models/pallas_call | solution.py:532
  15.3 1.5 %collective-permute-done.4.refs_0_ = bf16[1,136,256]{2,1,0:T(8,128)(2,1)S(1)} collective-permute-done((bf16[1,136,256]{2,1,0:T(8,128)(2,1)S(1)}, bf16[1,136,256]{2,1,0:T(8,128)(2,1)S(1)}, u32[]{:S(2)}, u32[]{:S(2)}) %collective-permute-start.4) | collective-permute-done | bytes 69664 | tf_op jit(solution)/shard_map/ppermute | solution.py:526
  16.8 0.9 %models.6 = (f32[2,24,256]{2,1,0:T(8,128)S(1)}, f32[2,24,256]{2,1,0:T(8,128)S(1)}, f32[1,24,256]{2,1,0:T(8,128)S(1)}) custom-call(f32[4,24,256]{2,1,0:T(8,128)S(1)} %get-tuple-element.20.sci, f32[4,24,256]{2,1,0:T(8,128)S(1)} %get-tuple-element.21.weight, bf16[4,16,256]{2,1,0:T(8,128)(2,1)S(1)} %get-tuple-element.22.r, ...), custom_call_target="tpu_custom_call" | custom-call | flops 800000000 | bytes 1000000 | tf_op jit(solution)/shard_map/models/pallas_call | solution.py:532
  17.6 0.0 collective-permute-done.3.refs_0_
  17.7 1.5 %models.7 = (f32[4,24,256]{2,1,0:T(8,128)}, f32[2,24,256]{2,1,0:T(8,128)}) custom-call(f32[4,24,256]{2,1,0:T(8,128)S(1)} %get-tuple-element.20.sci, f32[4,24,256]{2,1,0:T(8,128)S(1)} %get-tuple-element.21.weight, bf16[4,16,256]{2,1,0:T(8,128)(2,1)S(1)} %get-tuple-element.22.r, bf16[2,56,384]{2,1,0:T(8,128)(2,1)S(1)} %get-tuple-element.25.slabs, ...), custom_call_target="tpu_custom_call" | custom-call | flops 800000000 | bytes 1000000 | tf_op jit(solution)/shard_map/models/pallas_call | solution.py:532
Async XLA Ops:
  0.6 5.4 %collective-permute-start = (bf16[2,24,256]{2,1,0:T(8,128)(2,1)}, bf16[2,24,256]{2,1,0:T(8,128)(2,1)S(1)}, u32[]{:S(2)}, u32[]{:S(2)}) collective-permute-start(bf16[2,24,256]{2,1,0:T(8,128)(2,1)} %refs_0_.1), channel_id=1, source_target_pairs={{0,2},{1,3},{2,0},{3,1},{4,6},{5,7},{6,4},{7,5},{8,10},{9,11},{10,... | collective-permute-start | bytes 73736 | tf_op jit(solution)/shard_map/ppermute | solution.py:493
  3.6 3.5 %collective-permute-start.2 = (bf16[2,24,256]{2,1,0:T(8,128)(2,1)}, bf16[2,24,256]{2,1,0:T(8,128)(2,1)S(1)}, u32[]{:S(2)}, u32[]{:S(2)}) collective-permute-start(bf16[2,24,256]{2,1,0:T(8,128)(2,1)} %refs_0_.1), channel_id=1, source_target_pairs={{0,3},{1,2},{2,1},{3,0},{4,7},{5,6},{6,5},{7,4},{8,11},{9,10},{10,... | collective-permute-start | bytes 73736 | tf_op jit(solution)/shard_map/ppermute | solution.py:493
  3.6 3.5 %collective-permute-start.1 = (bf16[2,24,256]{2,1,0:T(8,128)(2,1)}, bf16[2,24,256]{2,1,0:T(8,128)(2,1)S(1)}, u32[]{:S(2)}, u32[]{:S(2)}) collective-permute-start(bf16[2,24,256]{2,1,0:T(8,128)(2,1)} %refs_0_.1), channel_id=1, source_target_pairs={{0,1},{1,0},{2,3},{3,2},{4,5},{5,4},{6,7},{7,6},{8,9},{9,8},{10,11... | collective-permute-start | bytes 73736 | tf_op jit(solution)/shard_map/ppermute | solution.py:493
  7.4 7.0 %collective-permute-start.5 = (bf16[1,136,256]{2,1,0:T(8,128)(2,1)S(1)}, bf16[1,136,256]{2,1,0:T(8,128)(2,1)S(1)}, u32[]{:S(2)}, u32[]{:S(2)}) collective-permute-start(bf16[1,136,256]{2,1,0:T(8,128)(2,1)S(1)} %get-tuple-element.28), channel_id=1, source_target_pairs={{0,12},{4,8},{8,4},{12,0},{1,13},{5,9},{9,5},{13,1},{2,14},{6,10},... | collective-permute-start | bytes 208904 | tf_op jit(solution)/shard_map/ppermute | solution.py:526
  11.0 6.6 %collective-permute-start.3 = (bf16[1,136,256]{2,1,0:T(8,128)(2,1)S(1)}, bf16[1,136,256]{2,1,0:T(8,128)(2,1)S(1)}, u32[]{:S(2)}, u32[]{:S(2)}) collective-permute-start(bf16[1,136,256]{2,1,0:T(8,128)(2,1)S(1)} %get-tuple-element.26), channel_id=1, source_target_pairs={{0,8},{4,12},{8,0},{12,4},{1,9},{5,13},{9,1},{13,5},{2,10},{6,14},... | collective-permute-start | bytes 208904 | tf_op jit(solution)/shard_map/ppermute | solution.py:526
  11.0 5.7 %collective-permute-start.4 = (bf16[1,136,256]{2,1,0:T(8,128)(2,1)S(1)}, bf16[1,136,256]{2,1,0:T(8,128)(2,1)S(1)}, u32[]{:S(2)}, u32[]{:S(2)}) collective-permute-start(bf16[1,136,256]{2,1,0:T(8,128)(2,1)S(1)} %get-tuple-element.27), channel_id=1, source_target_pairs={{0,4},{4,0},{8,12},{12,8},{1,5},{5,1},{9,13},{13,9},{2,6},{6,2},{1... | collective-permute-start | bytes 208904 | tf_op jit(solution)/shard_map/ppermute | solution.py:526

commit v7 on v6

--- a/solution.py
+++ b/solution.py
@@ -35,7 +35,7 @@
         self.lines = -(-KS // (self.per * self.phases))
         self.chunks = self.lines * self.phases
         self.depth = self.chunks * CHUNK
-        self.sw_rows = 3 * height
+        self.sw_rows = 2 * height
         self.r_rows = self.lines * SLOT
         self.one_side = strips <= 2
         self.sent = height + 16 if self.one_side else self.rows
@@ -54,28 +54,55 @@
     return lax.broadcasted_iota(jnp.int32, shape, axis)
 
 
-def split(value):
-    high = value.astype(bf16).astype(f32)
-    return high, value - high
-
-
-def encode(weight):
+def raised(value, power, bits):
+    for bit in range(bits):
+        more = (power >> bit) & 1 == 1
+        for _ in range(2 if bit == 7 else 1):
+            value = jnp.where(more, value * 2.0 ** (1 << min(bit, 6)), value)
+    return value
+
+
+def lowered(value, least, bits):
+    power = jnp.zeros(value.shape, jnp.int32)
+    for bit in reversed(range(bits)):
+        more = value >= 2.0 ** ((1 << bit) + least)
+        for _ in range(2 if bit == 7 else 1):
+            value = jnp.where(more, value * 2.0 ** -(1 << min(bit, 6)), value)
+        power = jnp.where(more, power + (1 << bit), power)
+    return value, power
+
+
+def encode_weight(weight):
     code = jnp.minimum((weight * 65536.0 + 0.5).astype(jnp.int32), 32767)
-    value = (128 + ((code >> 1) & 127)).astype(f32) * 2.0**-70
-    for bit in range(7):
-        value = jnp.where((code >> (8 + bit)) & 1 == 1, value * 2.0 ** (1 << bit), value)
+    value = raised((128 + ((code >> 1) & 127)).astype(f32) * 2.0**-70, code >> 8, 7)
     return jnp.where(code & 1 == 1, -value, value)
 
 
-def decode(value):
-    size = jnp.abs(value)
-    code = jnp.zeros_like(size)
-    for bit in range(6, -1, -1):
-        above = size >= 2.0 ** ((1 << bit) - 63)
-        size = jnp.where(above, size * 2.0 ** -(1 << bit), size)
-        code = jnp.where(above, code + (256 << bit), code)
-    code = code + (size * 2.0**71 - 256.0)
+def decode_weight(value):
+    size, power = lowered(jnp.abs(value), -63, 7)
+    code = (power * 256).astype(f32) + (size * 2.0**71 - 256.0)
     return jnp.where(value < 0.0, code + 1.0, code) * 2.0**-16
+
+
+def encode_science(science):
+    size, power = lowered(jnp.abs(science) * 2.0**26, 0, 5)
+    fine = power >= 14
+    code = ((size - 1.0) * jnp.where(fine, 2048.0, 128.0) + 0.5).astype(jnp.int32)
+    code = jnp.minimum(code, jnp.where(fine, 2047, 127))
+    exponent = jnp.where(fine, (power - 14) * 16 + (code & 15), 240 + power)
+    value = (128 + jnp.where(fine, code >> 4, code)).astype(f32) * 2.0**-66 * 2.0**-67
+    value = jnp.where(size >= 1.0, raised(value, exponent, 8), 0.0)
+    return jnp.where(science < 0.0, -value, value)
+
+
+def decode_science(value):
+    size, exponent = lowered(jnp.abs(value), -126, 8)
+    coarse = size * 2.0**66 * 2.0**67
+    fine = exponent < 240
+    mantissa = jnp.where(fine, coarse * 16.0 + (exponent & 15).astype(f32), coarse * 16.0)
+    power = jnp.where(fine, (exponent >> 4) + 14, exponent - 240)
+    size = jnp.where(value == 0.0, 0.0, raised(mantissa * 2.0**-37, power, 5))
+    return jnp.where(value < 0.0, -size, size)
 
 
 def prepare(sz, n_epoch, tiles, count, nsel):
@@ -124,7 +151,16 @@
         rows = lax.dot_general(
             images.astype(bf16), place[...], (((0,), (0,)), ((), ())), preferred_element_type=f32
         )
+        for copy in reversed(copies[:4]):
+            copy.wait()
         for e in range(count):
+            weight_out[e] = mask[e].astype(f32) / var[e]
+            science = jnp.where(mask[e] == 0, 0.0, sci_out[e])
+            top = jnp.max(jnp.abs(science), axis=(0, 1), keepdims=True)
+            _, power = lowered(top * 2.0**100, 0, 7)
+            science = science * raised(jnp.ones_like(top), 102 - power, 7)
+            parts = [encode_science(science), encode_weight(weight_out[e])]
+            sw_out[e] = jnp.concatenate(parts, axis=0).astype(bf16)
             mine = rows[e * SLOT : (e + 1) * SLOT]
             mine = jnp.concatenate(
                 [mine[:, i * CHUNK : (i + 1) * CHUNK] for i in range(sz.lines)], axis=0
@@ -132,16 +168,11 @@
             tile = inter[e // per_owner * count + me * per_owner + e % per_owner] - me * tiles
             tile = jnp.clip(tile, 0, tiles - 1).astype(f32)
             down, across = offs[0:1, e : e + 1].astype(f32), offs[1:2, e : e + 1].astype(f32)
+            scale = raised(jnp.full_like(top, 2.0**-102), power, 7)
             spare, spot = iota(mine.shape, 0) == NPOLY, iota(mine.shape, 1)
-            for lane, value in enumerate((down, across, tile)):
+            for lane, value in enumerate((down, across, tile, scale)):
                 mine = jnp.where(spare & (spot == lane), value, mine)
             r_out[e] = mine.astype(bf16)
-        for copy in reversed(copies[:4]):
-            copy.wait()
-        for e in range(count):
-            weight_out[e] = mask[e].astype(f32) / var[e]
-            parts = [*split(sci_out[e]), encode(weight_out[e])]
-            sw_out[e] = jnp.concatenate(parts, axis=0).astype(bf16)
 
     hbm, vmem = pl.BlockSpec(memory_space=pltpu.HBM), pl.BlockSpec(memory_space=pltpu.VMEM)
     shape = (count, sz.height, sz.width)
@@ -416,7 +447,8 @@
         for turn, (kind, mine, got, lines, scalars, tile, own) in enumerate(jobs):
             image = images[turn]
             if kind == "owned":
-                science, seen = got[:h] + got[h : 2 * h], decode(got[2 * h : 3 * h])
+                scale = jnp.broadcast_to(lines[NPOLY : NPOLY + 1, 3:4], (h, w))
+                science, seen = decode_science(got[:h]) * scale, decode_weight(got[h : 2 * h])
             else:
                 science, seen = sci[mine], weight[mine]
                 if last:

time: 19.3 us -> 18.1 us (0.938)
  waiting for transfers between devices: 4.55 us -> 2.8 us
  Pallas kernels: 6.28 us -> 6.86 us
    ppermute x3, waiting for transfers between devices: 3.44 us -> 2.1 us  [local(): pays[k] = lax.ppermute(send, 'epoch', pairs)]
    ppermute x3, waiting for transfers between devices: 1.11 us -> 0.7 us  [surroundings(): sent[key] = lax.ppermute(block, ('strip', 'band'), pairs)]
    pallas_call x1, Pallas kernels: 2.14 us -> 2.56 us  [call(): pl.pallas_call(body, in_specs=[hbm] * 9, out_specs=(vmem,) * 5, out_shape...]
  transfers between devices with their start and end apart: 6 -> 6, of which waited for: 3 -> 3; matrix products, arithmetic and copies ran while one was open for 0% -> 0% of each run, Pallas kernels for 23% -> 28%
where the time goes in v7:
time: 18.1 us; the launch traced here: 18 us
  starting transfers between devices  7.65 us (42%)
  Pallas kernels  6.86 us (38%)
  waiting for transfers between devices  2.8 us (15%)
  between operations  0.68 us (4%)
    ppermute x3, starting transfers between devices, local(): pays[k] = lax.ppermute(send, 'epoch', pairs)  4.45 us
    pallas_call x4, Pallas kernels, local(): models(sz, n_epoch, tiles, count, ks, first, last, kept)  4.03 us
    ppermute x3, starting transfers between devices, surroundings(): sent[key] = lax.ppermute(block, ('strip', 'band'), pairs)  3.2 us
    pallas_call x1, Pallas kernels, call(): pl.pallas_call(body, in_specs=[hbm] * 9, out_specs=(vmem,) * 5, out_shape...  2.56 us
    ppermute x3, waiting for transfers between devices, local(): pays[k] = lax.ppermute(send, 'epoch', pairs)  2.1 us
    ppermute x3, waiting for transfers between devices, surroundings(): sent[key] = lax.ppermute(block, ('strip', 'band'), pairs)  0.7 us
  transfers between devices with their start and end apart: 6, of which 3 were waited for; matrix products, arithmetic and copies ran while one was open for 0% of the time, Pallas kernels for 28%

profile of v7, /device:TPU:0, one launch (start us, length us, event | category | flops | bytes accessed | tf_op | source)
XLA Modules:
  0.0 18.0 jit_solution(5987028583002322134)
XLA Ops:
  0.6 3.0 %collective-permute-start = (bf16[2,24,256]{2,1,0:T(8,128)(2,1)}, bf16[2,24,256]{2,1,0:T(8,128)(2,1)S(1)}, u32[]{:S(2)}, u32[]{:S(2)}) collective-permute-start(bf16[2,24,256]{2,1,0:T(8,128)(2,1)} %refs_0_.1), channel_id=1, source_target_pairs={{0,2},{1,3},{2,0},{3,1},{4,6},{5,7},{6,4},{7,5},{8,10},{9,11},{10,... | collective-permute-start | bytes 73736 | tf_op jit(solution)/shard_map/ppermute | solution.py:525
  3.6 0.0 collective-permute-start.2
  3.6 0.2 %collective-permute-start.1 = (bf16[2,24,256]{2,1,0:T(8,128)(2,1)}, bf16[2,24,256]{2,1,0:T(8,128)(2,1)S(1)}, u32[]{:S(2)}, u32[]{:S(2)}) collective-permute-start(bf16[2,24,256]{2,1,0:T(8,128)(2,1)} %refs_0_.1), channel_id=1, source_target_pairs={{0,1},{1,0},{2,3},{3,2},{4,5},{5,4},{6,7},{7,6},{8,9},{9,8},{10,11... | collective-permute-start | bytes 73736 | tf_op jit(solution)/shard_map/ppermute | solution.py:525
  3.8 2.6 %prepare.1 = (bf16[4,16,256]{2,1,0:T(8,128)(2,1)S(1)}, bf16[4,48,256]{2,1,0:T(8,128)(2,1)S(1)}, bf16[2,24,256]{2,1,0:T(8,128)(2,1)S(1)}, f32[4,24,256]{2,1,0:T(8,128)S(1)}, f32[4,24,256]{2,1,0:T(8,128)S(1)}) custom-call(bf16[2,24,256]{2,1,0:T(8,128)(2,1)} %refs_0_.1, f32[4,24,256]{2,1,0:T(8,128)} %refs_1_.1, f32[4,24,256]{2,1,0:T(8,128)} %refs_2_.1, ...), custom_call_target="tpu_custom_call" | custom-call | flops 1000000000 | bytes 6000000 | tf_op jit(solution)/shard_map/prepare/pallas_call | solution.py:182
  6.4 0.0 collective-permute-done.low.high
  6.4 0.7 %collective-permute-done.2.low_left.high_left.low_right.high_right = bf16[2,24,256]{2,1,0:T(8,128)(2,1)S(1)} collective-permute-done((bf16[2,24,256]{2,1,0:T(8,128)(2,1)}, bf16[2,24,256]{2,1,0:T(8,128)(2,1)S(1)}, u32[]{:S(2)}, u32[]{:S(2)}) %collective-permute-start.2) | collective-permute-done | bytes 24608 | tf_op jit(solution)/shard_map/ppermute | solution.py:525
  7.1 0.0 collective-permute-done.1.left.right
  7.1 0.3 %pack.1 = (bf16[2,56,384]{2,1,0:T(8,128)(2,1)S(1)}, bf16[1,112,256]{2,1,0:T(8,128)(2,1)S(1)}, bf16[1,112,256]{2,1,0:T(8,128)(2,1)S(1)}, bf16[1,112,256]{2,1,0:T(8,128)(2,1)S(1)}) custom-call(bf16[2,24,256]{2,1,0:T(8,128)(2,1)S(1)} %get-tuple-element.23.own, bf16[2,24,256]{2,1,0:T(8,128)(2,1)S(1)} %collective-permute-done.low.high, ...), custom_call_target="tpu_custom_call" | custom-call | flops 1000000 | bytes 1000000 | tf_op jit(solution)/shard_map/pack/pallas_call | solution.py:552
  7.4 3.7 %collective-permute-start.5 = (bf16[1,112,256]{2,1,0:T(8,128)(2,1)S(1)}, bf16[1,112,256]{2,1,0:T(8,128)(2,1)S(1)}, u32[]{:S(2)}, u32[]{:S(2)}) collective-permute-start(bf16[1,112,256]{2,1,0:T(8,128)(2,1)S(1)} %get-tuple-element.28), channel_id=1, source_target_pairs={{0,12},{4,8},{8,4},{12,0},{1,13},{5,9},{9,5},{13,1},{2,14},{6,10},... | collective-permute-start | bytes 172040 | tf_op jit(solution)/shard_map/ppermute | solution.py:558
  11.0 0.0 collective-permute-start.3
  11.0 0.8 %collective-permute-start.4 = (bf16[1,112,256]{2,1,0:T(8,128)(2,1)S(1)}, bf16[1,112,256]{2,1,0:T(8,128)(2,1)S(1)}, u32[]{:S(2)}, u32[]{:S(2)}) collective-permute-start(bf16[1,112,256]{2,1,0:T(8,128)(2,1)S(1)} %get-tuple-element.27), channel_id=1, source_target_pairs={{0,4},{4,0},{8,12},{12,8},{1,5},{5,1},{9,13},{13,9},{2,6},{6,2},{1... | collective-permute-start | bytes 172040 | tf_op jit(solution)/shard_map/ppermute | solution.py:558
  11.8 0.7 %models.4 = (f32[2,24,256]{2,1,0:T(8,128)S(1)}, f32[2,24,256]{2,1,0:T(8,128)S(1)}, f32[1,24,256]{2,1,0:T(8,128)S(1)}) custom-call(f32[4,24,256]{2,1,0:T(8,128)S(1)} %get-tuple-element.20.sci, f32[4,24,256]{2,1,0:T(8,128)S(1)} %get-tuple-element.21.weight, bf16[4,16,256]{2,1,0:T(8,128)(2,1)S(1)} %get-tuple-element.22.r, ...), custom_call_target="tpu_custom_call" | custom-call | flops 400000000 | bytes 1000000 | tf_op jit(solution)/shard_map/models/pallas_call | solution.py:564
  12.5 1.4 %collective-permute-done.5.refs_0_ = bf16[1,112,256]{2,1,0:T(8,128)(2,1)S(1)} collective-permute-done((bf16[1,112,256]{2,1,0:T(8,128)(2,1)S(1)}, bf16[1,112,256]{2,1,0:T(8,128)(2,1)S(1)}, u32[]{:S(2)}, u32[]{:S(2)}) %collective-permute-start.5) | collective-permute-done | bytes 57376 | tf_op jit(solution)/shard_map/ppermute | solution.py:558
  13.9 0.9 %models.5 = (f32[2,24,256]{2,1,0:T(8,128)S(1)}, f32[2,24,256]{2,1,0:T(8,128)S(1)}, f32[1,24,256]{2,1,0:T(8,128)S(1)}) custom-call(f32[4,24,256]{2,1,0:T(8,128)S(1)} %get-tuple-element.20.sci, f32[4,24,256]{2,1,0:T(8,128)S(1)} %get-tuple-element.21.weight, bf16[4,16,256]{2,1,0:T(8,128)(2,1)S(1)} %get-tuple-element.22.r, ...), custom_call_target="tpu_custom_call" | custom-call | flops 800000000 | bytes 1000000 | tf_op jit(solution)/shard_map/models/pallas_call | solution.py:564
  14.8 0.7 %collective-permute-done.4.refs_0_ = bf16[1,112,256]{2,1,0:T(8,128)(2,1)S(1)} collective-permute-done((bf16[1,112,256]{2,1,0:T(8,128)(2,1)S(1)}, bf16[1,112,256]{2,1,0:T(8,128)(2,1)S(1)}, u32[]{:S(2)}, u32[]{:S(2)}) %collective-permute-start.4) | collective-permute-done | bytes 57376 | tf_op jit(solution)/shard_map/ppermute | solution.py:558
  15.5 0.9 %models.6 = (f32[2,24,256]{2,1,0:T(8,128)S(1)}, f32[2,24,256]{2,1,0:T(8,128)S(1)}, f32[1,24,256]{2,1,0:T(8,128)S(1)}) custom-call(f32[4,24,256]{2,1,0:T(8,128)S(1)} %get-tuple-element.20.sci, f32[4,24,256]{2,1,0:T(8,128)S(1)} %get-tuple-element.21.weight, bf16[4,16,256]{2,1,0:T(8,128)(2,1)S(1)} %get-tuple-element.22.r, ...), custom_call_target="tpu_custom_call" | custom-call | flops 800000000 | bytes 1000000 | tf_op jit(solution)/shard_map/models/pallas_call | solution.py:564
  16.4 0.0 collective-permute-done.3.refs_0_
  16.4 1.6 %models.7 = (f32[4,24,256]{2,1,0:T(8,128)}, f32[2,24,256]{2,1,0:T(8,128)}) custom-call(f32[4,24,256]{2,1,0:T(8,128)S(1)} %get-tuple-element.20.sci, f32[4,24,256]{2,1,0:T(8,128)S(1)} %get-tuple-element.21.weight, bf16[4,16,256]{2,1,0:T(8,128)(2,1)S(1)} %get-tuple-element.22.r, bf16[2,56,384]{2,1,0:T(8,128)(2,1)S(1)} %get-tuple-element.25.slabs, ...), custom_call_target="tpu_custom_call" | custom-call | flops 800000000 | bytes 1000000 | tf_op jit(solution)/shard_map/models/pallas_call | solution.py:564
Async XLA Ops:
  0.6 5.8 %collective-permute-start = (bf16[2,24,256]{2,1,0:T(8,128)(2,1)}, bf16[2,24,256]{2,1,0:T(8,128)(2,1)S(1)}, u32[]{:S(2)}, u32[]{:S(2)}) collective-permute-start(bf16[2,24,256]{2,1,0:T(8,128)(2,1)} %refs_0_.1), channel_id=1, source_target_pairs={{0,2},{1,3},{2,0},{3,1},{4,6},{5,7},{6,4},{7,5},{8,10},{9,11},{10,... | collective-permute-start | bytes 73736 | tf_op jit(solution)/shard_map/ppermute | solution.py:525
  3.6 3.5 %collective-permute-start.2 = (bf16[2,24,256]{2,1,0:T(8,128)(2,1)}, bf16[2,24,256]{2,1,0:T(8,128)(2,1)S(1)}, u32[]{:S(2)}, u32[]{:S(2)}) collective-permute-start(bf16[2,24,256]{2,1,0:T(8,128)(2,1)} %refs_0_.1), channel_id=1, source_target_pairs={{0,3},{1,2},{2,1},{3,0},{4,7},{5,6},{6,5},{7,4},{8,11},{9,10},{10,... | collective-permute-start | bytes 73736 | tf_op jit(solution)/shard_map/ppermute | solution.py:525
  3.6 3.5 %collective-permute-start.1 = (bf16[2,24,256]{2,1,0:T(8,128)(2,1)}, bf16[2,24,256]{2,1,0:T(8,128)(2,1)S(1)}, u32[]{:S(2)}, u32[]{:S(2)}) collective-permute-start(bf16[2,24,256]{2,1,0:T(8,128)(2,1)} %refs_0_.1), channel_id=1, source_target_pairs={{0,1},{1,0},{2,3},{3,2},{4,5},{5,4},{6,7},{7,6},{8,9},{9,8},{10,11... | collective-permute-start | bytes 73736 | tf_op jit(solution)/shard_map/ppermute | solution.py:525
  7.4 6.5 %collective-permute-start.5 = (bf16[1,112,256]{2,1,0:T(8,128)(2,1)S(1)}, bf16[1,112,256]{2,1,0:T(8,128)(2,1)S(1)}, u32[]{:S(2)}, u32[]{:S(2)}) collective-permute-start(bf16[1,112,256]{2,1,0:T(8,128)(2,1)S(1)} %get-tuple-element.28), channel_id=1, source_target_pairs={{0,12},{4,8},{8,4},{12,0},{1,13},{5,9},{9,5},{13,1},{2,14},{6,10},... | collective-permute-start | bytes 172040 | tf_op jit(solution)/shard_map/ppermute | solution.py:558
  11.0 5.4 %collective-permute-start.3 = (bf16[1,112,256]{2,1,0:T(8,128)(2,1)S(1)}, bf16[1,112,256]{2,1,0:T(8,128)(2,1)S(1)}, u32[]{:S(2)}, u32[]{:S(2)}) collective-permute-start(bf16[1,112,256]{2,1,0:T(8,128)(2,1)S(1)} %get-tuple-element.26), channel_id=1, source_target_pairs={{0,8},{4,12},{8,0},{12,4},{1,9},{5,13},{9,1},{13,5},{2,10},{6,14},... | collective-permute-start | bytes 172040 | tf_op jit(solution)/shard_map/ppermute | solution.py:558
  11.0 4.4 %collective-permute-start.4 = (bf16[1,112,256]{2,1,0:T(8,128)(2,1)S(1)}, bf16[1,112,256]{2,1,0:T(8,128)(2,1)S(1)}, u32[]{:S(2)}, u32[]{:S(2)}) collective-permute-start(bf16[1,112,256]{2,1,0:T(8,128)(2,1)S(1)} %get-tuple-element.27), channel_id=1, source_target_pairs={{0,4},{4,0},{8,12},{12,8},{1,5},{5,1},{9,13},{13,9},{2,6},{6,2},{1... | collective-permute-start | bytes 172040 | tf_op jit(solution)/shard_map/ppermute | solution.py:558

commit v8 on v7

--- a/solution.py
+++ b/solution.py
@@ -33,8 +33,7 @@
         self.phases = self.span // FINE
         self.per = CHUNK // self.span
         self.lines = -(-KS // (self.per * self.phases))
-        self.chunks = self.lines * self.phases
-        self.depth = self.chunks * CHUNK
+        self.depth = self.lines * CHUNK
         self.sw_rows = 2 * height
         self.r_rows = self.lines * SLOT
         self.one_side = strips <= 2
@@ -46,62 +45,67 @@
         self.total = self.halo_at + self.halo_rows
 
     def place(self, column):
-        slot, chunk = column // self.chunks, column % self.chunks
-        return chunk // self.phases * CHUNK + (slot * self.phases + chunk % self.phases) * FINE
+        slot, phase = column // self.phases, column % self.phases
+        return slot // self.per * CHUNK + (slot % self.per * self.phases + phase) * FINE
 
 
 def iota(shape, axis):
     return lax.broadcasted_iota(jnp.int32, shape, axis)
 
 
-def raised(value, power, bits):
-    for bit in range(bits):
-        more = (power >> bit) & 1 == 1
-        for _ in range(2 if bit == 7 else 1):
-            value = jnp.where(more, value * 2.0 ** (1 << min(bit, 6)), value)
-    return value
-
-
-def lowered(value, least, bits):
-    power = jnp.zeros(value.shape, jnp.int32)
-    for bit in reversed(range(bits)):
-        more = value >= 2.0 ** ((1 << bit) + least)
-        for _ in range(2 if bit == 7 else 1):
-            value = jnp.where(more, value * 2.0 ** -(1 << min(bit, 6)), value)
-        power = jnp.where(more, power + (1 << bit), power)
-    return value, power
+def whole(value):
+    return jnp.floor(value + 0.5)
+
+
+def exponent_of(value):
+    return jnp.floor(jnp.log2(value))
+
+
+def join(mantissa, exponent):
+    return (1.0 + mantissa * 2.0**-7) * jnp.exp2(exponent)
+
+
+def part(value):
+    exponent = jnp.floor(jnp.log2(value) + 0.003)
+    return whole((value * jnp.exp2(-exponent) - 1.0) * 128.0), exponent
 
 
 def encode_weight(weight):
-    code = jnp.minimum((weight * 65536.0 + 0.5).astype(jnp.int32), 32767)
-    value = raised((128 + ((code >> 1) & 127)).astype(f32) * 2.0**-70, code >> 8, 7)
-    return jnp.where(code & 1 == 1, -value, value)
+    code = jnp.minimum(whole(weight * 65536.0), 32767.0)
+    half = jnp.floor(code * 0.5)
+    exponent = jnp.floor(half * 2.0**-7)
+    value = join(half - exponent * 128.0, exponent - 63.0)
+    return jnp.where(code > 2.0 * half, -value, value)
 
 
 def decode_weight(value):
-    size, power = lowered(jnp.abs(value), -63, 7)
-    code = (power * 256).astype(f32) + (size * 2.0**71 - 256.0)
+    mantissa, exponent = part(jnp.abs(value))
+    code = (exponent + 63.0) * 256.0 + mantissa * 2.0
     return jnp.where(value < 0.0, code + 1.0, code) * 2.0**-16
 
 
 def encode_science(science):
-    size, power = lowered(jnp.abs(science) * 2.0**26, 0, 5)
-    fine = power >= 14
-    code = ((size - 1.0) * jnp.where(fine, 2048.0, 128.0) + 0.5).astype(jnp.int32)
-    code = jnp.minimum(code, jnp.where(fine, 2047, 127))
-    exponent = jnp.where(fine, (power - 14) * 16 + (code & 15), 240 + power)
-    value = (128 + jnp.where(fine, code >> 4, code)).astype(f32) * 2.0**-66 * 2.0**-67
-    value = jnp.where(size >= 1.0, raised(value, exponent, 8), 0.0)
+    size = jnp.abs(science)
+    power = jnp.clip(exponent_of(jnp.maximum(size, 2.0**-30)), -24.0, 2.0)
+    fine = power >= -12.0
+    steps = jnp.where(fine, 2048.0, 128.0)
+    code = jnp.clip(whole((size * jnp.exp2(-power) - 1.0) * steps), 0.0, steps - 1.0)
+    high = jnp.floor(code * 0.0625)
+    exponent = jnp.where(fine, power * 16.0 + (code - 16.0 * high) + 192.0, power + 264.0)
+    value = join(jnp.where(fine, high, code), exponent - 125.0)
+    value = jnp.where(size < 2.0**-24, 0.0, value)
     return jnp.where(science < 0.0, -value, value)
 
 
 def decode_science(value):
-    size, exponent = lowered(jnp.abs(value), -126, 8)
-    coarse = size * 2.0**66 * 2.0**67
-    fine = exponent < 240
-    mantissa = jnp.where(fine, coarse * 16.0 + (exponent & 15).astype(f32), coarse * 16.0)
-    power = jnp.where(fine, (exponent >> 4) + 14, exponent - 240)
-    size = jnp.where(value == 0.0, 0.0, raised(mantissa * 2.0**-37, power, 5))
+    size = jnp.abs(value)
+    mantissa, exponent = part(jnp.maximum(size, 2.0**-125))
+    exponent = exponent + 125.0
+    high = jnp.floor(exponent * 0.0625)
+    fine = exponent < 240.0
+    low = jnp.where(fine, exponent - 16.0 * high, 0.0)
+    power = jnp.where(fine, high - 12.0, exponent - 264.0)
+    size = jnp.where(size == 0.0, 0.0, (2048.0 + mantissa * 16.0 + low) * 2.0**-11 * jnp.exp2(power))
     return jnp.where(value < 0.0, -size, size)
 
 
@@ -157,8 +161,8 @@
             weight_out[e] = mask[e].astype(f32) / var[e]
             science = jnp.where(mask[e] == 0, 0.0, sci_out[e])
             top = jnp.max(jnp.abs(science), axis=(0, 1), keepdims=True)
-            _, power = lowered(top * 2.0**100, 0, 7)
-            science = science * raised(jnp.ones_like(top), 102 - power, 7)
+            scale = jnp.exp2(exponent_of(jnp.maximum(top, 2.0**-100)) - 2.0).astype(bf16).astype(f32)
+            science = science / scale
             parts = [encode_science(science), encode_weight(weight_out[e])]
             sw_out[e] = jnp.concatenate(parts, axis=0).astype(bf16)
             mine = rows[e * SLOT : (e + 1) * SLOT]
@@ -168,7 +172,6 @@
             tile = inter[e // per_owner * count + me * per_owner + e % per_owner] - me * tiles
             tile = jnp.clip(tile, 0, tiles - 1).astype(f32)
             down, across = offs[0:1, e : e + 1].astype(f32), offs[1:2, e : e + 1].astype(f32)
-            scale = raised(jnp.full_like(top, 2.0**-102), power, 7)
             spare, spot = iota(mine.shape, 0) == NPOLY, iota(mine.shape, 1)
             for lane, value in enumerate((down, across, tile, scale)):
                 mine = jnp.where(spare & (spot == lane), value, mine)
@@ -304,6 +307,7 @@
 
     def body(sci, weight, r, slabs, *refs):
         refs = list(refs)
+        ready = None if first else refs.pop(0)
         pays = [refs.pop(0) for _ in ks]
         before = [] if first else [refs.pop(0) for _ in range(2)]
         done = [refs.pop(0) for _ in carried]
@@ -312,6 +316,7 @@
         else:
             numer_out, denom_out = refs.pop(0), refs.pop(0)
             resid_outs = [refs.pop(0) for _ in range(len(ks) + first)]
+            ready_out = refs.pop(0) if first else None
         rhs, lhs, *refs = refs
         me, _ = here("epoch")
         strip, strips = here("strip")
@@ -355,42 +360,44 @@
         spot = iota((SLOT, CHUNK), 1)
         filled = (spot % sz.span < FINE) & (spot < sz.per * sz.span)
         c_units = []
-        for i in range(sz.chunks):
+        for i in range(sz.phases):
             col = (band * w + iota((8, sz.lanes), 1) - i).astype(f32)
             col = (2.0 * col + 1.0) / (w * bands) - 1.0
             c_units.append(jnp.concatenate([col] * (h // 8), axis=0))
         for slot in range(2):
-            used = sz.per * sz.span
-            if used < CHUNK:
-                rhs[slot, used:] = jnp.zeros((CHUNK - used, sz.lanes), bf16)
+            for line in range(sz.lines):
+                at = line * CHUNK + sz.per * sz.span
+                if at < (line + 1) * CHUNK:
+                    rhs[slot, at : (line + 1) * CHUNK] = jnp.zeros(((line + 1) * CHUNK - at, sz.lanes), bf16)
 
         def windows(turn, slab, scalars):
             window = rhs.at[turn % 2]
             down, across = scalars
             slab = pltpu.roll(slab, lax.rem(sz.rows + HALF - down, sz.rows), 0)[: sz.span]
             slab = pltpu.roll(slab.astype(bf16), lax.rem(sz.lanes + HALF - across, sz.lanes), 1)
-            for slot in range(sz.per):
-                moved = pltpu.roll(slab, sz.lanes - slot * sz.chunks, 1) if slot else slab
-                window[slot * sz.span : (slot + 1) * sz.span] = moved
+            for slot in range(sz.lines * sz.per):
+                moved = pltpu.roll(slab, sz.lanes - slot * sz.phases, 1) if slot else slab
+                at = slot // sz.per * CHUNK + slot % sz.per * sz.span
+                window[at : at + sz.span] = moved
 
         def band_matrix(turn, lines):
             band_rows = lhs.at[turn % 2]
-            for i in range(sz.chunks):
-                line, phase = divmod(i, sz.phases)
+            for i in range(sz.phases * sz.lines):
+                phase, line = divmod(i, sz.lines)
                 part = lines[line * SLOT : (line + 1) * SLOT]
                 if phase:
                     part = pltpu.roll(part, CHUNK - phase * FINE, 1)
                 part = jnp.where(filled, part, 0.0)
-                at = i * NPOLY * h
                 for p in range(NPOLY):
-                    band_rows[at + p * h : at + (p + 1) * h] = pltpu.roll(
+                    at = (phase * NPOLY + p) * h
+                    band_rows[at : at + h, line * CHUNK : (line + 1) * CHUNK] = pltpu.roll(
                         jnp.broadcast_to(part[p : p + 1], (h, CHUNK)), 0, 1, stride=1, stride_axis=0
                     )
 
-        def chunk_image(turn, i):
+        def chunk_image(turn, i, matrix):
             at = i * NPOLY * h
             conv = jnp.dot(
-                lhs[turn % 2, at : at + NPOLY * h].astype(bf16), rhs[turn % 2], preferred_element_type=f32
+                matrix[at : at + NPOLY * h].astype(bf16), rhs[turn % 2], preferred_element_type=f32
             )
             conv = [conv[p * h : (p + 1) * h] for p in range(NPOLY)]
             c_unit = c_units[i]
@@ -434,13 +441,14 @@
         for turn in range(0, len(jobs), 2):
             pair = list(enumerate(jobs))[turn : turn + 2]
             for at, (kind, mine, got, lines, scalars, tile, own) in pair:
-                band_matrix(at, lines)
+                if kind != "sent":
+                    band_matrix(at, lines)
             for at, (kind, mine, got, lines, scalars, tile, own) in pair:
                 windows(at, sent_slab(got) if kind == "sent" else slabs[tile].astype(f32), scalars)
             parts = [None for _ in pair]
-            for i in reversed(range(sz.chunks)):
+            for i in reversed(range(sz.phases)):
                 for slot, (at, _) in enumerate(pair):
-                    value = chunk_image(at, i)
+                    value = chunk_image(at, i, ready.at[pair[slot][1][1]] if pair[slot][1][0] == "sent" else lhs.at[at % 2])
                     value = pltpu.roll(value, sz.lanes - i, 1) if i else value
                     parts[slot] = value if parts[slot] is None else parts[slot] + value
             images += [part[:, :w] for part in parts]
@@ -473,6 +481,10 @@
                     send(sums, coadd_out)
         for copy in copies:
             copy.wait()
+        if first:
+            for e in range(count):
+                band_matrix(0, r[e].astype(f32))
+                ready_out[e] = lhs[0].astype(bf16)
 
     image = jax.ShapeDtypeStruct((per_owner, h, w), f32)
     sums = jax.ShapeDtypeStruct((tiles, h, w), f32)
@@ -480,10 +492,12 @@
         out_shape = (jax.ShapeDtypeStruct((count, h, w), f32), sums)
     else:
         out_shape = (sums, sums) + (image,) * (len(ks) + first)
+        if first:
+            out_shape += (jax.ShapeDtypeStruct((count, sz.phases * NPOLY * h, sz.depth), bf16),)
     vmem, hbm = pl.BlockSpec(memory_space=pltpu.VMEM), pl.BlockSpec(memory_space=pltpu.HBM)
     scratch = [
-        pltpu.VMEM((2, CHUNK, sz.lanes), bf16),
-        pltpu.VMEM((2, sz.chunks * NPOLY * h, CHUNK), f32),
+        pltpu.VMEM((2, sz.depth, sz.lanes), bf16),
+        pltpu.VMEM((2, sz.phases * NPOLY * h, sz.depth), f32),
     ]
     if last:
         new = len(ks) * per_owner
@@ -494,7 +508,7 @@
         ]
     return pl.pallas_call(
         body,
-        in_specs=[vmem] * (4 + len(ks) + (0 if first else 2) + len(carried)),
+        in_specs=[vmem] * (4 + len(ks) + (0 if first else 3) + len(carried)),
         out_specs=(hbm if last else vmem,) * len(out_shape),
         out_shape=out_shape,
         scratch_shapes=scratch,
@@ -557,7 +571,7 @@
         pairs = [(i, partner(i, n_epoch, k, False)) for i in range(n_epoch)]
         pays[k] = lax.ppermute(send, "epoch", pairs)
     stages = [[]] + [[k] for k in order]
-    sums, carried = [], []
+    sums, carried, ready = [], [], []
     for i, ks in enumerate(stages):
         first, last = i == 0, i == len(stages) - 1
         kept = [k for k, _ in carried] if last else []
@@ -566,6 +580,7 @@
             weight,
             r,
             slabs,
+            *ready,
             *[pays[k] for k in ks],
             *sums,
             *([value for _, value in carried] if last else []),
@@ -573,6 +588,9 @@
         if last:
             return out
         sums = list(out[:2])
+        if first:
+            *out, matrices = out
+            ready = [matrices]
         carried += list(zip(list(ks) + ([0] if first else []), out[2:]))
 
 

time: 18.1 us -> 17.7 us (0.978)
  waiting for transfers between devices: 2.8 us -> 2.4 us
    ppermute x3, waiting for transfers between devices: 2.1 us -> 1.45 us  [local(): pays[k] = lax.ppermute(send, 'epoch', pairs)]
    pallas_call x1, Pallas kernels: 2.56 us -> 2.3 us  [call(): pl.pallas_call(body, in_specs=[hbm] * 9, out_specs=(vmem,) * 5, out_shape...]
    ppermute x3, waiting for transfers between devices: 0.7 us -> 0.95 us  [surroundings(): sent[key] = lax.ppermute(block, ('strip', 'band'), pairs)]
    pallas_call x4, Pallas kernels: 4.03 us -> 4.24 us  [local(): models(sz, n_epoch, tiles, count, ks, first, last, kept)]
  transfers between devices with their start and end apart: 6 -> 6, of which waited for: 3 -> 3; matrix products, arithmetic and copies ran while one was open for 0% -> 0% of each run, Pallas kernels for 28% -> 29%
where the time goes in v8:
time: 17.7 us; the launch traced here: 17.5 us
  starting transfers between devices  7.65 us (43%)
  Pallas kernels  6.81 us (38%)
  waiting for transfers between devices  2.4 us (14%)
  between operations  0.68 us (4%)
    ppermute x3, starting transfers between devices, local(): pays[k] = lax.ppermute(send, 'epoch', pairs)  4.45 us
    pallas_call x4, Pallas kernels, local(): models(sz, n_epoch, tiles, count, ks, first, last, kept)  4.24 us
    ppermute x3, starting transfers between devices, surroundings(): sent[key] = lax.ppermute(block, ('strip', 'band'), pairs)  3.2 us
    pallas_call x1, Pallas kernels, call(): pl.pallas_call(body, in_specs=[hbm] * 9, out_specs=(vmem,) * 5, out_shape...  2.3 us
    ppermute x3, waiting for transfers between devices, local(): pays[k] = lax.ppermute(send, 'epoch', pairs)  1.45 us
    ppermute x3, waiting for transfers between devices, surroundings(): sent[key] = lax.ppermute(block, ('strip', 'band'), pairs)  0.95 us
  transfers between devices with their start and end apart: 6, of which 3 were waited for; matrix products, arithmetic and copies ran while one was open for 0% of the time, Pallas kernels for 29%

profile of v8, /device:TPU:0, one launch (start us, length us, event | category | flops | bytes accessed | tf_op | source)
XLA Modules:
  0.0 17.5 jit_solution(17558662719348383256)
XLA Ops:
  0.6 3.0 %collective-permute-start = (bf16[2,24,256]{2,1,0:T(8,128)(2,1)}, bf16[2,24,256]{2,1,0:T(8,128)(2,1)S(1)}, u32[]{:S(2)}, u32[]{:S(2)}) collective-permute-start(bf16[2,24,256]{2,1,0:T(8,128)(2,1)} %refs_0_.1), channel_id=1, source_target_pairs={{0,2},{1,3},{2,0},{3,1},{4,6},{5,7},{6,4},{7,5},{8,10},{9,11},{10,... | collective-permute-start | bytes 73736 | tf_op jit(solution)/shard_map/ppermute | solution.py:539
  3.6 0.0 collective-permute-start.2
  3.6 0.2 %collective-permute-start.1 = (bf16[2,24,256]{2,1,0:T(8,128)(2,1)}, bf16[2,24,256]{2,1,0:T(8,128)(2,1)S(1)}, u32[]{:S(2)}, u32[]{:S(2)}) collective-permute-start(bf16[2,24,256]{2,1,0:T(8,128)(2,1)} %refs_0_.1), channel_id=1, source_target_pairs={{0,1},{1,0},{2,3},{3,2},{4,5},{5,4},{6,7},{7,6},{8,9},{9,8},{10,11... | collective-permute-start | bytes 73736 | tf_op jit(solution)/shard_map/ppermute | solution.py:539
  3.8 2.3 %prepare.1 = (bf16[4,16,256]{2,1,0:T(8,128)(2,1)S(1)}, bf16[4,48,256]{2,1,0:T(8,128)(2,1)S(1)}, bf16[2,24,256]{2,1,0:T(8,128)(2,1)S(1)}, f32[4,24,256]{2,1,0:T(8,128)S(1)}, f32[4,24,256]{2,1,0:T(8,128)S(1)}) custom-call(bf16[2,24,256]{2,1,0:T(8,128)(2,1)} %refs_0_.1, f32[4,24,256]{2,1,0:T(8,128)} %refs_1_.1, f32[4,24,256]{2,1,0:T(8,128)} %refs_2_.1, ...), custom_call_target="tpu_custom_call" | custom-call | flops 1000000000 | bytes 6000000 | tf_op jit(solution)/shard_map/prepare/pallas_call | solution.py:185
  6.1 0.0 collective-permute-done.low.high
  6.2 0.9 %collective-permute-done.2.low_left.high_left.low_right.high_right = bf16[2,24,256]{2,1,0:T(8,128)(2,1)S(1)} collective-permute-done((bf16[2,24,256]{2,1,0:T(8,128)(2,1)}, bf16[2,24,256]{2,1,0:T(8,128)(2,1)S(1)}, u32[]{:S(2)}, u32[]{:S(2)}) %collective-permute-start.2) | collective-permute-done | bytes 24608 | tf_op jit(solution)/shard_map/ppermute | solution.py:539
  7.1 0.0 collective-permute-done.1.left.right
  7.1 0.3 %pack.1 = (bf16[2,56,384]{2,1,0:T(8,128)(2,1)S(1)}, bf16[1,112,256]{2,1,0:T(8,128)(2,1)S(1)}, bf16[1,112,256]{2,1,0:T(8,128)(2,1)S(1)}, bf16[1,112,256]{2,1,0:T(8,128)(2,1)S(1)}) custom-call(bf16[2,24,256]{2,1,0:T(8,128)(2,1)S(1)} %get-tuple-element.24.own, bf16[2,24,256]{2,1,0:T(8,128)(2,1)S(1)} %collective-permute-done.low.high, ...), custom_call_target="tpu_custom_call" | custom-call | flops 1000000 | bytes 1000000 | tf_op jit(solution)/shard_map/pack/pallas_call | solution.py:566
  7.4 3.7 %collective-permute-start.5 = (bf16[1,112,256]{2,1,0:T(8,128)(2,1)S(1)}, bf16[1,112,256]{2,1,0:T(8,128)(2,1)S(1)}, u32[]{:S(2)}, u32[]{:S(2)}) collective-permute-start(bf16[1,112,256]{2,1,0:T(8,128)(2,1)S(1)} %get-tuple-element.30), channel_id=1, source_target_pairs={{0,12},{4,8},{8,4},{12,0},{1,13},{5,9},{9,5},{13,1},{2,14},{6,10},... | collective-permute-start | bytes 172040 | tf_op jit(solution)/shard_map/ppermute | solution.py:572
  11.0 0.0 collective-permute-start.3
  11.0 0.8 %collective-permute-start.4 = (bf16[1,112,256]{2,1,0:T(8,128)(2,1)S(1)}, bf16[1,112,256]{2,1,0:T(8,128)(2,1)S(1)}, u32[]{:S(2)}, u32[]{:S(2)}) collective-permute-start(bf16[1,112,256]{2,1,0:T(8,128)(2,1)S(1)} %get-tuple-element.29), channel_id=1, source_target_pairs={{0,4},{4,0},{8,12},{12,8},{1,5},{5,1},{9,13},{13,9},{2,6},{6,2},{1... | collective-permute-start | bytes 172040 | tf_op jit(solution)/shard_map/ppermute | solution.py:572
  11.8 1.3 %models.4 = (f32[2,24,256]{2,1,0:T(8,128)S(1)}, f32[2,24,256]{2,1,0:T(8,128)S(1)}, f32[1,24,256]{2,1,0:T(8,128)S(1)}, bf16[4,288,512]{2,1,0:T(8,128)(2,1)S(1)}) custom-call(f32[4,24,256]{2,1,0:T(8,128)S(1)} %get-tuple-element.21.sci, f32[4,24,256]{2,1,0:T(8,128)S(1)} %get-tuple-element.22.weight, bf16[4,16,256]{2,1,0:T(8,128)(2,1)S(1)} %get-tuple-element.23.r, ...), custom_call_target="tpu_custom_call" | custom-call | flops 400000000 | bytes 1000000 | tf_op jit(solution)/shard_map/models/pallas_call | solution.py:578
  13.1 0.9 %collective-permute-done.5.refs_1_ = bf16[1,112,256]{2,1,0:T(8,128)(2,1)S(1)} collective-permute-done((bf16[1,112,256]{2,1,0:T(8,128)(2,1)S(1)}, bf16[1,112,256]{2,1,0:T(8,128)(2,1)S(1)}, u32[]{:S(2)}, u32[]{:S(2)}) %collective-permute-start.5) | collective-permute-done | bytes 57376 | tf_op jit(solution)/shard_map/ppermute | solution.py:572
  14.1 0.8 %models.5 = (f32[2,24,256]{2,1,0:T(8,128)S(1)}, f32[2,24,256]{2,1,0:T(8,128)S(1)}, f32[1,24,256]{2,1,0:T(8,128)S(1)}) custom-call(f32[4,24,256]{2,1,0:T(8,128)S(1)} %get-tuple-element.21.sci, f32[4,24,256]{2,1,0:T(8,128)S(1)} %get-tuple-element.22.weight, bf16[4,16,256]{2,1,0:T(8,128)(2,1)S(1)} %get-tuple-element.23.r, ...), custom_call_target="tpu_custom_call" | custom-call | flops 800000000 | bytes 1000000 | tf_op jit(solution)/shard_map/models/pallas_call | solution.py:578
  14.8 0.5 %collective-permute-done.4.refs_1_ = bf16[1,112,256]{2,1,0:T(8,128)(2,1)S(1)} collective-permute-done((bf16[1,112,256]{2,1,0:T(8,128)(2,1)S(1)}, bf16[1,112,256]{2,1,0:T(8,128)(2,1)S(1)}, u32[]{:S(2)}, u32[]{:S(2)}) %collective-permute-start.4) | collective-permute-done | bytes 57376 | tf_op jit(solution)/shard_map/ppermute | solution.py:572
  15.3 0.8 %models.6 = (f32[2,24,256]{2,1,0:T(8,128)S(1)}, f32[2,24,256]{2,1,0:T(8,128)S(1)}, f32[1,24,256]{2,1,0:T(8,128)S(1)}) custom-call(f32[4,24,256]{2,1,0:T(8,128)S(1)} %get-tuple-element.21.sci, f32[4,24,256]{2,1,0:T(8,128)S(1)} %get-tuple-element.22.weight, bf16[4,16,256]{2,1,0:T(8,128)(2,1)S(1)} %get-tuple-element.23.r, ...), custom_call_target="tpu_custom_call" | custom-call | flops 800000000 | bytes 1000000 | tf_op jit(solution)/shard_map/models/pallas_call | solution.py:578
  16.1 0.0 collective-permute-done.3.refs_1_
  16.1 1.4 %models.7 = (f32[4,24,256]{2,1,0:T(8,128)}, f32[2,24,256]{2,1,0:T(8,128)}) custom-call(f32[4,24,256]{2,1,0:T(8,128)S(1)} %get-tuple-element.21.sci, f32[4,24,256]{2,1,0:T(8,128)S(1)} %get-tuple-element.22.weight, bf16[4,16,256]{2,1,0:T(8,128)(2,1)S(1)} %get-tuple-element.23.r, bf16[2,56,384]{2,1,0:T(8,128)(2,1)S(1)} %get-tuple-element.26.slabs, ...), custom_call_target="tpu_custom_call" | custom-call | flops 800000000 | bytes 1000000 | tf_op jit(solution)/shard_map/models/pallas_call | solution.py:578
Async XLA Ops:
  0.6 5.5 %collective-permute-start = (bf16[2,24,256]{2,1,0:T(8,128)(2,1)}, bf16[2,24,256]{2,1,0:T(8,128)(2,1)S(1)}, u32[]{:S(2)}, u32[]{:S(2)}) collective-permute-start(bf16[2,24,256]{2,1,0:T(8,128)(2,1)} %refs_0_.1), channel_id=1, source_target_pairs={{0,2},{1,3},{2,0},{3,1},{4,6},{5,7},{6,4},{7,5},{8,10},{9,11},{10,... | collective-permute-start | bytes 73736 | tf_op jit(solution)/shard_map/ppermute | solution.py:539
  3.6 3.5 %collective-permute-start.2 = (bf16[2,24,256]{2,1,0:T(8,128)(2,1)}, bf16[2,24,256]{2,1,0:T(8,128)(2,1)S(1)}, u32[]{:S(2)}, u32[]{:S(2)}) collective-permute-start(bf16[2,24,256]{2,1,0:T(8,128)(2,1)} %refs_0_.1), channel_id=1, source_target_pairs={{0,3},{1,2},{2,1},{3,0},{4,7},{5,6},{6,5},{7,4},{8,11},{9,10},{10,... | collective-permute-start | bytes 73736 | tf_op jit(solution)/shard_map/ppermute | solution.py:539
  3.6 3.5 %collective-permute-start.1 = (bf16[2,24,256]{2,1,0:T(8,128)(2,1)}, bf16[2,24,256]{2,1,0:T(8,128)(2,1)S(1)}, u32[]{:S(2)}, u32[]{:S(2)}) collective-permute-start(bf16[2,24,256]{2,1,0:T(8,128)(2,1)} %refs_0_.1), channel_id=1, source_target_pairs={{0,1},{1,0},{2,3},{3,2},{4,5},{5,4},{6,7},{7,6},{8,9},{9,8},{10,11... | collective-permute-start | bytes 73736 | tf_op jit(solution)/shard_map/ppermute | solution.py:539
  7.4 6.7 %collective-permute-start.5 = (bf16[1,112,256]{2,1,0:T(8,128)(2,1)S(1)}, bf16[1,112,256]{2,1,0:T(8,128)(2,1)S(1)}, u32[]{:S(2)}, u32[]{:S(2)}) collective-permute-start(bf16[1,112,256]{2,1,0:T(8,128)(2,1)S(1)} %get-tuple-element.30), channel_id=1, source_target_pairs={{0,12},{4,8},{8,4},{12,0},{1,13},{5,9},{9,5},{13,1},{2,14},{6,10},... | collective-permute-start | bytes 172040 | tf_op jit(solution)/shard_map/ppermute | solution.py:572
  11.0 5.1 %collective-permute-start.3 = (bf16[1,112,256]{2,1,0:T(8,128)(2,1)S(1)}, bf16[1,112,256]{2,1,0:T(8,128)(2,1)S(1)}, u32[]{:S(2)}, u32[]{:S(2)}) collective-permute-start(bf16[1,112,256]{2,1,0:T(8,128)(2,1)S(1)} %get-tuple-element.28), channel_id=1, source_target_pairs={{0,8},{4,12},{8,0},{12,4},{1,9},{5,13},{9,1},{13,5},{2,10},{6,14},... | collective-permute-start | bytes 172040 | tf_op jit(solution)/shard_map/ppermute | solution.py:572
  11.0 4.3 %collective-permute-start.4 = (bf16[1,112,256]{2,1,0:T(8,128)(2,1)S(1)}, bf16[1,112,256]{2,1,0:T(8,128)(2,1)S(1)}, u32[]{:S(2)}, u32[]{:S(2)}) collective-permute-start(bf16[1,112,256]{2,1,0:T(8,128)(2,1)S(1)} %get-tuple-element.29), channel_id=1, source_target_pairs={{0,4},{4,0},{8,12},{12,8},{1,5},{5,1},{9,13},{13,9},{2,6},{6,2},{1... | collective-permute-start | bytes 172040 | tf_op jit(solution)/shard_map/ppermute | solution.py:572

commit v9 on v8

--- a/solution.py
+++ b/solution.py
@@ -246,39 +246,45 @@
                 parts.append(jnp.zeros((gap, below.shape[1]), f32))
             return jnp.concatenate(parts + [above], axis=0)
 
+        whole_slabs = []
         for t in range(tiles):
-            slabs[t, :, :w] = column(own, low, high, t, slice(None)).astype(bf16)
+            parts = [column(own, low, high, t, slice(None))]
             before = column(left, low_left, high_left, t, slice(w - 128, w))
             after = column(right, low_right, high_right, t, slice(0, 128))
             lane = iota(before.shape, 1)
             before = jnp.where((lane >= 128 - REACH) & (band > 0), before, 0.0)
             after = jnp.where((lane < REACH) & (band < bands - 1), after, 0.0)
             if sz.lanes - w == 128:
-                slabs[t, :, w:] = (before + after).astype(bf16)
+                parts.append(before + after)
             else:
-                slabs[t, :, w : w + 128] = after.astype(bf16)
-                slabs[t, :, sz.lanes - 128 :] = before.astype(bf16)
+                gap = sz.lanes - w - 256
+                parts += [after] + ([jnp.zeros((sz.rows, gap), f32)] if gap else []) + [before]
+            slab = jnp.concatenate(parts, axis=1)
+            slabs[t] = slab.astype(bf16)
+            if sz.one_side:
+                side = jnp.where(strip == 0, slab[h : h + 16], slab[sz.rows - 16 :])
+                slab = jnp.concatenate([slab[:h], side], axis=0)
+            whole_slabs.append(slab)
         for k, out in zip(peers, sends):
             q = partner(me, n_epoch, k, False)
             for c in range(per_owner):
                 mine = q * per_owner + c
                 lines = r[mine].astype(f32)
-                tile = lines[NPOLY, 2].astype(jnp.int32)
-                slab = slabs[tile].astype(f32)
-                if sz.one_side:
-                    side = jnp.where(strip == 0, slab[h : h + 16], slab[sz.rows - 16 :])
-                    slab = jnp.concatenate([slab[:h], side], axis=0)
-                halo = pltpu.roll(slab[:, sz.lanes - 128 :], REACH, 1)
+                covered = lines[NPOLY : NPOLY + 1, 2:3]
+                slab = whole_slabs[0]
+                for t in range(1, tiles):
+                    pick = jnp.broadcast_to(covered, slab.shape) == t
+                    slab = jnp.where(pick, whole_slabs[t], slab)
+                halo = slab[:, sz.lanes - 128 :]
                 if sz.lanes - w != 128:
-                    halo = halo + pltpu.roll(slab[:, w : w + 128], REACH, 1)
-                halo = jnp.where(iota(halo.shape, 1) < 32, halo, 0.0)
+                    halo = halo + slab[:, w : w + 128]
                 bits = []
                 for part in range(sz.halo_rows // 8 * (w // 128)):
                     piece = jnp.zeros((8, 128), f32)
                     for slot in range(4):
                         g = part * 4 + slot
                         if g < sz.groups:
-                            piece = piece + pltpu.roll(halo[g * 8 : g * 8 + 8], slot * 32, 1)
+                            piece = piece + pltpu.roll(halo[g * 8 : g * 8 + 8], slot * 32 + REACH, 1)
                     bits.append(piece)
                 wide = w // 128
                 bits = [
@@ -415,10 +421,10 @@
                 part, slot = g // 4, g % 4
                 line, side = part // wide, part % wide
                 piece = halo[line * 8 : line * 8 + 8, side * 128 : side * 128 + 128]
-                bits.append(pltpu.roll(piece, (128 - slot * 32) % 128, 1))
+                bits.append(pltpu.roll(piece, (256 - slot * 32 - REACH) % 128, 1))
             halo = jnp.concatenate(bits, axis=0)
             lane = iota(halo.shape, 1)
-            halo = pltpu.roll(jnp.where(lane < 2 * REACH, halo, 0.0), 128 - REACH, 1)
+            halo = jnp.where((lane < REACH) | (lane >= 128 - REACH), halo, 0.0)
             if sz.lanes - w != 128:
                 gap = sz.lanes - w - 256
                 pieces = [jnp.where(lane < 64, halo, 0.0)]

time: 17.7 us -> 17.6 us (level)
  no operation moved by 1% of the time
where the time goes in v9:
time: 17.6 us; the launch traced here: 17.5 us
  starting transfers between devices  7.65 us (43%)
  Pallas kernels  6.72 us (38%)
  waiting for transfers between devices  2.41 us (14%)
  between operations  0.69 us (4%)
    ppermute x3, starting transfers between devices, local(): pays[k] = lax.ppermute(send, 'epoch', pairs)  4.45 us
    pallas_call x4, Pallas kernels, local(): models(sz, n_epoch, tiles, count, ks, first, last, kept)  4.22 us
    ppermute x3, starting transfers between devices, surroundings(): sent[key] = lax.ppermute(block, ('strip', 'band'), pairs)  3.2 us
    pallas_call x1, Pallas kernels, call(): pl.pallas_call(body, in_specs=[hbm] * 9, out_specs=(vmem,) * 5, out_shape...  2.3 us
    ppermute x3, waiting for transfers between devices, local(): pays[k] = lax.ppermute(send, 'epoch', pairs)  1.46 us
    ppermute x3, waiting for transfers between devices, surroundings(): sent[key] = lax.ppermute(block, ('strip', 'band'), pairs)  0.95 us
  transfers between devices with their start and end apart: 6, of which 3 were waited for; matrix products, arithmetic and copies ran while one was open for 0% of the time, Pallas kernels for 29%

profile of v9, /device:TPU:0, one launch (start us, length us, event | category | flops | bytes accessed | tf_op | source)
XLA Modules:
  0.0 17.5 jit_solution(12811697675747526015)
XLA Ops:
  0.6 3.0 %collective-permute-start = (bf16[2,24,256]{2,1,0:T(8,128)(2,1)}, bf16[2,24,256]{2,1,0:T(8,128)(2,1)S(1)}, u32[]{:S(2)}, u32[]{:S(2)}) collective-permute-start(bf16[2,24,256]{2,1,0:T(8,128)(2,1)} %refs_0_.1), channel_id=1, source_target_pairs={{0,2},{1,3},{2,0},{3,1},{4,6},{5,7},{6,4},{7,5},{8,10},{9,11},{10,... | collective-permute-start | bytes 73736 | tf_op jit(solution)/shard_map/ppermute | solution.py:545
  3.6 0.0 collective-permute-start.2
  3.6 0.2 %collective-permute-start.1 = (bf16[2,24,256]{2,1,0:T(8,128)(2,1)}, bf16[2,24,256]{2,1,0:T(8,128)(2,1)S(1)}, u32[]{:S(2)}, u32[]{:S(2)}) collective-permute-start(bf16[2,24,256]{2,1,0:T(8,128)(2,1)} %refs_0_.1), channel_id=1, source_target_pairs={{0,1},{1,0},{2,3},{3,2},{4,5},{5,4},{6,7},{7,6},{8,9},{9,8},{10,11... | collective-permute-start | bytes 73736 | tf_op jit(solution)/shard_map/ppermute | solution.py:545
  3.8 2.3 %prepare.1 = (bf16[4,16,256]{2,1,0:T(8,128)(2,1)S(1)}, bf16[4,48,256]{2,1,0:T(8,128)(2,1)S(1)}, bf16[2,24,256]{2,1,0:T(8,128)(2,1)S(1)}, f32[4,24,256]{2,1,0:T(8,128)S(1)}, f32[4,24,256]{2,1,0:T(8,128)S(1)}) custom-call(bf16[2,24,256]{2,1,0:T(8,128)(2,1)} %refs_0_.1, f32[4,24,256]{2,1,0:T(8,128)} %refs_1_.1, f32[4,24,256]{2,1,0:T(8,128)} %refs_2_.1, ...), custom_call_target="tpu_custom_call" | custom-call | flops 1000000000 | bytes 6000000 | tf_op jit(solution)/shard_map/prepare/pallas_call | solution.py:185
  6.1 0.0 collective-permute-done.low.high
  6.2 0.9 %collective-permute-done.2.low_left.high_left.low_right.high_right = bf16[2,24,256]{2,1,0:T(8,128)(2,1)S(1)} collective-permute-done((bf16[2,24,256]{2,1,0:T(8,128)(2,1)}, bf16[2,24,256]{2,1,0:T(8,128)(2,1)S(1)}, u32[]{:S(2)}, u32[]{:S(2)}) %collective-permute-start.2) | collective-permute-done | bytes 24608 | tf_op jit(solution)/shard_map/ppermute | solution.py:545
  7.1 0.0 collective-permute-done.1.left.right
  7.1 0.2 %pack.1 = (bf16[2,56,384]{2,1,0:T(8,128)(2,1)S(1)}, bf16[1,112,256]{2,1,0:T(8,128)(2,1)S(1)}, bf16[1,112,256]{2,1,0:T(8,128)(2,1)S(1)}, bf16[1,112,256]{2,1,0:T(8,128)(2,1)S(1)}) custom-call(bf16[2,24,256]{2,1,0:T(8,128)(2,1)S(1)} %get-tuple-element.24.own, bf16[2,24,256]{2,1,0:T(8,128)(2,1)S(1)} %collective-permute-done.low.high, ...), custom_call_target="tpu_custom_call" | custom-call | flops 1000000 | bytes 1000000 | tf_op jit(solution)/shard_map/pack/pallas_call | solution.py:572
  7.3 3.7 %collective-permute-start.5 = (bf16[1,112,256]{2,1,0:T(8,128)(2,1)S(1)}, bf16[1,112,256]{2,1,0:T(8,128)(2,1)S(1)}, u32[]{:S(2)}, u32[]{:S(2)}) collective-permute-start(bf16[1,112,256]{2,1,0:T(8,128)(2,1)S(1)} %get-tuple-element.30), channel_id=1, source_target_pairs={{0,12},{4,8},{8,4},{12,0},{1,13},{5,9},{9,5},{13,1},{2,14},{6,10},... | collective-permute-start | bytes 172040 | tf_op jit(solution)/shard_map/ppermute | solution.py:578
  11.0 0.0 collective-permute-start.3
  11.0 0.8 %collective-permute-start.4 = (bf16[1,112,256]{2,1,0:T(8,128)(2,1)S(1)}, bf16[1,112,256]{2,1,0:T(8,128)(2,1)S(1)}, u32[]{:S(2)}, u32[]{:S(2)}) collective-permute-start(bf16[1,112,256]{2,1,0:T(8,128)(2,1)S(1)} %get-tuple-element.29), channel_id=1, source_target_pairs={{0,4},{4,0},{8,12},{12,8},{1,5},{5,1},{9,13},{13,9},{2,6},{6,2},{1... | collective-permute-start | bytes 172040 | tf_op jit(solution)/shard_map/ppermute | solution.py:578
  11.8 1.3 %models.4 = (f32[2,24,256]{2,1,0:T(8,128)S(1)}, f32[2,24,256]{2,1,0:T(8,128)S(1)}, f32[1,24,256]{2,1,0:T(8,128)S(1)}, bf16[4,288,512]{2,1,0:T(8,128)(2,1)S(1)}) custom-call(f32[4,24,256]{2,1,0:T(8,128)S(1)} %get-tuple-element.21.sci, f32[4,24,256]{2,1,0:T(8,128)S(1)} %get-tuple-element.22.weight, bf16[4,16,256]{2,1,0:T(8,128)(2,1)S(1)} %get-tuple-element.23.r, ...), custom_call_target="tpu_custom_call" | custom-call | flops 400000000 | bytes 1000000 | tf_op jit(solution)/shard_map/models/pallas_call | solution.py:584
  13.1 0.9 %collective-permute-done.5.refs_1_ = bf16[1,112,256]{2,1,0:T(8,128)(2,1)S(1)} collective-permute-done((bf16[1,112,256]{2,1,0:T(8,128)(2,1)S(1)}, bf16[1,112,256]{2,1,0:T(8,128)(2,1)S(1)}, u32[]{:S(2)}, u32[]{:S(2)}) %collective-permute-start.5) | collective-permute-done | bytes 57376 | tf_op jit(solution)/shard_map/ppermute | solution.py:578
  14.0 0.8 %models.5 = (f32[2,24,256]{2,1,0:T(8,128)S(1)}, f32[2,24,256]{2,1,0:T(8,128)S(1)}, f32[1,24,256]{2,1,0:T(8,128)S(1)}) custom-call(f32[4,24,256]{2,1,0:T(8,128)S(1)} %get-tuple-element.21.sci, f32[4,24,256]{2,1,0:T(8,128)S(1)} %get-tuple-element.22.weight, bf16[4,16,256]{2,1,0:T(8,128)(2,1)S(1)} %get-tuple-element.23.r, ...), custom_call_target="tpu_custom_call" | custom-call | flops 800000000 | bytes 1000000 | tf_op jit(solution)/shard_map/models/pallas_call | solution.py:584
  14.8 0.5 %collective-permute-done.4.refs_1_ = bf16[1,112,256]{2,1,0:T(8,128)(2,1)S(1)} collective-permute-done((bf16[1,112,256]{2,1,0:T(8,128)(2,1)S(1)}, bf16[1,112,256]{2,1,0:T(8,128)(2,1)S(1)}, u32[]{:S(2)}, u32[]{:S(2)}) %collective-permute-start.4) | collective-permute-done | bytes 57376 | tf_op jit(solution)/shard_map/ppermute | solution.py:578
  15.2 0.8 %models.6 = (f32[2,24,256]{2,1,0:T(8,128)S(1)}, f32[2,24,256]{2,1,0:T(8,128)S(1)}, f32[1,24,256]{2,1,0:T(8,128)S(1)}) custom-call(f32[4,24,256]{2,1,0:T(8,128)S(1)} %get-tuple-element.21.sci, f32[4,24,256]{2,1,0:T(8,128)S(1)} %get-tuple-element.22.weight, bf16[4,16,256]{2,1,0:T(8,128)(2,1)S(1)} %get-tuple-element.23.r, ...), custom_call_target="tpu_custom_call" | custom-call | flops 800000000 | bytes 1000000 | tf_op jit(solution)/shard_map/models/pallas_call | solution.py:584
  16.0 0.0 collective-permute-done.3.refs_1_
  16.0 1.4 %models.7 = (f32[4,24,256]{2,1,0:T(8,128)}, f32[2,24,256]{2,1,0:T(8,128)}) custom-call(f32[4,24,256]{2,1,0:T(8,128)S(1)} %get-tuple-element.21.sci, f32[4,24,256]{2,1,0:T(8,128)S(1)} %get-tuple-element.22.weight, bf16[4,16,256]{2,1,0:T(8,128)(2,1)S(1)} %get-tuple-element.23.r, bf16[2,56,384]{2,1,0:T(8,128)(2,1)S(1)} %get-tuple-element.26.slabs, ...), custom_call_target="tpu_custom_call" | custom-call | flops 800000000 | bytes 1000000 | tf_op jit(solution)/shard_map/models/pallas_call | solution.py:584
Async XLA Ops:
  0.6 5.5 %collective-permute-start = (bf16[2,24,256]{2,1,0:T(8,128)(2,1)}, bf16[2,24,256]{2,1,0:T(8,128)(2,1)S(1)}, u32[]{:S(2)}, u32[]{:S(2)}) collective-permute-start(bf16[2,24,256]{2,1,0:T(8,128)(2,1)} %refs_0_.1), channel_id=1, source_target_pairs={{0,2},{1,3},{2,0},{3,1},{4,6},{5,7},{6,4},{7,5},{8,10},{9,11},{10,... | collective-permute-start | bytes 73736 | tf_op jit(solution)/shard_map/ppermute | solution.py:545
  3.6 3.5 %collective-permute-start.2 = (bf16[2,24,256]{2,1,0:T(8,128)(2,1)}, bf16[2,24,256]{2,1,0:T(8,128)(2,1)S(1)}, u32[]{:S(2)}, u32[]{:S(2)}) collective-permute-start(bf16[2,24,256]{2,1,0:T(8,128)(2,1)} %refs_0_.1), channel_id=1, source_target_pairs={{0,3},{1,2},{2,1},{3,0},{4,7},{5,6},{6,5},{7,4},{8,11},{9,10},{10,... | collective-permute-start | bytes 73736 | tf_op jit(solution)/shard_map/ppermute | solution.py:545
  3.6 3.5 %collective-permute-start.1 = (bf16[2,24,256]{2,1,0:T(8,128)(2,1)}, bf16[2,24,256]{2,1,0:T(8,128)(2,1)S(1)}, u32[]{:S(2)}, u32[]{:S(2)}) collective-permute-start(bf16[2,24,256]{2,1,0:T(8,128)(2,1)} %refs_0_.1), channel_id=1, source_target_pairs={{0,1},{1,0},{2,3},{3,2},{4,5},{5,4},{6,7},{7,6},{8,9},{9,8},{10,11... | collective-permute-start | bytes 73736 | tf_op jit(solution)/shard_map/ppermute | solution.py:545
  7.3 6.7 %collective-permute-start.5 = (bf16[1,112,256]{2,1,0:T(8,128)(2,1)S(1)}, bf16[1,112,256]{2,1,0:T(8,128)(2,1)S(1)}, u32[]{:S(2)}, u32[]{:S(2)}) collective-permute-start(bf16[1,112,256]{2,1,0:T(8,128)(2,1)S(1)} %get-tuple-element.30), channel_id=1, source_target_pairs={{0,12},{4,8},{8,4},{12,0},{1,13},{5,9},{9,5},{13,1},{2,14},{6,10},... | collective-permute-start | bytes 172040 | tf_op jit(solution)/shard_map/ppermute | solution.py:578
  11.0 5.1 %collective-permute-start.3 = (bf16[1,112,256]{2,1,0:T(8,128)(2,1)S(1)}, bf16[1,112,256]{2,1,0:T(8,128)(2,1)S(1)}, u32[]{:S(2)}, u32[]{:S(2)}) collective-permute-start(bf16[1,112,256]{2,1,0:T(8,128)(2,1)S(1)} %get-tuple-element.28), channel_id=1, source_target_pairs={{0,8},{4,12},{8,0},{12,4},{1,9},{5,13},{9,1},{13,5},{2,10},{6,14},... | collective-permute-start | bytes 172040 | tf_op jit(solution)/shard_map/ppermute | solution.py:578
  11.0 4.3 %collective-permute-start.4 = (bf16[1,112,256]{2,1,0:T(8,128)(2,1)S(1)}, bf16[1,112,256]{2,1,0:T(8,128)(2,1)S(1)}, u32[]{:S(2)}, u32[]{:S(2)}) collective-permute-start(bf16[1,112,256]{2,1,0:T(8,128)(2,1)S(1)} %get-tuple-element.29), channel_id=1, source_target_pairs={{0,4},{4,0},{8,12},{12,8},{1,5},{5,1},{9,13},{13,9},{2,6},{6,2},{1... | collective-permute-start | bytes 172040 | tf_op jit(solution)/shard_map/ppermute | solution.py:578

commit v10 on v9

--- a/solution.py
+++ b/solution.py
@@ -573,7 +573,7 @@
         *[around[down, across] for across in (0, -1, 1) for down in (0, -1, 1)], sw, r
     )
     pays = {}
-    for k, send in zip(order, [sends[peers.index(k)] for k in order]):
+    for k, send in reversed(list(zip(peers, sends))):
         pairs = [(i, partner(i, n_epoch, k, False)) for i in range(n_epoch)]
         pays[k] = lax.ppermute(send, "epoch", pairs)
     stages = [[]] + [[k] for k in order]

time: 17.6 us -> 17.6 us (level)
  no operation moved by 1% of the time
where the time goes in v10:
time: 17.6 us; the launch traced here: 17.5 us
  starting transfers between devices  7.65 us (43%)
  Pallas kernels  6.72 us (38%)
  waiting for transfers between devices  2.41 us (14%)
  between operations  0.69 us (4%)
    ppermute x3, starting transfers between devices, local(): pays[k] = lax.ppermute(send, 'epoch', pairs)  4.45 us
    pallas_call x4, Pallas kernels, local(): models(sz, n_epoch, tiles, count, ks, first, last, kept)  4.22 us
    ppermute x3, starting transfers between devices, surroundings(): sent[key] = lax.ppermute(block, ('strip', 'band'), pairs)  3.2 us
    pallas_call x1, Pallas kernels, call(): pl.pallas_call(body, in_specs=[hbm] * 9, out_specs=(vmem,) * 5, out_shape...  2.3 us
    ppermute x3, waiting for transfers between devices, local(): pays[k] = lax.ppermute(send, 'epoch', pairs)  1.46 us
    ppermute x3, waiting for transfers between devices, surroundings(): sent[key] = lax.ppermute(block, ('strip', 'band'), pairs)  0.95 us
  transfers between devices with their start and end apart: 6, of which 3 were waited for; matrix products, arithmetic and copies ran while one was open for 0% of the time, Pallas kernels for 29%

profile of v10, /device:TPU:0, one launch (start us, length us, event | category | flops | bytes accessed | tf_op | source)
XLA Modules:
  0.0 17.5 jit_solution(12811697675747526015)
XLA Ops:
  0.6 3.0 %collective-permute-start = (bf16[2,24,256]{2,1,0:T(8,128)(2,1)}, bf16[2,24,256]{2,1,0:T(8,128)(2,1)S(1)}, u32[]{:S(2)}, u32[]{:S(2)}) collective-permute-start(bf16[2,24,256]{2,1,0:T(8,128)(2,1)} %refs_0_.1), channel_id=1, source_target_pairs={{0,2},{1,3},{2,0},{3,1},{4,6},{5,7},{6,4},{7,5},{8,10},{9,11},{10,... | collective-permute-start | bytes 73736 | tf_op jit(solution)/shard_map/ppermute | solution.py:545
  3.6 0.0 collective-permute-start.2
  3.6 0.2 %collective-permute-start.1 = (bf16[2,24,256]{2,1,0:T(8,128)(2,1)}, bf16[2,24,256]{2,1,0:T(8,128)(2,1)S(1)}, u32[]{:S(2)}, u32[]{:S(2)}) collective-permute-start(bf16[2,24,256]{2,1,0:T(8,128)(2,1)} %refs_0_.1), channel_id=1, source_target_pairs={{0,1},{1,0},{2,3},{3,2},{4,5},{5,4},{6,7},{7,6},{8,9},{9,8},{10,11... | collective-permute-start | bytes 73736 | tf_op jit(solution)/shard_map/ppermute | solution.py:545
  3.8 2.3 %prepare.1 = (bf16[4,16,256]{2,1,0:T(8,128)(2,1)S(1)}, bf16[4,48,256]{2,1,0:T(8,128)(2,1)S(1)}, bf16[2,24,256]{2,1,0:T(8,128)(2,1)S(1)}, f32[4,24,256]{2,1,0:T(8,128)S(1)}, f32[4,24,256]{2,1,0:T(8,128)S(1)}) custom-call(bf16[2,24,256]{2,1,0:T(8,128)(2,1)} %refs_0_.1, f32[4,24,256]{2,1,0:T(8,128)} %refs_1_.1, f32[4,24,256]{2,1,0:T(8,128)} %refs_2_.1, ...), custom_call_target="tpu_custom_call" | custom-call | flops 1000000000 | bytes 6000000 | tf_op jit(solution)/shard_map/prepare/pallas_call | solution.py:185
  6.1 0.0 collective-permute-done.low.high
  6.2 0.9 %collective-permute-done.2.low_left.high_left.low_right.high_right = bf16[2,24,256]{2,1,0:T(8,128)(2,1)S(1)} collective-permute-done((bf16[2,24,256]{2,1,0:T(8,128)(2,1)}, bf16[2,24,256]{2,1,0:T(8,128)(2,1)S(1)}, u32[]{:S(2)}, u32[]{:S(2)}) %collective-permute-start.2) | collective-permute-done | bytes 24608 | tf_op jit(solution)/shard_map/ppermute | solution.py:545
  7.1 0.0 collective-permute-done.1.left.right
  7.1 0.2 %pack.1 = (bf16[2,56,384]{2,1,0:T(8,128)(2,1)S(1)}, bf16[1,112,256]{2,1,0:T(8,128)(2,1)S(1)}, bf16[1,112,256]{2,1,0:T(8,128)(2,1)S(1)}, bf16[1,112,256]{2,1,0:T(8,128)(2,1)S(1)}) custom-call(bf16[2,24,256]{2,1,0:T(8,128)(2,1)S(1)} %get-tuple-element.24.own, bf16[2,24,256]{2,1,0:T(8,128)(2,1)S(1)} %collective-permute-done.low.high, ...), custom_call_target="tpu_custom_call" | custom-call | flops 1000000 | bytes 1000000 | tf_op jit(solution)/shard_map/pack/pallas_call | solution.py:572
  7.3 3.7 %collective-permute-start.5 = (bf16[1,112,256]{2,1,0:T(8,128)(2,1)S(1)}, bf16[1,112,256]{2,1,0:T(8,128)(2,1)S(1)}, u32[]{:S(2)}, u32[]{:S(2)}) collective-permute-start(bf16[1,112,256]{2,1,0:T(8,128)(2,1)S(1)} %get-tuple-element.30), channel_id=1, source_target_pairs={{0,12},{4,8},{8,4},{12,0},{1,13},{5,9},{9,5},{13,1},{2,14},{6,10},... | collective-permute-start | bytes 172040 | tf_op jit(solution)/shard_map/ppermute | solution.py:578
  11.0 0.0 collective-permute-start.3
  11.0 0.8 %collective-permute-start.4 = (bf16[1,112,256]{2,1,0:T(8,128)(2,1)S(1)}, bf16[1,112,256]{2,1,0:T(8,128)(2,1)S(1)}, u32[]{:S(2)}, u32[]{:S(2)}) collective-permute-start(bf16[1,112,256]{2,1,0:T(8,128)(2,1)S(1)} %get-tuple-element.29), channel_id=1, source_target_pairs={{0,4},{4,0},{8,12},{12,8},{1,5},{5,1},{9,13},{13,9},{2,6},{6,2},{1... | collective-permute-start | bytes 172040 | tf_op jit(solution)/shard_map/ppermute | solution.py:578
  11.8 1.3 %models.4 = (f32[2,24,256]{2,1,0:T(8,128)S(1)}, f32[2,24,256]{2,1,0:T(8,128)S(1)}, f32[1,24,256]{2,1,0:T(8,128)S(1)}, bf16[4,288,512]{2,1,0:T(8,128)(2,1)S(1)}) custom-call(f32[4,24,256]{2,1,0:T(8,128)S(1)} %get-tuple-element.21.sci, f32[4,24,256]{2,1,0:T(8,128)S(1)} %get-tuple-element.22.weight, bf16[4,16,256]{2,1,0:T(8,128)(2,1)S(1)} %get-tuple-element.23.r, ...), custom_call_target="tpu_custom_call" | custom-call | flops 400000000 | bytes 1000000 | tf_op jit(solution)/shard_map/models/pallas_call | solution.py:584
  13.1 0.9 %collective-permute-done.5.refs_1_ = bf16[1,112,256]{2,1,0:T(8,128)(2,1)S(1)} collective-permute-done((bf16[1,112,256]{2,1,0:T(8,128)(2,1)S(1)}, bf16[1,112,256]{2,1,0:T(8,128)(2,1)S(1)}, u32[]{:S(2)}, u32[]{:S(2)}) %collective-permute-start.5) | collective-permute-done | bytes 57376 | tf_op jit(solution)/shard_map/ppermute | solution.py:578
  14.0 0.8 %models.5 = (f32[2,24,256]{2,1,0:T(8,128)S(1)}, f32[2,24,256]{2,1,0:T(8,128)S(1)}, f32[1,24,256]{2,1,0:T(8,128)S(1)}) custom-call(f32[4,24,256]{2,1,0:T(8,128)S(1)} %get-tuple-element.21.sci, f32[4,24,256]{2,1,0:T(8,128)S(1)} %get-tuple-element.22.weight, bf16[4,16,256]{2,1,0:T(8,128)(2,1)S(1)} %get-tuple-element.23.r, ...), custom_call_target="tpu_custom_call" | custom-call | flops 800000000 | bytes 1000000 | tf_op jit(solution)/shard_map/models/pallas_call | solution.py:584
  14.8 0.5 %collective-permute-done.4.refs_1_ = bf16[1,112,256]{2,1,0:T(8,128)(2,1)S(1)} collective-permute-done((bf16[1,112,256]{2,1,0:T(8,128)(2,1)S(1)}, bf16[1,112,256]{2,1,0:T(8,128)(2,1)S(1)}, u32[]{:S(2)}, u32[]{:S(2)}) %collective-permute-start.4) | collective-permute-done | bytes 57376 | tf_op jit(solution)/shard_map/ppermute | solution.py:578
  15.2 0.8 %models.6 = (f32[2,24,256]{2,1,0:T(8,128)S(1)}, f32[2,24,256]{2,1,0:T(8,128)S(1)}, f32[1,24,256]{2,1,0:T(8,128)S(1)}) custom-call(f32[4,24,256]{2,1,0:T(8,128)S(1)} %get-tuple-element.21.sci, f32[4,24,256]{2,1,0:T(8,128)S(1)} %get-tuple-element.22.weight, bf16[4,16,256]{2,1,0:T(8,128)(2,1)S(1)} %get-tuple-element.23.r, ...), custom_call_target="tpu_custom_call" | custom-call | flops 800000000 | bytes 1000000 | tf_op jit(solution)/shard_map/models/pallas_call | solution.py:584
  16.0 0.0 collective-permute-done.3.refs_1_
  16.0 1.4 %models.7 = (f32[4,24,256]{2,1,0:T(8,128)}, f32[2,24,256]{2,1,0:T(8,128)}) custom-call(f32[4,24,256]{2,1,0:T(8,128)S(1)} %get-tuple-element.21.sci, f32[4,24,256]{2,1,0:T(8,128)S(1)} %get-tuple-element.22.weight, bf16[4,16,256]{2,1,0:T(8,128)(2,1)S(1)} %get-tuple-element.23.r, bf16[2,56,384]{2,1,0:T(8,128)(2,1)S(1)} %get-tuple-element.26.slabs, ...), custom_call_target="tpu_custom_call" | custom-call | flops 800000000 | bytes 1000000 | tf_op jit(solution)/shard_map/models/pallas_call | solution.py:584
Async XLA Ops:
  0.6 5.5 %collective-permute-start = (bf16[2,24,256]{2,1,0:T(8,128)(2,1)}, bf16[2,24,256]{2,1,0:T(8,128)(2,1)S(1)}, u32[]{:S(2)}, u32[]{:S(2)}) collective-permute-start(bf16[2,24,256]{2,1,0:T(8,128)(2,1)} %refs_0_.1), channel_id=1, source_target_pairs={{0,2},{1,3},{2,0},{3,1},{4,6},{5,7},{6,4},{7,5},{8,10},{9,11},{10,... | collective-permute-start | bytes 73736 | tf_op jit(solution)/shard_map/ppermute | solution.py:545
  3.6 3.5 %collective-permute-start.2 = (bf16[2,24,256]{2,1,0:T(8,128)(2,1)}, bf16[2,24,256]{2,1,0:T(8,128)(2,1)S(1)}, u32[]{:S(2)}, u32[]{:S(2)}) collective-permute-start(bf16[2,24,256]{2,1,0:T(8,128)(2,1)} %refs_0_.1), channel_id=1, source_target_pairs={{0,3},{1,2},{2,1},{3,0},{4,7},{5,6},{6,5},{7,4},{8,11},{9,10},{10,... | collective-permute-start | bytes 73736 | tf_op jit(solution)/shard_map/ppermute | solution.py:545
  3.6 3.5 %collective-permute-start.1 = (bf16[2,24,256]{2,1,0:T(8,128)(2,1)}, bf16[2,24,256]{2,1,0:T(8,128)(2,1)S(1)}, u32[]{:S(2)}, u32[]{:S(2)}) collective-permute-start(bf16[2,24,256]{2,1,0:T(8,128)(2,1)} %refs_0_.1), channel_id=1, source_target_pairs={{0,1},{1,0},{2,3},{3,2},{4,5},{5,4},{6,7},{7,6},{8,9},{9,8},{10,11... | collective-permute-start | bytes 73736 | tf_op jit(solution)/shard_map/ppermute | solution.py:545
  7.3 6.7 %collective-permute-start.5 = (bf16[1,112,256]{2,1,0:T(8,128)(2,1)S(1)}, bf16[1,112,256]{2,1,0:T(8,128)(2,1)S(1)}, u32[]{:S(2)}, u32[]{:S(2)}) collective-permute-start(bf16[1,112,256]{2,1,0:T(8,128)(2,1)S(1)} %get-tuple-element.30), channel_id=1, source_target_pairs={{0,12},{4,8},{8,4},{12,0},{1,13},{5,9},{9,5},{13,1},{2,14},{6,10},... | collective-permute-start | bytes 172040 | tf_op jit(solution)/shard_map/ppermute | solution.py:578
  11.0 5.1 %collective-permute-start.3 = (bf16[1,112,256]{2,1,0:T(8,128)(2,1)S(1)}, bf16[1,112,256]{2,1,0:T(8,128)(2,1)S(1)}, u32[]{:S(2)}, u32[]{:S(2)}) collective-permute-start(bf16[1,112,256]{2,1,0:T(8,128)(2,1)S(1)} %get-tuple-element.28), channel_id=1, source_target_pairs={{0,8},{4,12},{8,0},{12,4},{1,9},{5,13},{9,1},{13,5},{2,10},{6,14},... | collective-permute-start | bytes 172040 | tf_op jit(solution)/shard_map/ppermute | solution.py:578
  11.0 4.3 %collective-permute-start.4 = (bf16[1,112,256]{2,1,0:T(8,128)(2,1)S(1)}, bf16[1,112,256]{2,1,0:T(8,128)(2,1)S(1)}, u32[]{:S(2)}, u32[]{:S(2)}) collective-permute-start(bf16[1,112,256]{2,1,0:T(8,128)(2,1)S(1)} %get-tuple-element.29), channel_id=1, source_target_pairs={{0,4},{4,0},{8,12},{12,8},{1,5},{5,1},{9,13},{13,9},{2,6},{6,2},{1... | collective-permute-start | bytes 172040 | tf_op jit(solution)/shard_map/ppermute | solution.py:578

commit v11 on v10

--- a/solution.py
+++ b/solution.py
@@ -362,7 +362,7 @@
 
         row = (strip * h + iota((h, 128), 0)).astype(f32)
         r_unit = (2.0 * row + 1.0) / (h * strips) - 1.0
-        r_unit = jnp.concatenate([r_unit] * (sz.lanes // 128), axis=1)
+        r_units = jnp.concatenate([r_unit] * (sz.lanes // 128), axis=1)
         spot = iota((SLOT, CHUNK), 1)
         filled = (spot % sz.span < FINE) & (spot < sz.per * sz.span)
         c_units = []
@@ -402,11 +402,14 @@
 
         def chunk_image(turn, i, matrix):
             at = i * NPOLY * h
+            wide = sz.lanes if i else w
             conv = jnp.dot(
-                matrix[at : at + NPOLY * h].astype(bf16), rhs[turn % 2], preferred_element_type=f32
+                matrix[at : at + NPOLY * h].astype(bf16),
+                rhs[turn % 2, :, :wide],
+                preferred_element_type=f32,
             )
             conv = [conv[p * h : (p + 1) * h] for p in range(NPOLY)]
-            c_unit = c_units[i]
+            c_unit, r_unit = c_units[i][:, :wide], r_units[:, :wide]
             return (
                 conv[0]
                 + r_unit * (conv[1] + r_unit * conv[3] + c_unit * conv[4])
@@ -455,9 +458,9 @@
             for i in reversed(range(sz.phases)):
                 for slot, (at, _) in enumerate(pair):
                     value = chunk_image(at, i, ready.at[pair[slot][1][1]] if pair[slot][1][0] == "sent" else lhs.at[at % 2])
-                    value = pltpu.roll(value, sz.lanes - i, 1) if i else value
+                    value = pltpu.roll(value, sz.lanes - i, 1)[:, :w] if i else value
                     parts[slot] = value if parts[slot] is None else parts[slot] + value
-            images += [part[:, :w] for part in parts]
+            images += parts
         for turn, (kind, mine, got, lines, scalars, tile, own) in enumerate(jobs):
             image = images[turn]
             if kind == "owned":
@@ -481,10 +484,9 @@
                 for t in range(tiles):
                     if last:
                         sums[t] = numer[t] / (denom[t] + 1.0)
+                        send(sums.at[t], coadd_out.at[t])
                     else:
                         numer_out[t], denom_out[t] = numer[t], denom[t]
-                if last:
-                    send(sums, coadd_out)
         for copy in copies:
             copy.wait()
         if first:
@@ -510,7 +512,7 @@
         scratch += [
             pltpu.VMEM((new, h, w), f32),
             pltpu.VMEM((tiles, h, w), f32),
-            pltpu.SemaphoreType.DMA((len(carried) + new + 1,)),
+            pltpu.SemaphoreType.DMA((len(carried) + new + tiles,)),
         ]
     return pl.pallas_call(
         body,

time: 17.6 us -> 17.6 us (level)
  no operation moved by 1% of the time
where the time goes in v11:
time: 17.6 us; the launch traced here: 17.5 us
  starting transfers between devices  7.65 us (43%)
  Pallas kernels  6.73 us (38%)
  waiting for transfers between devices  2.41 us (14%)
  between operations  0.69 us (4%)
    ppermute x3, starting transfers between devices, local(): pays[k] = lax.ppermute(send, 'epoch', pairs)  4.45 us
    pallas_call x4, Pallas kernels, local(): models(sz, n_epoch, tiles, count, ks, first, last, kept)  4.24 us
    ppermute x3, starting transfers between devices, surroundings(): sent[key] = lax.ppermute(block, ('strip', 'band'), pairs)  3.2 us
    pallas_call x1, Pallas kernels, call(): pl.pallas_call(body, in_specs=[hbm] * 9, out_specs=(vmem,) * 5, out_shape...  2.3 us
    ppermute x3, waiting for transfers between devices, local(): pays[k] = lax.ppermute(send, 'epoch', pairs)  1.45 us
    ppermute x3, waiting for transfers between devices, surroundings(): sent[key] = lax.ppermute(block, ('strip', 'band'), pairs)  0.95 us
  transfers between devices with their start and end apart: 6, of which 3 were waited for; matrix products, arithmetic and copies ran while one was open for 0% of the time, Pallas kernels for 29%

profile of v11, /device:TPU:0, one launch (start us, length us, event | category | flops | bytes accessed | tf_op | source)
XLA Modules:
  0.0 17.5 jit_solution(16578926849195097494)
XLA Ops:
  0.6 3.0 %collective-permute-start = (bf16[2,24,256]{2,1,0:T(8,128)(2,1)}, bf16[2,24,256]{2,1,0:T(8,128)(2,1)S(1)}, u32[]{:S(2)}, u32[]{:S(2)}) collective-permute-start(bf16[2,24,256]{2,1,0:T(8,128)(2,1)} %refs_0_.1), channel_id=1, source_target_pairs={{0,2},{1,3},{2,0},{3,1},{4,6},{5,7},{6,4},{7,5},{8,10},{9,11},{10,... | collective-permute-start | bytes 73736 | tf_op jit(solution)/shard_map/ppermute | solution.py:547
  3.6 0.0 collective-permute-start.2
  3.6 0.2 %collective-permute-start.1 = (bf16[2,24,256]{2,1,0:T(8,128)(2,1)}, bf16[2,24,256]{2,1,0:T(8,128)(2,1)S(1)}, u32[]{:S(2)}, u32[]{:S(2)}) collective-permute-start(bf16[2,24,256]{2,1,0:T(8,128)(2,1)} %refs_0_.1), channel_id=1, source_target_pairs={{0,1},{1,0},{2,3},{3,2},{4,5},{5,4},{6,7},{7,6},{8,9},{9,8},{10,11... | collective-permute-start | bytes 73736 | tf_op jit(solution)/shard_map/ppermute | solution.py:547
  3.8 2.3 %prepare.1 = (bf16[4,16,256]{2,1,0:T(8,128)(2,1)S(1)}, bf16[4,48,256]{2,1,0:T(8,128)(2,1)S(1)}, bf16[2,24,256]{2,1,0:T(8,128)(2,1)S(1)}, f32[4,24,256]{2,1,0:T(8,128)S(1)}, f32[4,24,256]{2,1,0:T(8,128)S(1)}) custom-call(bf16[2,24,256]{2,1,0:T(8,128)(2,1)} %refs_0_.1, f32[4,24,256]{2,1,0:T(8,128)} %refs_1_.1, f32[4,24,256]{2,1,0:T(8,128)} %refs_2_.1, ...), custom_call_target="tpu_custom_call" | custom-call | flops 1000000000 | bytes 6000000 | tf_op jit(solution)/shard_map/prepare/pallas_call | solution.py:185
  6.1 0.0 collective-permute-done.low.high
  6.2 0.9 %collective-permute-done.2.low_left.high_left.low_right.high_right = bf16[2,24,256]{2,1,0:T(8,128)(2,1)S(1)} collective-permute-done((bf16[2,24,256]{2,1,0:T(8,128)(2,1)}, bf16[2,24,256]{2,1,0:T(8,128)(2,1)S(1)}, u32[]{:S(2)}, u32[]{:S(2)}) %collective-permute-start.2) | collective-permute-done | bytes 24608 | tf_op jit(solution)/shard_map/ppermute | solution.py:547
  7.1 0.0 collective-permute-done.1.left.right
  7.1 0.2 %pack.1 = (bf16[2,56,384]{2,1,0:T(8,128)(2,1)S(1)}, bf16[1,112,256]{2,1,0:T(8,128)(2,1)S(1)}, bf16[1,112,256]{2,1,0:T(8,128)(2,1)S(1)}, bf16[1,112,256]{2,1,0:T(8,128)(2,1)S(1)}) custom-call(bf16[2,24,256]{2,1,0:T(8,128)(2,1)S(1)} %get-tuple-element.24.own, bf16[2,24,256]{2,1,0:T(8,128)(2,1)S(1)} %collective-permute-done.low.high, ...), custom_call_target="tpu_custom_call" | custom-call | flops 1000000 | bytes 1000000 | tf_op jit(solution)/shard_map/pack/pallas_call | solution.py:574
  7.3 3.7 %collective-permute-start.5 = (bf16[1,112,256]{2,1,0:T(8,128)(2,1)S(1)}, bf16[1,112,256]{2,1,0:T(8,128)(2,1)S(1)}, u32[]{:S(2)}, u32[]{:S(2)}) collective-permute-start(bf16[1,112,256]{2,1,0:T(8,128)(2,1)S(1)} %get-tuple-element.30), channel_id=1, source_target_pairs={{0,12},{4,8},{8,4},{12,0},{1,13},{5,9},{9,5},{13,1},{2,14},{6,10},... | collective-permute-start | bytes 172040 | tf_op jit(solution)/shard_map/ppermute | solution.py:580
  11.0 0.0 collective-permute-start.3
  11.0 0.8 %collective-permute-start.4 = (bf16[1,112,256]{2,1,0:T(8,128)(2,1)S(1)}, bf16[1,112,256]{2,1,0:T(8,128)(2,1)S(1)}, u32[]{:S(2)}, u32[]{:S(2)}) collective-permute-start(bf16[1,112,256]{2,1,0:T(8,128)(2,1)S(1)} %get-tuple-element.29), channel_id=1, source_target_pairs={{0,4},{4,0},{8,12},{12,8},{1,5},{5,1},{9,13},{13,9},{2,6},{6,2},{1... | collective-permute-start | bytes 172040 | tf_op jit(solution)/shard_map/ppermute | solution.py:580
  11.8 1.3 %models.4 = (f32[2,24,256]{2,1,0:T(8,128)S(1)}, f32[2,24,256]{2,1,0:T(8,128)S(1)}, f32[1,24,256]{2,1,0:T(8,128)S(1)}, bf16[4,288,512]{2,1,0:T(8,128)(2,1)S(1)}) custom-call(f32[4,24,256]{2,1,0:T(8,128)S(1)} %get-tuple-element.21.sci, f32[4,24,256]{2,1,0:T(8,128)S(1)} %get-tuple-element.22.weight, bf16[4,16,256]{2,1,0:T(8,128)(2,1)S(1)} %get-tuple-element.23.r, ...), custom_call_target="tpu_custom_call" | custom-call | flops 400000000 | bytes 1000000 | tf_op jit(solution)/shard_map/models/pallas_call | solution.py:586
  13.1 0.9 %collective-permute-done.5.refs_1_ = bf16[1,112,256]{2,1,0:T(8,128)(2,1)S(1)} collective-permute-done((bf16[1,112,256]{2,1,0:T(8,128)(2,1)S(1)}, bf16[1,112,256]{2,1,0:T(8,128)(2,1)S(1)}, u32[]{:S(2)}, u32[]{:S(2)}) %collective-permute-start.5) | collective-permute-done | bytes 57376 | tf_op jit(solution)/shard_map/ppermute | solution.py:580
  14.0 0.8 %models.5 = (f32[2,24,256]{2,1,0:T(8,128)S(1)}, f32[2,24,256]{2,1,0:T(8,128)S(1)}, f32[1,24,256]{2,1,0:T(8,128)S(1)}) custom-call(f32[4,24,256]{2,1,0:T(8,128)S(1)} %get-tuple-element.21.sci, f32[4,24,256]{2,1,0:T(8,128)S(1)} %get-tuple-element.22.weight, bf16[4,16,256]{2,1,0:T(8,128)(2,1)S(1)} %get-tuple-element.23.r, ...), custom_call_target="tpu_custom_call" | custom-call | flops 800000000 | bytes 1000000 | tf_op jit(solution)/shard_map/models/pallas_call | solution.py:586
  14.8 0.5 %collective-permute-done.4.refs_1_ = bf16[1,112,256]{2,1,0:T(8,128)(2,1)S(1)} collective-permute-done((bf16[1,112,256]{2,1,0:T(8,128)(2,1)S(1)}, bf16[1,112,256]{2,1,0:T(8,128)(2,1)S(1)}, u32[]{:S(2)}, u32[]{:S(2)}) %collective-permute-start.4) | collective-permute-done | bytes 57376 | tf_op jit(solution)/shard_map/ppermute | solution.py:580
  15.2 0.8 %models.6 = (f32[2,24,256]{2,1,0:T(8,128)S(1)}, f32[2,24,256]{2,1,0:T(8,128)S(1)}, f32[1,24,256]{2,1,0:T(8,128)S(1)}) custom-call(f32[4,24,256]{2,1,0:T(8,128)S(1)} %get-tuple-element.21.sci, f32[4,24,256]{2,1,0:T(8,128)S(1)} %get-tuple-element.22.weight, bf16[4,16,256]{2,1,0:T(8,128)(2,1)S(1)} %get-tuple-element.23.r, ...), custom_call_target="tpu_custom_call" | custom-call | flops 800000000 | bytes 1000000 | tf_op jit(solution)/shard_map/models/pallas_call | solution.py:586
  16.0 0.0 collective-permute-done.3.refs_1_
  16.0 1.4 %models.7 = (f32[4,24,256]{2,1,0:T(8,128)}, f32[2,24,256]{2,1,0:T(8,128)}) custom-call(f32[4,24,256]{2,1,0:T(8,128)S(1)} %get-tuple-element.21.sci, f32[4,24,256]{2,1,0:T(8,128)S(1)} %get-tuple-element.22.weight, bf16[4,16,256]{2,1,0:T(8,128)(2,1)S(1)} %get-tuple-element.23.r, bf16[2,56,384]{2,1,0:T(8,128)(2,1)S(1)} %get-tuple-element.26.slabs, ...), custom_call_target="tpu_custom_call" | custom-call | flops 800000000 | bytes 1000000 | tf_op jit(solution)/shard_map/models/pallas_call | solution.py:586
Async XLA Ops:
  0.6 5.5 %collective-permute-start = (bf16[2,24,256]{2,1,0:T(8,128)(2,1)}, bf16[2,24,256]{2,1,0:T(8,128)(2,1)S(1)}, u32[]{:S(2)}, u32[]{:S(2)}) collective-permute-start(bf16[2,24,256]{2,1,0:T(8,128)(2,1)} %refs_0_.1), channel_id=1, source_target_pairs={{0,2},{1,3},{2,0},{3,1},{4,6},{5,7},{6,4},{7,5},{8,10},{9,11},{10,... | collective-permute-start | bytes 73736 | tf_op jit(solution)/shard_map/ppermute | solution.py:547
  3.6 3.5 %collective-permute-start.2 = (bf16[2,24,256]{2,1,0:T(8,128)(2,1)}, bf16[2,24,256]{2,1,0:T(8,128)(2,1)S(1)}, u32[]{:S(2)}, u32[]{:S(2)}) collective-permute-start(bf16[2,24,256]{2,1,0:T(8,128)(2,1)} %refs_0_.1), channel_id=1, source_target_pairs={{0,3},{1,2},{2,1},{3,0},{4,7},{5,6},{6,5},{7,4},{8,11},{9,10},{10,... | collective-permute-start | bytes 73736 | tf_op jit(solution)/shard_map/ppermute | solution.py:547
  3.6 3.5 %collective-permute-start.1 = (bf16[2,24,256]{2,1,0:T(8,128)(2,1)}, bf16[2,24,256]{2,1,0:T(8,128)(2,1)S(1)}, u32[]{:S(2)}, u32[]{:S(2)}) collective-permute-start(bf16[2,24,256]{2,1,0:T(8,128)(2,1)} %refs_0_.1), channel_id=1, source_target_pairs={{0,1},{1,0},{2,3},{3,2},{4,5},{5,4},{6,7},{7,6},{8,9},{9,8},{10,11... | collective-permute-start | bytes 73736 | tf_op jit(solution)/shard_map/ppermute | solution.py:547
  7.3 6.7 %collective-permute-start.5 = (bf16[1,112,256]{2,1,0:T(8,128)(2,1)S(1)}, bf16[1,112,256]{2,1,0:T(8,128)(2,1)S(1)}, u32[]{:S(2)}, u32[]{:S(2)}) collective-permute-start(bf16[1,112,256]{2,1,0:T(8,128)(2,1)S(1)} %get-tuple-element.30), channel_id=1, source_target_pairs={{0,12},{4,8},{8,4},{12,0},{1,13},{5,9},{9,5},{13,1},{2,14},{6,10},... | collective-permute-start | bytes 172040 | tf_op jit(solution)/shard_map/ppermute | solution.py:580
  11.0 5.1 %collective-permute-start.3 = (bf16[1,112,256]{2,1,0:T(8,128)(2,1)S(1)}, bf16[1,112,256]{2,1,0:T(8,128)(2,1)S(1)}, u32[]{:S(2)}, u32[]{:S(2)}) collective-permute-start(bf16[1,112,256]{2,1,0:T(8,128)(2,1)S(1)} %get-tuple-element.28), channel_id=1, source_target_pairs={{0,8},{4,12},{8,0},{12,4},{1,9},{5,13},{9,1},{13,5},{2,10},{6,14},... | collective-permute-start | bytes 172040 | tf_op jit(solution)/shard_map/ppermute | solution.py:580
  11.0 4.3 %collective-permute-start.4 = (bf16[1,112,256]{2,1,0:T(8,128)(2,1)S(1)}, bf16[1,112,256]{2,1,0:T(8,128)(2,1)S(1)}, u32[]{:S(2)}, u32[]{:S(2)}) collective-permute-start(bf16[1,112,256]{2,1,0:T(8,128)(2,1)S(1)} %get-tuple-element.29), channel_id=1, source_target_pairs={{0,4},{4,0},{8,12},{12,8},{1,5},{5,1},{9,13},{13,9},{2,6},{6,2},{1... | collective-permute-start | bytes 172040 | tf_op jit(solution)/shard_map/ppermute | solution.py:580

commit v12 on v10

--- a/solution.py
+++ b/solution.py
@@ -291,8 +291,9 @@
                     jnp.concatenate(bits[i * wide : (i + 1) * wide], axis=1)
                     for i in range(sz.halo_rows // 8)
                 ]
-                parts = [sw[mine].astype(f32), lines, slab[:, :w]] + bits
-                out[c] = jnp.concatenate(parts, axis=0).astype(bf16)
+                out[c, : sz.sw_rows] = sw[mine]
+                out[c, sz.sw_rows : sz.main_at] = r[mine]
+                out[c, sz.main_at :] = jnp.concatenate([slab[:, :w]] + bits, axis=0).astype(bf16)
 
     vmem = pl.BlockSpec(memory_space=pltpu.VMEM)
     return pl.pallas_call(

time: 17.6 us -> 17.6 us (level)
  no operation moved by 1% of the time
where the time goes in v12:
time: 17.6 us; the launch traced here: 17.5 us
  starting transfers between devices  7.65 us (43%)
  Pallas kernels  6.72 us (38%)
  waiting for transfers between devices  2.41 us (14%)
  between operations  0.69 us (4%)
    ppermute x3, starting transfers between devices, local(): pays[k] = lax.ppermute(send, 'epoch', pairs)  4.45 us
    pallas_call x4, Pallas kernels, local(): models(sz, n_epoch, tiles, count, ks, first, last, kept)  4.22 us
    ppermute x3, starting transfers between devices, surroundings(): sent[key] = lax.ppermute(block, ('strip', 'band'), pairs)  3.2 us
    pallas_call x1, Pallas kernels, call(): pl.pallas_call(body, in_specs=[hbm] * 9, out_specs=(vmem,) * 5, out_shape...  2.3 us
    ppermute x3, waiting for transfers between devices, local(): pays[k] = lax.ppermute(send, 'epoch', pairs)  1.46 us
    ppermute x3, waiting for transfers between devices, surroundings(): sent[key] = lax.ppermute(block, ('strip', 'band'), pairs)  0.95 us
  transfers between devices with their start and end apart: 6, of which 3 were waited for; matrix products, arithmetic and copies ran while one was open for 0% of the time, Pallas kernels for 29%

profile of v12, /device:TPU:0, one launch (start us, length us, event | category | flops | bytes accessed | tf_op | source)
XLA Modules:
  0.0 17.5 jit_solution(9294815482514480844)
XLA Ops:
  0.6 3.0 %collective-permute-start = (bf16[2,24,256]{2,1,0:T(8,128)(2,1)}, bf16[2,24,256]{2,1,0:T(8,128)(2,1)S(1)}, u32[]{:S(2)}, u32[]{:S(2)}) collective-permute-start(bf16[2,24,256]{2,1,0:T(8,128)(2,1)} %refs_0_.1), channel_id=1, source_target_pairs={{0,2},{1,3},{2,0},{3,1},{4,6},{5,7},{6,4},{7,5},{8,10},{9,11},{10,... | collective-permute-start | bytes 73736 | tf_op jit(solution)/shard_map/ppermute | solution.py:546
  3.6 0.0 collective-permute-start.2
  3.6 0.2 %collective-permute-start.1 = (bf16[2,24,256]{2,1,0:T(8,128)(2,1)}, bf16[2,24,256]{2,1,0:T(8,128)(2,1)S(1)}, u32[]{:S(2)}, u32[]{:S(2)}) collective-permute-start(bf16[2,24,256]{2,1,0:T(8,128)(2,1)} %refs_0_.1), channel_id=1, source_target_pairs={{0,1},{1,0},{2,3},{3,2},{4,5},{5,4},{6,7},{7,6},{8,9},{9,8},{10,11... | collective-permute-start | bytes 73736 | tf_op jit(solution)/shard_map/ppermute | solution.py:546
  3.8 2.3 %prepare.1 = (bf16[4,16,256]{2,1,0:T(8,128)(2,1)S(1)}, bf16[4,48,256]{2,1,0:T(8,128)(2,1)S(1)}, bf16[2,24,256]{2,1,0:T(8,128)(2,1)S(1)}, f32[4,24,256]{2,1,0:T(8,128)S(1)}, f32[4,24,256]{2,1,0:T(8,128)S(1)}) custom-call(bf16[2,24,256]{2,1,0:T(8,128)(2,1)} %refs_0_.1, f32[4,24,256]{2,1,0:T(8,128)} %refs_1_.1, f32[4,24,256]{2,1,0:T(8,128)} %refs_2_.1, ...), custom_call_target="tpu_custom_call" | custom-call | flops 1000000000 | bytes 6000000 | tf_op jit(solution)/shard_map/prepare/pallas_call | solution.py:185
  6.1 0.0 collective-permute-done.low.high
  6.2 0.9 %collective-permute-done.2.low_left.high_left.low_right.high_right = bf16[2,24,256]{2,1,0:T(8,128)(2,1)S(1)} collective-permute-done((bf16[2,24,256]{2,1,0:T(8,128)(2,1)}, bf16[2,24,256]{2,1,0:T(8,128)(2,1)S(1)}, u32[]{:S(2)}, u32[]{:S(2)}) %collective-permute-start.2) | collective-permute-done | bytes 24608 | tf_op jit(solution)/shard_map/ppermute | solution.py:546
  7.1 0.0 collective-permute-done.1.left.right
  7.1 0.2 %pack.1 = (bf16[2,56,384]{2,1,0:T(8,128)(2,1)S(1)}, bf16[1,112,256]{2,1,0:T(8,128)(2,1)S(1)}, bf16[1,112,256]{2,1,0:T(8,128)(2,1)S(1)}, bf16[1,112,256]{2,1,0:T(8,128)(2,1)S(1)}) custom-call(bf16[2,24,256]{2,1,0:T(8,128)(2,1)S(1)} %get-tuple-element.24.own, bf16[2,24,256]{2,1,0:T(8,128)(2,1)S(1)} %collective-permute-done.low.high, ...), custom_call_target="tpu_custom_call" | custom-call | flops 1000000 | bytes 1000000 | tf_op jit(solution)/shard_map/pack/pallas_call | solution.py:573
  7.3 3.7 %collective-permute-start.5 = (bf16[1,112,256]{2,1,0:T(8,128)(2,1)S(1)}, bf16[1,112,256]{2,1,0:T(8,128)(2,1)S(1)}, u32[]{:S(2)}, u32[]{:S(2)}) collective-permute-start(bf16[1,112,256]{2,1,0:T(8,128)(2,1)S(1)} %get-tuple-element.30), channel_id=1, source_target_pairs={{0,12},{4,8},{8,4},{12,0},{1,13},{5,9},{9,5},{13,1},{2,14},{6,10},... | collective-permute-start | bytes 172040 | tf_op jit(solution)/shard_map/ppermute | solution.py:579
  11.0 0.0 collective-permute-start.3
  11.0 0.8 %collective-permute-start.4 = (bf16[1,112,256]{2,1,0:T(8,128)(2,1)S(1)}, bf16[1,112,256]{2,1,0:T(8,128)(2,1)S(1)}, u32[]{:S(2)}, u32[]{:S(2)}) collective-permute-start(bf16[1,112,256]{2,1,0:T(8,128)(2,1)S(1)} %get-tuple-element.29), channel_id=1, source_target_pairs={{0,4},{4,0},{8,12},{12,8},{1,5},{5,1},{9,13},{13,9},{2,6},{6,2},{1... | collective-permute-start | bytes 172040 | tf_op jit(solution)/shard_map/ppermute | solution.py:579
  11.8 1.3 %models.4 = (f32[2,24,256]{2,1,0:T(8,128)S(1)}, f32[2,24,256]{2,1,0:T(8,128)S(1)}, f32[1,24,256]{2,1,0:T(8,128)S(1)}, bf16[4,288,512]{2,1,0:T(8,128)(2,1)S(1)}) custom-call(f32[4,24,256]{2,1,0:T(8,128)S(1)} %get-tuple-element.21.sci, f32[4,24,256]{2,1,0:T(8,128)S(1)} %get-tuple-element.22.weight, bf16[4,16,256]{2,1,0:T(8,128)(2,1)S(1)} %get-tuple-element.23.r, ...), custom_call_target="tpu_custom_call" | custom-call | flops 400000000 | bytes 1000000 | tf_op jit(solution)/shard_map/models/pallas_call | solution.py:585
  13.1 0.9 %collective-permute-done.5.refs_1_ = bf16[1,112,256]{2,1,0:T(8,128)(2,1)S(1)} collective-permute-done((bf16[1,112,256]{2,1,0:T(8,128)(2,1)S(1)}, bf16[1,112,256]{2,1,0:T(8,128)(2,1)S(1)}, u32[]{:S(2)}, u32[]{:S(2)}) %collective-permute-start.5) | collective-permute-done | bytes 57376 | tf_op jit(solution)/shard_map/ppermute | solution.py:579
  14.0 0.8 %models.5 = (f32[2,24,256]{2,1,0:T(8,128)S(1)}, f32[2,24,256]{2,1,0:T(8,128)S(1)}, f32[1,24,256]{2,1,0:T(8,128)S(1)}) custom-call(f32[4,24,256]{2,1,0:T(8,128)S(1)} %get-tuple-element.21.sci, f32[4,24,256]{2,1,0:T(8,128)S(1)} %get-tuple-element.22.weight, bf16[4,16,256]{2,1,0:T(8,128)(2,1)S(1)} %get-tuple-element.23.r, ...), custom_call_target="tpu_custom_call" | custom-call | flops 800000000 | bytes 1000000 | tf_op jit(solution)/shard_map/models/pallas_call | solution.py:585
  14.8 0.5 %collective-permute-done.4.refs_1_ = bf16[1,112,256]{2,1,0:T(8,128)(2,1)S(1)} collective-permute-done((bf16[1,112,256]{2,1,0:T(8,128)(2,1)S(1)}, bf16[1,112,256]{2,1,0:T(8,128)(2,1)S(1)}, u32[]{:S(2)}, u32[]{:S(2)}) %collective-permute-start.4) | collective-permute-done | bytes 57376 | tf_op jit(solution)/shard_map/ppermute | solution.py:579
  15.2 0.8 %models.6 = (f32[2,24,256]{2,1,0:T(8,128)S(1)}, f32[2,24,256]{2,1,0:T(8,128)S(1)}, f32[1,24,256]{2,1,0:T(8,128)S(1)}) custom-call(f32[4,24,256]{2,1,0:T(8,128)S(1)} %get-tuple-element.21.sci, f32[4,24,256]{2,1,0:T(8,128)S(1)} %get-tuple-element.22.weight, bf16[4,16,256]{2,1,0:T(8,128)(2,1)S(1)} %get-tuple-element.23.r, ...), custom_call_target="tpu_custom_call" | custom-call | flops 800000000 | bytes 1000000 | tf_op jit(solution)/shard_map/models/pallas_call | solution.py:585
  16.0 0.0 collective-permute-done.3.refs_1_
  16.0 1.4 %models.7 = (f32[4,24,256]{2,1,0:T(8,128)}, f32[2,24,256]{2,1,0:T(8,128)}) custom-call(f32[4,24,256]{2,1,0:T(8,128)S(1)} %get-tuple-element.21.sci, f32[4,24,256]{2,1,0:T(8,128)S(1)} %get-tuple-element.22.weight, bf16[4,16,256]{2,1,0:T(8,128)(2,1)S(1)} %get-tuple-element.23.r, bf16[2,56,384]{2,1,0:T(8,128)(2,1)S(1)} %get-tuple-element.26.slabs, ...), custom_call_target="tpu_custom_call" | custom-call | flops 800000000 | bytes 1000000 | tf_op jit(solution)/shard_map/models/pallas_call | solution.py:585
Async XLA Ops:
  0.6 5.5 %collective-permute-start = (bf16[2,24,256]{2,1,0:T(8,128)(2,1)}, bf16[2,24,256]{2,1,0:T(8,128)(2,1)S(1)}, u32[]{:S(2)}, u32[]{:S(2)}) collective-permute-start(bf16[2,24,256]{2,1,0:T(8,128)(2,1)} %refs_0_.1), channel_id=1, source_target_pairs={{0,2},{1,3},{2,0},{3,1},{4,6},{5,7},{6,4},{7,5},{8,10},{9,11},{10,... | collective-permute-start | bytes 73736 | tf_op jit(solution)/shard_map/ppermute | solution.py:546
  3.6 3.5 %collective-permute-start.2 = (bf16[2,24,256]{2,1,0:T(8,128)(2,1)}, bf16[2,24,256]{2,1,0:T(8,128)(2,1)S(1)}, u32[]{:S(2)}, u32[]{:S(2)}) collective-permute-start(bf16[2,24,256]{2,1,0:T(8,128)(2,1)} %refs_0_.1), channel_id=1, source_target_pairs={{0,3},{1,2},{2,1},{3,0},{4,7},{5,6},{6,5},{7,4},{8,11},{9,10},{10,... | collective-permute-start | bytes 73736 | tf_op jit(solution)/shard_map/ppermute | solution.py:546
  3.6 3.5 %collective-permute-start.1 = (bf16[2,24,256]{2,1,0:T(8,128)(2,1)}, bf16[2,24,256]{2,1,0:T(8,128)(2,1)S(1)}, u32[]{:S(2)}, u32[]{:S(2)}) collective-permute-start(bf16[2,24,256]{2,1,0:T(8,128)(2,1)} %refs_0_.1), channel_id=1, source_target_pairs={{0,1},{1,0},{2,3},{3,2},{4,5},{5,4},{6,7},{7,6},{8,9},{9,8},{10,11... | collective-permute-start | bytes 73736 | tf_op jit(solution)/shard_map/ppermute | solution.py:546
  7.3 6.7 %collective-permute-start.5 = (bf16[1,112,256]{2,1,0:T(8,128)(2,1)S(1)}, bf16[1,112,256]{2,1,0:T(8,128)(2,1)S(1)}, u32[]{:S(2)}, u32[]{:S(2)}) collective-permute-start(bf16[1,112,256]{2,1,0:T(8,128)(2,1)S(1)} %get-tuple-element.30), channel_id=1, source_target_pairs={{0,12},{4,8},{8,4},{12,0},{1,13},{5,9},{9,5},{13,1},{2,14},{6,10},... | collective-permute-start | bytes 172040 | tf_op jit(solution)/shard_map/ppermute | solution.py:579
  11.0 5.1 %collective-permute-start.3 = (bf16[1,112,256]{2,1,0:T(8,128)(2,1)S(1)}, bf16[1,112,256]{2,1,0:T(8,128)(2,1)S(1)}, u32[]{:S(2)}, u32[]{:S(2)}) collective-permute-start(bf16[1,112,256]{2,1,0:T(8,128)(2,1)S(1)} %get-tuple-element.28), channel_id=1, source_target_pairs={{0,8},{4,12},{8,0},{12,4},{1,9},{5,13},{9,1},{13,5},{2,10},{6,14},... | collective-permute-start | bytes 172040 | tf_op jit(solution)/shard_map/ppermute | solution.py:579
  11.0 4.3 %collective-permute-start.4 = (bf16[1,112,256]{2,1,0:T(8,128)(2,1)S(1)}, bf16[1,112,256]{2,1,0:T(8,128)(2,1)S(1)}, u32[]{:S(2)}, u32[]{:S(2)}) collective-permute-start(bf16[1,112,256]{2,1,0:T(8,128)(2,1)S(1)} %get-tuple-element.29), channel_id=1, source_target_pairs={{0,4},{4,0},{8,12},{12,8},{1,5},{5,1},{9,13},{13,9},{2,6},{6,2},{1... | collective-permute-start | bytes 172040 | tf_op jit(solution)/shard_map/ppermute | solution.py:579

commit v13 on v12

--- a/solution.py
+++ b/solution.py
@@ -521,7 +521,7 @@
         scratch_shapes=scratch,
         compiler_params=pltpu.CompilerParams(vmem_limit_bytes=VMEM_LIMIT),
         cost_estimate=pl.CostEstimate(
-            flops=total_models * 400_000_000, bytes_accessed=1_000_000, transcendentals=0
+            flops=total_models * 1_000_000, bytes_accessed=100_000, transcendentals=0
         ),
         name="models",
     )

time: 17.6 us -> 17.7 us (level)
  transfers between devices with their start and end apart: 6 -> 6, of which waited for: 3 -> 4; matrix products, arithmetic and copies ran while one was open for 0% -> 0% of each run, Pallas kernels for 29% -> 29%
where the time goes in v13:
time: 17.7 us; the launch traced here: 17.6 us
  starting transfers between devices  7.65 us (43%)
  Pallas kernels  6.75 us (38%)
  waiting for transfers between devices  2.49 us (14%)
  between operations  0.69 us (4%)
    ppermute x3, starting transfers between devices, local(): pays[k] = lax.ppermute(send, 'epoch', pairs)  4.45 us
    pallas_call x4, Pallas kernels, local(): models(sz, n_epoch, tiles, count, ks, first, last, kept)  4.25 us
    ppermute x3, starting transfers between devices, surroundings(): sent[key] = lax.ppermute(block, ('strip', 'band'), pairs)  3.2 us
    pallas_call x1, Pallas kernels, call(): pl.pallas_call(body, in_specs=[hbm] * 9, out_specs=(vmem,) * 5, out_shape...  2.3 us
    ppermute x3, waiting for transfers between devices, local(): pays[k] = lax.ppermute(send, 'epoch', pairs)  1.54 us
    ppermute x3, waiting for transfers between devices, surroundings(): sent[key] = lax.ppermute(block, ('strip', 'band'), pairs)  0.95 us
  transfers between devices with their start and end apart: 6, of which 4 were waited for; matrix products, arithmetic and copies ran while one was open for 0% of the time, Pallas kernels for 29%

profile of v13, /device:TPU:0, one launch (start us, length us, event | category | flops | bytes accessed | tf_op | source)
XLA Modules:
  0.0 17.6 jit_solution(4078693191974756970)
XLA Ops:
  0.6 3.0 %collective-permute-start = (bf16[2,24,256]{2,1,0:T(8,128)(2,1)}, bf16[2,24,256]{2,1,0:T(8,128)(2,1)S(1)}, u32[]{:S(2)}, u32[]{:S(2)}) collective-permute-start(bf16[2,24,256]{2,1,0:T(8,128)(2,1)} %refs_0_.1), channel_id=1, source_target_pairs={{0,2},{1,3},{2,0},{3,1},{4,6},{5,7},{6,4},{7,5},{8,10},{9,11},{10,... | collective-permute-start | bytes 73736 | tf_op jit(solution)/shard_map/ppermute | solution.py:546
  3.6 0.0 collective-permute-start.2
  3.6 0.2 %collective-permute-start.1 = (bf16[2,24,256]{2,1,0:T(8,128)(2,1)}, bf16[2,24,256]{2,1,0:T(8,128)(2,1)S(1)}, u32[]{:S(2)}, u32[]{:S(2)}) collective-permute-start(bf16[2,24,256]{2,1,0:T(8,128)(2,1)} %refs_0_.1), channel_id=1, source_target_pairs={{0,1},{1,0},{2,3},{3,2},{4,5},{5,4},{6,7},{7,6},{8,9},{9,8},{10,11... | collective-permute-start | bytes 73736 | tf_op jit(solution)/shard_map/ppermute | solution.py:546
  3.8 2.3 %prepare.1 = (bf16[4,16,256]{2,1,0:T(8,128)(2,1)S(1)}, bf16[4,48,256]{2,1,0:T(8,128)(2,1)S(1)}, bf16[2,24,256]{2,1,0:T(8,128)(2,1)S(1)}, f32[4,24,256]{2,1,0:T(8,128)S(1)}, f32[4,24,256]{2,1,0:T(8,128)S(1)}) custom-call(bf16[2,24,256]{2,1,0:T(8,128)(2,1)} %refs_0_.1, f32[4,24,256]{2,1,0:T(8,128)} %refs_1_.1, f32[4,24,256]{2,1,0:T(8,128)} %refs_2_.1, ...), custom_call_target="tpu_custom_call" | custom-call | flops 1000000000 | bytes 6000000 | tf_op jit(solution)/shard_map/prepare/pallas_call | solution.py:185
  6.1 0.0 collective-permute-done.low.high
  6.2 0.9 %collective-permute-done.2.low_left.high_left.low_right.high_right = bf16[2,24,256]{2,1,0:T(8,128)(2,1)S(1)} collective-permute-done((bf16[2,24,256]{2,1,0:T(8,128)(2,1)}, bf16[2,24,256]{2,1,0:T(8,128)(2,1)S(1)}, u32[]{:S(2)}, u32[]{:S(2)}) %collective-permute-start.2) | collective-permute-done | bytes 24608 | tf_op jit(solution)/shard_map/ppermute | solution.py:546
  7.1 0.0 collective-permute-done.1.left.right
  7.1 0.2 %pack.1 = (bf16[2,56,384]{2,1,0:T(8,128)(2,1)S(1)}, bf16[1,112,256]{2,1,0:T(8,128)(2,1)S(1)}, bf16[1,112,256]{2,1,0:T(8,128)(2,1)S(1)}, bf16[1,112,256]{2,1,0:T(8,128)(2,1)S(1)}) custom-call(bf16[2,24,256]{2,1,0:T(8,128)(2,1)S(1)} %get-tuple-element.24.own, bf16[2,24,256]{2,1,0:T(8,128)(2,1)S(1)} %collective-permute-done.low.high, ...), custom_call_target="tpu_custom_call" | custom-call | flops 1000000 | bytes 1000000 | tf_op jit(solution)/shard_map/pack/pallas_call | solution.py:573
  7.3 3.7 %collective-permute-start.5 = (bf16[1,112,256]{2,1,0:T(8,128)(2,1)S(1)}, bf16[1,112,256]{2,1,0:T(8,128)(2,1)S(1)}, u32[]{:S(2)}, u32[]{:S(2)}) collective-permute-start(bf16[1,112,256]{2,1,0:T(8,128)(2,1)S(1)} %get-tuple-element.30), channel_id=1, source_target_pairs={{0,12},{4,8},{8,4},{12,0},{1,13},{5,9},{9,5},{13,1},{2,14},{6,10},... | collective-permute-start | bytes 172040 | tf_op jit(solution)/shard_map/ppermute | solution.py:579
  11.0 0.0 collective-permute-start.4
  11.0 0.8 %collective-permute-start.3 = (bf16[1,112,256]{2,1,0:T(8,128)(2,1)S(1)}, bf16[1,112,256]{2,1,0:T(8,128)(2,1)S(1)}, u32[]{:S(2)}, u32[]{:S(2)}) collective-permute-start(bf16[1,112,256]{2,1,0:T(8,128)(2,1)S(1)} %get-tuple-element.28), channel_id=1, source_target_pairs={{0,8},{4,12},{8,0},{12,4},{1,9},{5,13},{9,1},{13,5},{2,10},{6,14},... | collective-permute-start | bytes 172040 | tf_op jit(solution)/shard_map/ppermute | solution.py:579
  11.8 1.3 %models.4 = (f32[2,24,256]{2,1,0:T(8,128)S(1)}, f32[2,24,256]{2,1,0:T(8,128)S(1)}, f32[1,24,256]{2,1,0:T(8,128)S(1)}, bf16[4,288,512]{2,1,0:T(8,128)(2,1)S(1)}) custom-call(f32[4,24,256]{2,1,0:T(8,128)S(1)} %get-tuple-element.21.sci, f32[4,24,256]{2,1,0:T(8,128)S(1)} %get-tuple-element.22.weight, bf16[4,16,256]{2,1,0:T(8,128)(2,1)S(1)} %get-tuple-element.23.r, ...), custom_call_target="tpu_custom_call" | custom-call | flops 1000000 | bytes 100000 | tf_op jit(solution)/shard_map/models/pallas_call | solution.py:585
  13.1 0.3 %collective-permute-done.5.refs_1_ = bf16[1,112,256]{2,1,0:T(8,128)(2,1)S(1)} collective-permute-done((bf16[1,112,256]{2,1,0:T(8,128)(2,1)S(1)}, bf16[1,112,256]{2,1,0:T(8,128)(2,1)S(1)}, u32[]{:S(2)}, u32[]{:S(2)}) %collective-permute-start.5) | collective-permute-done | bytes 57376 | tf_op jit(solution)/shard_map/ppermute | solution.py:579
  13.4 0.8 %models.5 = (f32[2,24,256]{2,1,0:T(8,128)S(1)}, f32[2,24,256]{2,1,0:T(8,128)S(1)}, f32[1,24,256]{2,1,0:T(8,128)S(1)}) custom-call(f32[4,24,256]{2,1,0:T(8,128)S(1)} %get-tuple-element.21.sci, f32[4,24,256]{2,1,0:T(8,128)S(1)} %get-tuple-element.22.weight, bf16[4,16,256]{2,1,0:T(8,128)(2,1)S(1)} %get-tuple-element.23.r, ...), custom_call_target="tpu_custom_call" | custom-call | flops 2000000 | bytes 100000 | tf_op jit(solution)/shard_map/models/pallas_call | solution.py:585
  14.2 1.0 %collective-permute-done.4.refs_1_ = bf16[1,112,256]{2,1,0:T(8,128)(2,1)S(1)} collective-permute-done((bf16[1,112,256]{2,1,0:T(8,128)(2,1)S(1)}, bf16[1,112,256]{2,1,0:T(8,128)(2,1)S(1)}, u32[]{:S(2)}, u32[]{:S(2)}) %collective-permute-start.4) | collective-permute-done | bytes 57376 | tf_op jit(solution)/shard_map/ppermute | solution.py:579
  15.2 0.8 %models.6 = (f32[2,24,256]{2,1,0:T(8,128)S(1)}, f32[2,24,256]{2,1,0:T(8,128)S(1)}, f32[1,24,256]{2,1,0:T(8,128)S(1)}) custom-call(f32[4,24,256]{2,1,0:T(8,128)S(1)} %get-tuple-element.21.sci, f32[4,24,256]{2,1,0:T(8,128)S(1)} %get-tuple-element.22.weight, bf16[4,16,256]{2,1,0:T(8,128)(2,1)S(1)} %get-tuple-element.23.r, ...), custom_call_target="tpu_custom_call" | custom-call | flops 2000000 | bytes 100000 | tf_op jit(solution)/shard_map/models/pallas_call | solution.py:585
  16.0 0.2 %collective-permute-done.3.refs_1_ = bf16[1,112,256]{2,1,0:T(8,128)(2,1)S(1)} collective-permute-done((bf16[1,112,256]{2,1,0:T(8,128)(2,1)S(1)}, bf16[1,112,256]{2,1,0:T(8,128)(2,1)S(1)}, u32[]{:S(2)}, u32[]{:S(2)}) %collective-permute-start.3) | collective-permute-done | bytes 57376 | tf_op jit(solution)/shard_map/ppermute | solution.py:579
  16.1 1.4 %models.7 = (f32[4,24,256]{2,1,0:T(8,128)}, f32[2,24,256]{2,1,0:T(8,128)}) custom-call(f32[4,24,256]{2,1,0:T(8,128)S(1)} %get-tuple-element.21.sci, f32[4,24,256]{2,1,0:T(8,128)S(1)} %get-tuple-element.22.weight, bf16[4,16,256]{2,1,0:T(8,128)(2,1)S(1)} %get-tuple-element.23.r, bf16[2,56,384]{2,1,0:T(8,128)(2,1)S(1)} %get-tuple-element.26.slabs, ...), custom_call_target="tpu_custom_call" | custom-call | flops 2000000 | bytes 100000 | tf_op jit(solution)/shard_map/models/pallas_call | solution.py:585
Async XLA Ops:
  0.6 5.5 %collective-permute-start = (bf16[2,24,256]{2,1,0:T(8,128)(2,1)}, bf16[2,24,256]{2,1,0:T(8,128)(2,1)S(1)}, u32[]{:S(2)}, u32[]{:S(2)}) collective-permute-start(bf16[2,24,256]{2,1,0:T(8,128)(2,1)} %refs_0_.1), channel_id=1, source_target_pairs={{0,2},{1,3},{2,0},{3,1},{4,6},{5,7},{6,4},{7,5},{8,10},{9,11},{10,... | collective-permute-start | bytes 73736 | tf_op jit(solution)/shard_map/ppermute | solution.py:546
  3.6 3.5 %collective-permute-start.2 = (bf16[2,24,256]{2,1,0:T(8,128)(2,1)}, bf16[2,24,256]{2,1,0:T(8,128)(2,1)S(1)}, u32[]{:S(2)}, u32[]{:S(2)}) collective-permute-start(bf16[2,24,256]{2,1,0:T(8,128)(2,1)} %refs_0_.1), channel_id=1, source_target_pairs={{0,3},{1,2},{2,1},{3,0},{4,7},{5,6},{6,5},{7,4},{8,11},{9,10},{10,... | collective-permute-start | bytes 73736 | tf_op jit(solution)/shard_map/ppermute | solution.py:546
  3.6 3.5 %collective-permute-start.1 = (bf16[2,24,256]{2,1,0:T(8,128)(2,1)}, bf16[2,24,256]{2,1,0:T(8,128)(2,1)S(1)}, u32[]{:S(2)}, u32[]{:S(2)}) collective-permute-start(bf16[2,24,256]{2,1,0:T(8,128)(2,1)} %refs_0_.1), channel_id=1, source_target_pairs={{0,1},{1,0},{2,3},{3,2},{4,5},{5,4},{6,7},{7,6},{8,9},{9,8},{10,11... | collective-permute-start | bytes 73736 | tf_op jit(solution)/shard_map/ppermute | solution.py:546
  7.3 6.1 %collective-permute-start.5 = (bf16[1,112,256]{2,1,0:T(8,128)(2,1)S(1)}, bf16[1,112,256]{2,1,0:T(8,128)(2,1)S(1)}, u32[]{:S(2)}, u32[]{:S(2)}) collective-permute-start(bf16[1,112,256]{2,1,0:T(8,128)(2,1)S(1)} %get-tuple-element.30), channel_id=1, source_target_pairs={{0,12},{4,8},{8,4},{12,0},{1,13},{5,9},{9,5},{13,1},{2,14},{6,10},... | collective-permute-start | bytes 172040 | tf_op jit(solution)/shard_map/ppermute | solution.py:579
  11.0 4.2 %collective-permute-start.4 = (bf16[1,112,256]{2,1,0:T(8,128)(2,1)S(1)}, bf16[1,112,256]{2,1,0:T(8,128)(2,1)S(1)}, u32[]{:S(2)}, u32[]{:S(2)}) collective-permute-start(bf16[1,112,256]{2,1,0:T(8,128)(2,1)S(1)} %get-tuple-element.29), channel_id=1, source_target_pairs={{0,4},{4,0},{8,12},{12,8},{1,5},{5,1},{9,13},{13,9},{2,6},{6,2},{1... | collective-permute-start | bytes 172040 | tf_op jit(solution)/shard_map/ppermute | solution.py:579
  11.0 5.2 %collective-permute-start.3 = (bf16[1,112,256]{2,1,0:T(8,128)(2,1)S(1)}, bf16[1,112,256]{2,1,0:T(8,128)(2,1)S(1)}, u32[]{:S(2)}, u32[]{:S(2)}) collective-permute-start(bf16[1,112,256]{2,1,0:T(8,128)(2,1)S(1)} %get-tuple-element.28), channel_id=1, source_target_pairs={{0,8},{4,12},{8,0},{12,4},{1,9},{5,13},{9,1},{13,5},{2,10},{6,14},... | collective-permute-start | bytes 172040 | tf_op jit(solution)/shard_map/ppermute | solution.py:579
